TPU v7x, 256 devices: a whole 4x4x8 slice. The times are simulated.
256 devices in a mesh: lat: 32 (over y, x, z_hi), lon: 4 (over z_lo), ens: 2 (over core).
Axes of the slice: x: 4, y: 4, z: 8 (z_hi: 2, z_lo: 4; z = z_hi * 4 + z_lo), core: 2. Of those that a mesh axis runs over, the one named last changes fastest.
Arguments:
- states: bfloat16 [2, 128, 1440, 256], P('ens', 'lat', 'lon'), may hold values from -6 to 6
- cotangent: bfloat16 [2, 128, 1440, 256], P('ens', 'lat', 'lon'), may hold values from -6 to 6
- kernels: bfloat16 [3, 128, 4, 7], replicated, may hold values from -1 to 1
- offsets: int32 [128], replicated, may hold values from -3 to 127, as said below
- mixing: bfloat16 [3, 2, 128, 128], replicated, may hold values from -0.3125 to 0.3125
- legendre: bfloat16 [384, 384, 128], P('lat'), may hold values from -0.5 to 0.5
- owner_order: int32 [384], replicated, may hold values from 0 to 383, each once
- spectral_gain: bfloat16 [384, 256], replicated, may hold values from -5 to 5
Outputs:
- next_state: bfloat16 [2, 128, 1440, 256], P('ens', 'lat', 'lon')
- grad_state: bfloat16 [2, 128, 1440, 256], P('ens', 'lat', 'lon')
- grad_mixing: float32 [3, 2, 128, 128], replicated
- grad_gain: float32 [384, 256], P(None, 'lon')
Inputs may be any that keep to these rules, and one draw needn't show every extreme that they name: offsets[i] - i lies between -3 and 0. `owner_order`: every wavenumber 0 to 383 appears once.
All inputs are finite; a program needn't handle non-finite values.
Results may differ from a plain program's by a relative error of at most 0.01.
Values may be sent and summed in bfloat16 or wider, within the bound.
No kernel may reach another device: no remote copies, remote signals or barrier semaphores. Data moves between devices by JAX's collectives and lax.ppermute only.
A program may use at most 128 MiB of HBM per device.

v0:
```python
import math

import jax
import jax.numpy as jnp
from jax import lax
from jax.sharding import PartitionSpec as P

LONGITUDES = 1440
BAND_REACH = 3
SUPPORT = 4


highest = lax.Precision.HIGHEST
far_below = -1000000


def padded_2(x, sides, width):
    for axis, dim in sides:
        peers, length = (lax.axis_size(axis), x.shape[dim])
        up = [(i, (i + 1) % peers) for i in range(peers)]
        down = [(j, i) for i, j in up]
        last = lax.slice_in_dim(x, length - width, length, axis=dim)
        initial = lax.slice_in_dim(x, 0, width, axis=dim)
        before = lax.ppermute(last, axis, up)
        after = lax.ppermute(initial, axis, down)
        x = jnp.concatenate([before, x, after], axis=dim)
    return x


def fourier_table(owner_order, points):
    longitudes = jnp.arange(points, dtype=jnp.int32)
    phases = longitudes[:, None] * owner_order[None, :] % points
    angles = phases.astype(jnp.float32) * (2.0 * math.pi / points)
    factor = 1.0 / math.sqrt(points)
    return jnp.stack([jnp.cos(angles) * factor, -jnp.sin(angles) * factor], axis=-1).astype(
        jnp.bfloat16
    )


def band_table(kernels_pad, offsets_pad, first_in, count_in, first_out, output_count):
    rows_kern = lax.dynamic_slice_in_dim(kernels_pad, first_in + BAND_REACH, count_in, 1)
    rows_start = lax.dynamic_slice_in_dim(offsets_pad, first_in + BAND_REACH, count_in, 0)
    targets = first_out + jnp.arange(output_count, dtype=jnp.int32)
    support_index = jnp.arange(SUPPORT, dtype=jnp.int32)
    matches = (
        rows_start[:, None, None] + support_index[None, :, None] == targets[None, None, :]
    ).astype(jnp.float32)
    return jnp.einsum(
        "bikd,ikr->ibrd", rows_kern.astype(jnp.float32), matches, precision=highest
    ).astype(jnp.bfloat16)


def haloed(fields, lat_first, lat_total):
    extended = padded_2(fields, (("lat", 0), ("lon", 1)), BAND_REACH)
    rows_global = lat_first - BAND_REACH + jnp.arange(extended.shape[0], dtype=jnp.int32)
    inside = (rows_global >= 0) & (rows_global < lat_total)
    return jnp.where(inside[:, None, None], extended, jnp.zeros_like(extended))


def to_owners(blocks):
    moved = lax.all_to_all(blocks, "lat", split_axis=1, concat_axis=0, tiled=True)
    return moved


def spectral(fields, wave_table, legendre, owner_order, spectral_gain):
    lat_index = lax.axis_index("lat")
    lon_index = lax.axis_index("lon")
    lon_count = lax.axis_size("lon")
    lat_rows = fields.shape[0]
    channels = fields.shape[2]
    owned_count = legendre.shape[0]
    owned_total = wave_table.shape[1]
    columns = channels // lon_count
    circle = lax.all_to_all(fields, "lon", split_axis=2, concat_axis=1, tiled=True)
    first_owned = lat_index * owned_count
    gains_here = lax.dynamic_slice_in_dim(spectral_gain, lon_index * columns, columns, 1)
    owned_here = legendre.shape[0]
    degrees_total = legendre.shape[1]
    analysed = jnp.einsum("tnc,nkr->tkrc", circle, wave_table, preferred_element_type=jnp.float32)
    analysed = analysed.astype(jnp.bfloat16).reshape(lat_rows, owned_total, 2 * columns)
    owned_rows = to_owners(analysed)
    orders = lax.dynamic_slice_in_dim(owner_order, first_owned, owned_here, 0)
    degrees_index = jnp.arange(degrees_total, dtype=jnp.int32)
    triangle = (degrees_index[None, :] >= orders[:, None]).astype(jnp.float32)
    coeffs = (
        jnp.einsum("klt,tkq->klq", legendre, owned_rows, preferred_element_type=jnp.float32)
        * triangle[:, :, None]
    )
    coeffs = coeffs.reshape(owned_here, degrees_total, 2, columns)
    weighted_terms = (coeffs * gains_here.astype(jnp.float32)[None, :, None, :]).astype(
        jnp.bfloat16
    )
    weighted_terms = weighted_terms.reshape(owned_here, degrees_total, 2 * columns)
    synthesis = jnp.einsum(
        "rjo,rji->roi", legendre, weighted_terms, preferred_element_type=jnp.float32
    ).astype(jnp.bfloat16)
    returned = to_owners(synthesis)
    spectrum = jnp.einsum(
        "ktrc,nkr->tnc",
        returned.reshape(owned_total, lat_rows, 2, columns),
        wave_table,
        preferred_element_type=jnp.float32,
    ).astype(jnp.bfloat16)
    angular_slices = lax.all_to_all(spectrum, "lon", split_axis=1, concat_axis=2, tiled=True)
    return (angular_slices, coeffs)


def on_device(states, cotangent, kernels, offsets, mixing, legendre, owner_order, spectral_gain):
    fields = states[0]
    lat_rows = fields.shape[0]
    angular_slice = fields.shape[1]
    channels = fields.shape[2]
    lon_index = lax.axis_index("lon")
    lon_count = lax.axis_size("lon")
    lat_first = lax.axis_index("lat") * lat_rows
    lat_total = lat_rows * lax.axis_size("lat")
    tap_count = 2 * BAND_REACH + 1
    extent = lat_rows + 2 * BAND_REACH
    kernel_number = mixing.shape[0]
    group_count = mixing.shape[1]
    group_width = mixing.shape[2]
    wave_table = fourier_table(owner_order, LONGITUDES)
    kernels_pad = jnp.pad(kernels, ((0, 0), (BAND_REACH, BAND_REACH), (0, 0), (0, 0)))
    offsets_pad = jnp.pad(offsets, BAND_REACH, constant_values=far_below)
    spectrum, coeffs = spectral(fields, wave_table, legendre, owner_order, spectral_gain)
    padded = haloed(fields, lat_first, lat_total)
    stacked = jnp.stack(
        [padded[:, step_lon : step_lon + angular_slice] for step_lon in range(tap_count)], axis=1
    )
    forward_band = band_table(
        kernels_pad, offsets_pad, lat_first, lat_rows, lat_first - BAND_REACH, extent
    )
    basis_field = jnp.einsum(
        "ibrd,rdjc->ibjc", forward_band, stacked, preferred_element_type=jnp.float32
    ).astype(jnp.bfloat16)
    basis_groups = basis_field.reshape(
        lat_rows, kernel_number, angular_slice, group_count, group_width
    )
    mixed_part = jnp.einsum(
        "ibjgc,bgce->ijge", basis_groups, mixing, preferred_element_type=jnp.float32
    ).reshape(lat_rows, angular_slice, channels)
    preact = spectrum.astype(jnp.float32) + mixed_part
    activated, pullback = jax.vjp(jax.nn.gelu, preact)
    next_state = (fields.astype(jnp.float32) + activated).astype(jnp.bfloat16)
    incoming = cotangent[0].astype(jnp.float32)
    grad_pre = pullback(incoming)[0].astype(jnp.bfloat16)
    spec_back, coeffs_back = spectral(grad_pre, wave_table, legendre, owner_order, spectral_gain)
    gain_part = jnp.sum(coeffs * coeffs_back, axis=(0, 2))
    mix_part = jnp.einsum(
        "ibjgc,ijge->bgce",
        basis_groups,
        grad_pre.reshape(lat_rows, angular_slice, group_count, group_width),
        preferred_element_type=jnp.float32,
    )
    padded_back = haloed(grad_pre, lat_first, lat_total)
    stacked_back = jnp.stack(
        [
            padded_back[:, 2 * BAND_REACH - step_lon : 2 * BAND_REACH - step_lon + angular_slice]
            for step_lon in range(tap_count)
        ],
        axis=1,
    )
    backward_band = band_table(
        kernels_pad, offsets_pad, lat_first - BAND_REACH, extent, lat_first, lat_rows
    )
    spread = jnp.einsum(
        "ibrd,idjc->rbjc", backward_band, stacked_back, preferred_element_type=jnp.float32
    ).astype(jnp.bfloat16)
    backward = jnp.einsum(
        "rbjge,bgce->rjgc",
        spread.reshape(lat_rows, kernel_number, angular_slice, group_count, group_width),
        mixing,
        preferred_element_type=jnp.float32,
    ).reshape(lat_rows, angular_slice, channels)
    grad_state = (incoming + spec_back.astype(jnp.float32) + backward).astype(jnp.bfloat16)
    quarter = channels // lon_count
    full_gain = lax.dynamic_update_slice(
        jnp.zeros((gain_part.shape[0], channels), jnp.float32), gain_part, (0, lon_index * quarter)
    )
    mix_total, gain_total = lax.psum((mix_part, full_gain), ("lat", "lon", "ens"))
    members = states.shape[0] * lax.axis_size("ens")
    mix_scale = 1.0 / math.sqrt(members * lat_total * LONGITUDES)
    gain_scale = 1.0 / math.sqrt(2 * members * gain_part.shape[0])
    grad_gain = lax.dynamic_slice_in_dim(gain_total, lon_index * quarter, quarter, 1) * gain_scale
    return (next_state[None], grad_state[None], mix_total * mix_scale, grad_gain)


def solution(mesh):
    in_specs = (
        P("ens", "lat", "lon", None),
        P("ens", "lat", "lon", None),
        P(),
        P(),
        P(),
        P("lat", None, None),
        P(),
        P(),
    )
    out_specs = (P("ens", "lat", "lon", None), P("ens", "lat", "lon", None), P(), P(None, "lon"))
    return jax.shard_map(
        on_device, mesh=mesh, in_specs=in_specs, out_specs=out_specs, check_vma=False
    )
```

profile of v0, /device:TPU:2, one launch (start us, length us, event | category | flops | bytes accessed | tf_op | source)
XLA Modules:
  0.0 602.9 jit_solution(414831005022442554)
XLA Ops:
  9.6 7.3 %collective-permute-start = (bf16[3,360,256]{2,1,0:T(8,128)(2,1)}, bf16[3,360,256]{2,1,0:T(8,128)(2,1)S(1)}, u32[]{:S(2)}, u32[]{:S(2)}) collective-permute-start(bf16[3,360,256]{2,1,0:T(8,128)(2,1)} %get-tuple-element.32), channel_id=1, source_target_pairs={{0,8},{8,16},{16,24},{24,32},{32,40},{40,48},{48,56},{56,64},{64,7... | collective-permute-start | bytes 1658888 | tf_op jit(solution)/shard_map/ppermute | solution.py:24
  18.3 5.5 all-to-all-start
  25.6 10.5 %multiply_convert_fusion.1 = (bf16[1440,384,1]{1,0,2:T(8,128)(2,1)}, bf16[1440,384,1]{1,0,2:T(8,128)(2,1)}) fusion(s32[384]{0:T(512)S(1)} %copy-done.23), kind=kLoop, calls=%fused_computation.38 | loop fusion | flops 7741440 | bytes 2213376 | tf_op jit(solution)/shard_map/convert.14
  36.2 29.5 %collective-permute-done.1 = bf16[3,360,256]{2,1,0:T(8,128)(2,1)} collective-permute-done((bf16[3,360,256]{2,1,0:T(8,128)(2,1)}, bf16[3,360,256]{2,1,0:T(8,128)(2,1)}, u32[]{:S(2)}, u32[]{:S(2)}) %collective-permute-start.1) | collective-permute-done | bytes 552992 | tf_op jit(solution)/shard_map/ppermute | solution.py:25
  66.4 5.2 collective-permute-start.2
  74.8 4.6 collective-permute-done.2
  92.3 12.7 %all-to-all-start.1 = ((bf16[4,384,128]{2,0,1:T(4,128)(2,1)}), bf16[4,384,128]{2,0,1:T(4,128)(2,1)S(1)}, u32[]{:S(2)}, u32[]{:S(2)}) async-start(bf16[4,384,128]{2,0,1:T(4,128)(2,1)} %copy.223), calls=%async_computation.1 | async-start | bytes 786432 | tf_op jit(solution)/shard_map/all_to_all | solution.py:61
  110.1 7.8 %all-to-all-done.1 = bf16[4,384,128]{2,0,1:T(4,128)(2,1)S(1)} async-done(((bf16[4,384,128]{2,0,1:T(4,128)(2,1)}), bf16[4,384,128]{2,0,1:T(4,128)(2,1)S(1)}, u32[]{:S(2)}, u32[]{:S(2)}) %all-to-all-start.1) | async-done | bytes 393248 | tf_op jit(solution)/shard_map/all_to_all | solution.py:61
  122.0 5.9 all-to-all-start.2
  132.9 8.6 %all-to-all-done.2 = bf16[12,128,128]{2,0,1:T(8,128)(2,1)} async-done(((bf16[12,128,128]{2,0,1:T(8,128)(2,1)}), bf16[12,128,128]{2,0,1:T(8,128)(2,1)}, u32[]{:S(2)}, u32[]{:S(2)}) %all-to-all-start.2) | async-done | bytes 393248 | tf_op jit(solution)/shard_map/all_to_all | solution.py:61
  151.3 9.3 %all-to-all-start.3 = ((bf16[4,2,46080]{2,1,0:T(2,128)(2,1)}), bf16[4,2,46080]{2,1,0:T(2,128)(2,1)S(1)}, u32[]{:S(2)}, u32[]{:S(2)}) async-start(bf16[4,2,46080]{2,1,0:T(2,128)(2,1)} %reshape.341), calls=%async_computation.3 | async-start | bytes 1474560 | tf_op jit(solution)/shard_map/all_to_all | solution.py:104
  160.6 10.2 %bitcast_convert_fusion.1 = bf16[4,3,360,256]{3,0,2,1:T(4,128)(2,1)} fusion(bf16[10,7,360,256]{3,2,0,1:T(8,128)(2,1)} %fusion.41, bf16[4,3,10,7,1]{2,3,1,0,4:T(8,128)(2,1)S(1)} %fusion.101), kind=kOutput, calls=%fused_computation.6 | convolution fusion | flops 155934720 | bytes 15115920 | tf_op jit(solution)/shard_map/ibrd,rdjc->ibjc/dot_general | solution.py:133
  170.8 5.5 reshape.303
  194.3 5.1 all-to-all-start.4
  199.6 6.6 %collective-permute-start.5 = (bf16[3,360,256]{2,1,0:T(8,128)(2,1)}, bf16[3,360,256]{2,1,0:T(8,128)(2,1)S(1)}, u32[]{:S(2)}, u32[]{:S(2)}) collective-permute-start(bf16[3,360,256]{2,1,0:T(8,128)(2,1)} %get-tuple-element.31), channel_id=1, source_target_pairs={{8,0},{16,8},{24,16},{32,24},{40,32},{48,40},{56,48},{64,56},{72,6... | collective-permute-start | bytes 1658888 | tf_op jit(solution)/shard_map/ppermute | solution.py:25
  206.3 5.3 fusion.91
  211.6 39.4 %collective-permute-done.4 = bf16[3,360,256]{2,1,0:T(8,128)(2,1)S(1)} collective-permute-done((bf16[3,360,256]{2,1,0:T(8,128)(2,1)}, bf16[3,360,256]{2,1,0:T(8,128)(2,1)S(1)}, u32[]{:S(2)}, u32[]{:S(2)}) %collective-permute-start.4) | collective-permute-done | bytes 552992 | tf_op jit(solution)/shard_map/ppermute | solution.py:24
  251.0 8.9 %collective-permute-done.5 = bf16[3,360,256]{2,1,0:T(8,128)(2,1)S(1)} collective-permute-done((bf16[3,360,256]{2,1,0:T(8,128)(2,1)}, bf16[3,360,256]{2,1,0:T(8,128)(2,1)S(1)}, u32[]{:S(2)}, u32[]{:S(2)}) %collective-permute-start.5) | collective-permute-done | bytes 552992 | tf_op jit(solution)/shard_map/ppermute | solution.py:25
  280.2 12.2 %all-to-all-start.5 = ((bf16[4,384,128]{2,0,1:T(4,128)(2,1)}), bf16[4,384,128]{2,0,1:T(4,128)(2,1)S(1)}, u32[]{:S(2)}, u32[]{:S(2)}) async-start(bf16[4,384,128]{2,0,1:T(4,128)(2,1)} %copy.246), calls=%async_computation.5 | async-start | bytes 786432 | tf_op jit(solution)/shard_map/all_to_all | solution.py:61
  297.6 8.8 %all-to-all-done.5 = bf16[4,384,128]{2,0,1:T(4,128)(2,1)S(1)} async-done(((bf16[4,384,128]{2,0,1:T(4,128)(2,1)}), bf16[4,384,128]{2,0,1:T(4,128)(2,1)S(1)}, u32[]{:S(2)}, u32[]{:S(2)}) %all-to-all-start.5) | async-done | bytes 393248 | tf_op jit(solution)/shard_map/all_to_all | solution.py:61
  311.4 5.6 all-to-all-start.6
  322.7 10.9 %all-to-all-done.6 = bf16[12,128,128]{2,0,1:T(8,128)(2,1)} async-done(((bf16[12,128,128]{2,0,1:T(8,128)(2,1)}), bf16[12,128,128]{2,0,1:T(8,128)(2,1)}, u32[]{:S(2)}, u32[]{:S(2)}) %all-to-all-start.6) | async-done | bytes 393248 | tf_op jit(solution)/shard_map/all_to_all | solution.py:61
  347.7 25.1 %fusion.14 = bf16[4,3,360,256]{3,0,1,2:T(4,128)(2,1)} fusion(bf16[10,7,360,256,1]{3,2,0,1,4:T(8,128)(2,1)} %bitcast.296, bf16[10,3,4,7,1]{3,2,1,0,4:T(4,128)(2,1)S(1)} %copy-done.21), kind=kOutput, calls=%fused_computation.23 | convolution fusion | flops 155934720 | bytes 15115920 | tf_op jit(solution)/shard_map/ibrd,idjc->rbjc/dot_general | solution.py:166
  382.7 198.4 %all-reduce.5.cloned.1.call-done = (f32[3,2,128,128]{2,3,0,1:T(8,128)}, f32[384,256]{0,1:T(8,128)}) async-done(((f32[3,2,128,128]{2,3,0,1:T(8,128)}, f32[384,256]{0,1:T(8,128)}), (f32[3,2,128,128]{2,3,0,1:T(8,128)}, f32[384,256]{0,1:T(8,128)})) %all-reduce.5.cloned.1.call-update) | async-done | bytes 786448 | tf_op jit(solution)/shard_map/psum | solution.py:180
  (164 shorter events, 139.3 us)
Async XLA Ops:
  7.2 110.9 %copy-start = (bf16[12,384,128]{2,1,0:T(8,128)(2,1)S(1)}, bf16[12,384,128]{2,1,0:T(8,128)(2,1)}, u32[]{:S(2)}) copy-start(bf16[12,384,128]{2,1,0:T(8,128)(2,1)} %param.13) | copy-start | bytes 3538948
  9.6 26.6 %collective-permute-start = (bf16[3,360,256]{2,1,0:T(8,128)(2,1)}, bf16[3,360,256]{2,1,0:T(8,128)(2,1)S(1)}, u32[]{:S(2)}, u32[]{:S(2)}) collective-permute-start(bf16[3,360,256]{2,1,0:T(8,128)(2,1)} %get-tuple-element.32), channel_id=1, source_target_pairs={{0,8},{8,16},{16,24},{24,32},{32,40},{40,48},{48,56},{56,64},{64,7... | collective-permute-start | bytes 1658888 | tf_op jit(solution)/shard_map/ppermute | solution.py:24
  16.9 48.8 %collective-permute-start.1 = (bf16[3,360,256]{2,1,0:T(8,128)(2,1)}, bf16[3,360,256]{2,1,0:T(8,128)(2,1)}, u32[]{:S(2)}, u32[]{:S(2)}) collective-permute-start(bf16[3,360,256]{2,1,0:T(8,128)(2,1)} %get-tuple-element.33), channel_id=1, source_target_pairs={{8,0},{16,8},{24,16},{32,24},{40,32},{48,40},{56,48},{64,56},{72,6... | collective-permute-start | bytes 1658888 | tf_op jit(solution)/shard_map/ppermute | solution.py:25
  18.3 65.2 %all-to-all-start = ((bf16[4,360,256]{1,0,2:T(4,128)(2,1)}), bf16[4,360,256]{1,0,2:T(4,128)(2,1)}, u32[]{:S(2)}, u32[]{:S(2)}) async-start(bf16[4,360,256]{1,0,2:T(4,128)(2,1)} %copy.219), calls=%async_computation | async-start | bytes 1572864 | tf_op jit(solution)/shard_map/all_to_all | solution.py:74
  36.1 36.8 %copy-start.5 = (bf16[1,4,360,256]{3,2,1,0:T(8,128)(2,1)S(1)}, bf16[1,4,360,256]{3,2,1,0:T(8,128)(2,1)}, u32[]{:S(2)}) copy-start(bf16[1,4,360,256]{3,2,1,0:T(8,128)(2,1)} %param.9) | copy-start | bytes 2211844
  36.2 82.6 %copy-start.18 = (f32[12,384]{1,0:T(8,128)}, f32[12,384]{1,0:T(8,128)S(1)}, u32[]{:S(2)}) copy-start(f32[12,384]{1,0:T(8,128)S(1)} %fusion.109) | copy-start | bytes 55300
  36.2 38.6 %copy-start.9 = (bf16[3,360,256]{2,1,0:T(8,128)(2,1)}, bf16[3,360,256]{2,1,0:T(8,128)(2,1)S(1)}, u32[]{:S(2)}) copy-start(bf16[3,360,256]{2,1,0:T(8,128)(2,1)S(1)} %collective-permute-done) | copy-start | bytes 1658884
  66.4 13.0 %collective-permute-start.2 = (bf16[10,3,256]{2,1,0:T(4,128)(2,1)S(1)}, bf16[10,3,256]{2,1,0:T(4,128)(2,1)S(1)}, u32[]{:S(2)}, u32[]{:S(2)}) collective-permute-start(bf16[10,3,256]{2,1,0:T(4,128)(2,1)S(1)} %get-tuple-element.28), channel_id=1, source_target_pairs={{0,2},{2,4},{4,6},{6,0},{1,3},{3,5},{5,7},{7,1},{8,10},{10,12},{12... | collective-permute-start | bytes 46088 | tf_op jit(solution)/shard_map/ppermute | solution.py:24
  71.6 7.8 %collective-permute-start.3 = (bf16[10,3,256]{2,1,0:T(4,128)(2,1)S(1)}, bf16[10,3,256]{2,1,0:T(4,128)(2,1)S(1)}, u32[]{:S(2)}, u32[]{:S(2)}) collective-permute-start(bf16[10,3,256]{2,1,0:T(4,128)(2,1)S(1)} %get-tuple-element.29), channel_id=1, source_target_pairs={{2,0},{4,2},{6,4},{0,6},{3,1},{5,3},{7,5},{1,7},{10,8},{12,10},{14... | collective-permute-start | bytes 46088 | tf_op jit(solution)/shard_map/ppermute | solution.py:25
  92.3 25.6 %all-to-all-start.1 = ((bf16[4,384,128]{2,0,1:T(4,128)(2,1)}), bf16[4,384,128]{2,0,1:T(4,128)(2,1)S(1)}, u32[]{:S(2)}, u32[]{:S(2)}) async-start(bf16[4,384,128]{2,0,1:T(4,128)(2,1)} %copy.223), calls=%async_computation.1 | async-start | bytes 786432 | tf_op jit(solution)/shard_map/all_to_all | solution.py:61
  122.0 19.6 %all-to-all-start.2 = ((bf16[12,128,128]{2,0,1:T(8,128)(2,1)}), bf16[12,128,128]{2,0,1:T(8,128)(2,1)}, u32[]{:S(2)}, u32[]{:S(2)}) async-start(bf16[12,128,128]{2,0,1:T(8,128)(2,1)} %copy.227), calls=%async_computation.2 | async-start | bytes 1048576 | tf_op jit(solution)/shard_map/all_to_all | solution.py:61
  151.3 29.3 %all-to-all-start.3 = ((bf16[4,2,46080]{2,1,0:T(2,128)(2,1)}), bf16[4,2,46080]{2,1,0:T(2,128)(2,1)S(1)}, u32[]{:S(2)}, u32[]{:S(2)}) async-start(bf16[4,2,46080]{2,1,0:T(2,128)(2,1)} %reshape.341), calls=%async_computation.3 | async-start | bytes 1474560 | tf_op jit(solution)/shard_map/all_to_all | solution.py:104
  190.4 69.5 %copy-start.1 = (bf16[4,360,256]{2,1,0:T(8,128)(2,1)}, bf16[4,360,256]{2,1,0:T(8,128)(2,1)S(1)}, u32[]{:S(2)}) copy-start(bf16[4,360,256]{2,1,0:T(8,128)(2,1)S(1)} %fusion.63) | copy-start | bytes 2211844
  194.3 77.0 %all-to-all-start.4 = ((bf16[4,360,256]{1,0,2:T(4,128)(2,1)}), bf16[4,360,256]{1,0,2:T(4,128)(2,1)}, u32[]{:S(2)}, u32[]{:S(2)}) async-start(bf16[4,360,256]{1,0,2:T(4,128)(2,1)} %copy.242), calls=%async_computation.4 | async-start | bytes 1572864 | tf_op jit(solution)/shard_map/all_to_all | solution.py:74
  199.4 51.5 %collective-permute-start.4 = (bf16[3,360,256]{2,1,0:T(8,128)(2,1)}, bf16[3,360,256]{2,1,0:T(8,128)(2,1)S(1)}, u32[]{:S(2)}, u32[]{:S(2)}) collective-permute-start(bf16[3,360,256]{2,1,0:T(8,128)(2,1)} %get-tuple-element.30), channel_id=1, source_target_pairs={{0,8},{8,16},{16,24},{24,32},{32,40},{40,48},{48,56},{56,64},{64,7... | collective-permute-start | bytes 1658888 | tf_op jit(solution)/shard_map/ppermute | solution.py:24
  199.6 60.3 %collective-permute-start.5 = (bf16[3,360,256]{2,1,0:T(8,128)(2,1)}, bf16[3,360,256]{2,1,0:T(8,128)(2,1)S(1)}, u32[]{:S(2)}, u32[]{:S(2)}) collective-permute-start(bf16[3,360,256]{2,1,0:T(8,128)(2,1)} %get-tuple-element.31), channel_id=1, source_target_pairs={{8,0},{16,8},{24,16},{32,24},{40,32},{48,40},{56,48},{64,56},{72,6... | collective-permute-start | bytes 1658888 | tf_op jit(solution)/shard_map/ppermute | solution.py:25
  206.2 58.6 %copy-start.8 = (bf16[1,4,360,256]{2,3,1,0:T(8,128)(2,1)S(1)}, bf16[1,4,360,256]{2,3,1,0:T(8,128)(2,1)}, u32[]{:S(2)}) copy-start(bf16[1,4,360,256]{2,3,1,0:T(8,128)(2,1)} %copy.218) | copy-start | bytes 2211844
  211.5 53.3 %copy-start.7 = (f32[4,360,2,128]{1,3,2,0:T(8,128)S(1)}, f32[4,360,2,128]{1,3,2,0:T(8,128)}, u32[]{:S(2)}) copy-start(f32[4,360,2,128]{1,3,2,0:T(8,128)} %copy.289) | copy-start | bytes 4423684
  260.6 6.1 %collective-permute-start.6 = (bf16[10,3,256]{2,1,0:T(4,128)(2,1)}, bf16[10,3,256]{2,1,0:T(4,128)(2,1)}, u32[]{:S(2)}, u32[]{:S(2)}) collective-permute-start(bf16[10,3,256]{2,1,0:T(4,128)(2,1)} %get-tuple-element.26), channel_id=1, source_target_pairs={{0,2},{2,4},{4,6},{6,0},{1,3},{3,5},{5,7},{7,1},{8,10},{10,12},{12... | collective-permute-start | bytes 46088 | tf_op jit(solution)/shard_map/ppermute | solution.py:24
  260.6 6.9 %collective-permute-start.7 = (bf16[10,3,256]{2,1,0:T(4,128)(2,1)}, bf16[10,3,256]{2,1,0:T(4,128)(2,1)}, u32[]{:S(2)}, u32[]{:S(2)}) collective-permute-start(bf16[10,3,256]{2,1,0:T(4,128)(2,1)} %get-tuple-element.27), channel_id=1, source_target_pairs={{2,0},{4,2},{6,4},{0,6},{3,1},{5,3},{7,5},{1,7},{10,8},{12,10},{14... | collective-permute-start | bytes 46088 | tf_op jit(solution)/shard_map/ppermute | solution.py:25
  280.2 26.2 %all-to-all-start.5 = ((bf16[4,384,128]{2,0,1:T(4,128)(2,1)}), bf16[4,384,128]{2,0,1:T(4,128)(2,1)S(1)}, u32[]{:S(2)}, u32[]{:S(2)}) async-start(bf16[4,384,128]{2,0,1:T(4,128)(2,1)} %copy.246), calls=%async_computation.5 | async-start | bytes 786432 | tf_op jit(solution)/shard_map/all_to_all | solution.py:61
  311.4 22.2 %all-to-all-start.6 = ((bf16[12,128,128]{2,0,1:T(8,128)(2,1)}), bf16[12,128,128]{2,0,1:T(8,128)(2,1)}, u32[]{:S(2)}, u32[]{:S(2)}) async-start(bf16[12,128,128]{2,0,1:T(8,128)(2,1)} %copy.249), calls=%async_computation.6 | async-start | bytes 1048576 | tf_op jit(solution)/shard_map/all_to_all | solution.py:61
  317.0 264.1 %all-reduce.5.cloned.1.call-start = ((), (), s32[]{:S(2)}) async-start(), calls=%async_computation.8 | async-start | bytes 1572864 | tf_op jit(solution)/shard_map/psum | solution.py:180
  343.4 241.2 %all-to-all-start.7 = ((bf16[4,2,46080]{2,1,0:T(2,128)(2,1)}), bf16[4,2,46080]{2,1,0:T(2,128)(2,1)}, u32[]{:S(2)}, u32[]{:S(2)}) async-start(bf16[4,2,46080]{2,1,0:T(2,128)(2,1)} %reshape.343), calls=%async_computation.7 | async-start | bytes 1474560 | tf_op jit(solution)/shard_map/all_to_all | solution.py:104
  (20 other events, 151.6 us)
Sparse Core Ops, SparseCore 0:
  324.1 256.9 all-reduce.4
where the time goes:
time: 612 us; the launch traced here: 603 us
  waiting for transfers between devices  318 us (52%)
  local copies, waits for them, and re-layouts  97.9 us (16%)
  starting transfers between devices  84.3 us (14%)
  matrix products  61.9 us (10%)
  other arithmetic  25.9 us (4%)
  between operations  14.7 us (2%)
    psum x1, waiting for transfers between devices, on_device(): lax.psum((mix_part, full_gain), ('lat', 'lon', 'ens'))  198 us
    ppermute x4, waiting for transfers between devices, padded_2(): before = lax.ppermute(last, axis, up)  44 us
    ppermute x4, waiting for transfers between devices, padded_2(): after = lax.ppermute(initial, axis, down)  39.2 us
    unnamed x75, local copies, waits for them, and re-layouts  36.5 us
    all_to_all x4, starting transfers between devices, to_owners(): lax.all_to_all(blocks, 'lat', split_axis=1, concat_axis=0, tiled=True)  36.4 us
    all_to_all x4, waiting for transfers between devices, to_owners(): lax.all_to_all(blocks, 'lat', split_axis=1, concat_axis=0, tiled=True)  36.1 us
    dot_general x1, matrix products, on_device(): jnp.einsum('ibrd,idjc->rbjc', backward_band, stacked_back, preferred_elem...  25.1 us
    all_to_all x2, starting transfers between devices, spectral(): lax.all_to_all(spectrum, 'lon', split_axis=1, concat_axis=2, tiled=True)  13.7 us
  transfers between devices with their start and end apart: 17, of which 11 were waited for; matrix products, arithmetic and copies ran while one was open for 20% of the time, Pallas kernels for 0%

commit v1 on v0

v1 whole, which is shorter than its diff:
```python
import math

import jax
import jax.numpy as jnp
from jax import lax
from jax.experimental import pallas as pl
from jax.experimental.pallas import tpu as pltpu
from jax.sharding import PartitionSpec as P

LONGITUDES = 1440
BAND_REACH = 3
SUPPORT = 4
HALF = 64
LANES = 128
BLOCK = 32
WINDOW = 48
CHUNK = 48

bf16 = jnp.bfloat16
f32 = jnp.float32
highest = lax.Precision.HIGHEST
far_below = -1000000


def call(kernel, out_shape, args, flops, scratch=(), smem=(), limit=24):
    moved = sum(a.size * a.dtype.itemsize for a in args)
    moved += sum(math.prod(o.shape) * o.dtype.itemsize for o in out_shape)
    specs = [
        pl.BlockSpec(memory_space=pltpu.SMEM if i in smem else pltpu.VMEM)
        for i in range(len(args))
    ]
    return pl.pallas_call(
        kernel,
        out_shape=out_shape,
        in_specs=specs,
        out_specs=[pl.BlockSpec(memory_space=pltpu.VMEM) for _ in out_shape],
        scratch_shapes=list(scratch),
        compiler_params=pltpu.CompilerParams(vmem_limit_bytes=limit * 1024 * 1024),
        cost_estimate=pl.CostEstimate(
            flops=int(flops), bytes_accessed=int(moved), transcendentals=0
        ),
    )(*args)


def dot(a, b):
    return lax.dot_general(a, b, (((1,), (0,)), ((), ())), preferred_element_type=f32)


def swap_pair(first, second):
    left = lax.broadcasted_iota(jnp.int32, first.shape, 1) < HALF
    low = jnp.where(left, first, pltpu.roll(second, HALF, 1))
    high = jnp.where(left, pltpu.roll(first, HALF, 1), second)
    return low, high


def chunks(rows):
    return [(first, min(CHUNK, rows - first)) for first in range(0, rows, CHUNK)]


def pieces(rows):
    for first, count in chunks(rows):
        for a in range(2):
            for v in range(2):
                yield pl.ds(first, count), a, v, pl.ds(a * LANES, LANES), pl.ds(v * LANES, LANES)


def pack_kernel(x_ref, out_ref):
    for rows, a, v, at, av in pieces(x_ref.shape[1]):
        low, high = swap_pair(
            x_ref[2 * a, rows, av].astype(f32), x_ref[2 * a + 1, rows, av].astype(f32)
        )
        out_ref[2 * v, rows, at] = low.astype(bf16)
        out_ref[2 * v + 1, rows, at] = high.astype(bf16)


def analysis_kernel(circle_ref, wave_ref, *rest):
    extra_ref = rest[0] if len(rest) == 3 else None
    out_ref, rows_ref = rest[-2:]
    waves = wave_ref.shape[1] // 2
    sums = []
    for r in range(2):
        total = dot(wave_ref[0, r * waves : (r + 1) * waves, :], circle_ref[0])
        for s in range(1, wave_ref.shape[0]):
            total += dot(wave_ref[s, r * waves : (r + 1) * waves, :], circle_ref[s])
        sums.append(total)
    for a in range(2):
        lanes = slice(a * LANES, (a + 1) * LANES)
        low, high = swap_pair(sums[0][:, lanes], sums[1][:, lanes])
        rows_ref[pl.ds(2 * a, waves, stride=4), :] = low
        rows_ref[pl.ds(2 * a + 1, waves, stride=4), :] = high
    peers = out_ref.shape[0]
    main = 4 * waves // peers
    out_ref[:, 0:main, :] = rows_ref[...].reshape(peers, main, LANES).astype(bf16)
    if extra_ref is not None:
        out_ref[:, main:, :] = extra_ref[...]


def legendre_steps(order_ref, rows_in_ref, leg_ref, leg_turned_ref, gain_ref, rows_out_ref, peers, use):
    owned, degrees = leg_ref.shape[0], leg_ref.shape[1]
    step = 4 * owned
    degree = lax.broadcasted_iota(jnp.int32, (degrees, LANES), 0)
    for k in range(owned):
        field = jnp.concatenate(
            [rows_in_ref[pl.ds(4 * k + t, peers, stride=step), :] for t in range(4)], axis=0
        ).astype(bf16)
        coeffs = dot(leg_ref[k], field)
        coeffs = jnp.where(degree >= order_ref[k], coeffs, 0.0)
        use(k, coeffs)
        weighted = (coeffs * gain_ref[...]).astype(bf16)
        synthesis = dot(leg_turned_ref[k], weighted)
        for t in range(4):
            rows_out_ref[pl.ds(4 * k + t, peers, stride=step), :] = synthesis[
                t * peers : (t + 1) * peers
            ]


def legendre_forward_kernel(
    order_ref, got_ref, leg_ref, leg_turned_ref, gain_ref, out_ref, coeffs_ref, rows_in_ref, rows_out_ref
):
    peers = got_ref.shape[0]
    main = rows_in_ref.shape[0] // peers
    rows_in_ref[...] = got_ref[...].astype(f32).reshape(peers * main, LANES)

    def use(k, coeffs):
        coeffs_ref[k] = coeffs

    legendre_steps(order_ref, rows_in_ref, leg_ref, leg_turned_ref, gain_ref, rows_out_ref, peers, use)
    out_ref[...] = rows_out_ref[...].reshape(peers, main, LANES).astype(bf16)


def legendre_backward_kernel(
    order_ref, got_ref, leg_ref, leg_turned_ref, gain_ref, coeffs_ref, out_ref, rows_in_ref, rows_out_ref, sum_ref
):
    peers = got_ref.shape[0]
    main = rows_in_ref.shape[0] // peers
    rows_in_ref[...] = got_ref[:, 0:main, :].astype(f32).reshape(peers * main, LANES)

    def use(k, coeffs):
        term = coeffs * coeffs_ref[k]
        if k == 0:
            sum_ref[...] = term
        else:
            sum_ref[...] += term

    legendre_steps(order_ref, rows_in_ref, leg_ref, leg_turned_ref, gain_ref, rows_out_ref, peers, use)
    out_ref[:, 0:main, :] = rows_out_ref[...].reshape(peers, main, LANES).astype(bf16)
    total = sum_ref[...]
    total = total + pltpu.roll(total, HALF, 1)
    half = total.shape[0] // 2
    left = lax.broadcasted_iota(jnp.int32, (half, LANES), 1) < HALF
    packed = jnp.where(left, total[:half], total[half:])
    high = packed.astype(bf16).astype(f32)
    low = packed - high
    used = half // 8
    both = jnp.concatenate([high.reshape(used, 8, LANES), low.reshape(used, 8, LANES)], axis=1)
    out_ref[0:used, main : main + 16, :] = both.astype(bf16)
    if used < peers:
        out_ref[used:peers, main : main + 16, :] = jnp.zeros((peers - used, 16, LANES), bf16)


def synthesis_kernel(got_ref, wave_ref, out_ref, rows_ref):
    waves = wave_ref.shape[2] // 2
    peers = got_ref.shape[0]
    main = 4 * waves // peers
    rows_ref[...] = got_ref[:, 0:main, :].astype(f32).reshape(4 * waves, LANES)
    low, high = [], []
    for a in range(2):
        lo, hi = swap_pair(
            rows_ref[pl.ds(2 * a, waves, stride=4), :], rows_ref[pl.ds(2 * a + 1, waves, stride=4), :]
        )
        low.append(lo)
        high.append(hi)
    spectrum = jnp.concatenate(
        [jnp.concatenate(low, axis=1), jnp.concatenate(high, axis=1)], axis=0
    ).astype(bf16)
    for s in range(wave_ref.shape[0]):
        out_ref[s] = dot(wave_ref[s], spectrum).astype(bf16)


def band_kernel(x_ref, toeplitz_ref, mix_ref, *outs):
    mixed_ref = outs[0]
    basis_ref = outs[1] if len(outs) > 1 else None
    kernels = mix_ref.shape[0]
    span, channels = x_ref.shape[0], x_ref.shape[2]
    per_kernel = toeplitz_ref.shape[0] // kernels
    rows = per_kernel // BLOCK

    def step(j, carry):
        start = pl.multiple_of(j * BLOCK, BLOCK)
        window = x_ref[:, pl.ds(start, WINDOW), :].reshape(span * WINDOW, channels)
        basis = dot(toeplitz_ref[...], window).astype(bf16)
        total = None
        for b in range(kernels):
            part = basis[b * per_kernel : (b + 1) * per_kernel]
            if basis_ref is not None:
                basis_ref[b, :, pl.ds(start, BLOCK), :] = part.reshape(rows, BLOCK, channels)
            term = dot(part, mix_ref[b])
            total = term if total is None else total + term
        mixed_ref[:, pl.ds(start, BLOCK), :] = total.reshape(rows, BLOCK, channels)
        return carry

    lax.fori_loop(0, mixed_ref.shape[1] // BLOCK, step, 0)


def activation_kernel(
    spec_ref, mixed_ref, state_ref, cot_ref, next_ref, grad_ref, packed_ref
):
    scale = math.sqrt(2.0 / math.pi)
    for rows, a, v, at, av in pieces(state_ref.shape[1]):
        spectra = swap_pair(spec_ref[2 * v, rows, at].astype(f32), spec_ref[2 * v + 1, rows, at].astype(f32))
        grads = []
        for h in range(2):
            t = 2 * a + h
            value = spectra[h] + mixed_ref[t, rows, av]
            square = value * value
            turn = jnp.tanh(scale * value * (1.0 + 0.044715 * square))
            share = 0.5 + 0.5 * turn
            next_ref[t, rows, av] = (state_ref[t, rows, av].astype(f32) + value * share).astype(bf16)
            slope = share + (0.5 * scale) * value * (1.0 - turn * turn) * (1.0 + (3.0 * 0.044715) * square)
            grad = cot_ref[t, rows, av].astype(f32) * slope
            grad_ref[t, rows, av] = grad.astype(bf16)
            grads.append(grad)
        low, high = swap_pair(*grads)
        packed_ref[2 * v, rows, at] = low.astype(bf16)
        packed_ref[2 * v + 1, rows, at] = high.astype(bf16)


def finish_kernel(spec_ref, back_ref, cot_ref, out_ref):
    for rows, a, v, at, av in pieces(cot_ref.shape[1]):
        spectra = swap_pair(spec_ref[2 * v, rows, at].astype(f32), spec_ref[2 * v + 1, rows, at].astype(f32))
        for h in range(2):
            t = 2 * a + h
            out_ref[t, rows, av] = (
                cot_ref[t, rows, av].astype(f32) + spectra[h] + back_ref[t, rows, av]
            ).astype(bf16)


def mixing_gradient_kernel(basis_ref, grad_ref, out_ref):
    kernels, lat_rows = basis_ref.shape[0], basis_ref.shape[1]
    sector = grad_ref.shape[1]
    for g in range(2):
        lanes = pl.ds(g * LANES, LANES)
        totals = [None] * kernels
        for i in range(lat_rows):
            turned = grad_ref[i, :, lanes].astype(f32).T.astype(bf16)
            for b in range(kernels):
                term = dot(turned, basis_ref[b, i, 0:sector, lanes])
                totals[b] = term if totals[b] is None else totals[b] + term
        for b in range(kernels):
            out_ref[g, b] = totals[b].T


def wave_tables(owner_order, sector, sectors):
    factor = 1.0 / math.sqrt(LONGITUDES)
    n = jnp.arange(sector, dtype=jnp.int32)

    def table(phases, orders, axis):
        angles = (phases % LONGITUDES).astype(f32) * (2.0 * math.pi / LONGITUDES)
        c = jnp.cos(angles) * factor
        s = jnp.sin(angles) * factor
        c, s = lax.optimization_barrier((c, s))
        out = []
        for part in range(sectors):
            turns = (orders * part) % 4
            swap = turns % 2 == 1
            flip_c = jnp.where((turns == 1) | (turns == 2), -1.0, 1.0)
            flip_s = jnp.where((turns == 0) | (turns == 1), -1.0, 1.0)
            cos_part = jnp.where(swap, s, c) * flip_c
            sin_part = jnp.where(swap, c, s) * flip_s
            out.append(jnp.concatenate([cos_part, sin_part], axis=axis))
        return jnp.stack(out).astype(bf16)

    by_wave = table(owner_order[:, None] * n[None, :], owner_order[:, None], 0)
    by_point = table(n[:, None] * owner_order[None, :], owner_order[None, :], 1)
    return by_wave, by_point


def band_table(kernels_pad, offsets_pad, first_in, count_in, first_out, output_count):
    rows_kern = lax.dynamic_slice_in_dim(kernels_pad, first_in + BAND_REACH, count_in, 1)
    rows_start = lax.dynamic_slice_in_dim(offsets_pad, first_in + BAND_REACH, count_in, 0)
    targets = first_out + jnp.arange(output_count, dtype=jnp.int32)
    support_index = jnp.arange(SUPPORT, dtype=jnp.int32)
    matches = (
        rows_start[:, None, None] + support_index[None, :, None] == targets[None, None, :]
    ).astype(f32)
    return jnp.einsum("bikd,ikr->ibrd", rows_kern.astype(f32), matches, precision=highest)


def toeplitz(table, taps_turned):
    b, o, r, d = table.shape
    if taps_turned:
        table = table[..., ::-1]
    n = jnp.arange(BLOCK, dtype=jnp.int32)
    m = jnp.arange(WINDOW, dtype=jnp.int32)
    tap = m[None, :] - n[:, None]
    spread = (tap[None] == jnp.arange(d, dtype=jnp.int32)[:, None, None]).astype(bf16)
    out = jnp.einsum("bord,dnm->bonrm", table.astype(bf16), spread, preferred_element_type=f32)
    return out.astype(bf16).reshape(b * o * BLOCK, r * WINDOW)


def exchange(x, axis):
    return lax.all_to_all(x, axis, split_axis=0, concat_axis=0, tiled=True)


def with_columns(x):
    peers = lax.axis_size("lon")
    width = x.shape[1]
    up = [(i, (i + 1) % peers) for i in range(peers)]
    down = [(j, i) for i, j in up]
    before = lax.ppermute(x[:, width - BAND_REACH :], "lon", up)
    after = lax.ppermute(x[:, :BAND_REACH], "lon", down)
    return jnp.concatenate([before, x, after], axis=1)


def with_rows(x, even, width):
    peers = lax.axis_size("lat")
    pair = [(i, i ^ 1) for i in range(peers)]
    relay = [(i, (i + 2) % peers if i % 2 == 0 else (i - 2) % peers) for i in range(peers)]
    reach = BAND_REACH
    far = lax.ppermute(jnp.where(even, x[:reach], x[1 : reach + 1]), "lat", pair)
    rest = lax.ppermute(jnp.where(even, x[reach:], x[:1]), "lat", pair)
    other = lax.ppermute(far, "lat", relay)
    near = jnp.where(
        even, jnp.concatenate([rest, far[: reach - 1]]), jnp.concatenate([far[1:], rest])
    )
    before = jnp.where(even, other, near)
    after = jnp.where(even, near, other)
    whole = jnp.concatenate([before, x, after], axis=0)
    return jnp.pad(whole, ((0, 0), (0, width - whole.shape[1]), (0, 0)))


def on_device(states, cotangent, kernels, offsets, mixing, legendre, owner_order, spectral_gain):
    fields = states[0]
    cot = cotangent[0]
    lat_rows, sector, channels = fields.shape
    lon_index = lax.axis_index("lon")
    lat_index = lax.axis_index("lat")
    ens_index = lax.axis_index("ens")
    lon_count = lax.axis_size("lon")
    lat_count = lax.axis_size("lat")
    members = states.shape[0] * lax.axis_size("ens")
    lat_first = lat_index * lat_rows
    lat_total = lat_rows * lat_count
    extent = lat_rows + 2 * BAND_REACH
    kernel_number, group_count, width = mixing.shape[0], mixing.shape[1], mixing.shape[2]
    quarter = channels // lon_count
    owned, degrees = legendre.shape[0], legendre.shape[1]
    waves = owner_order.shape[0]
    main = 4 * owned
    even = lat_index % 2 == 0
    blocks = -(-sector // BLOCK)
    padded = blocks * BLOCK
    padded_in = padded + WINDOW - BLOCK
    sds = jax.ShapeDtypeStruct
    field_shape = sds((lat_rows, sector, channels), bf16)
    wide_shape = sds((lat_rows, padded, channels), f32)

    by_wave, by_point = wave_tables(owner_order, sector, lon_count)
    orders = lax.dynamic_slice_in_dim(owner_order, lat_index * owned, owned, 0)
    gains = lax.dynamic_slice_in_dim(spectral_gain, lon_index * quarter, quarter, 1).astype(f32)
    gains = jnp.concatenate([gains, gains], axis=1)
    leg = legendre.reshape(owned, degrees, lat_count, lat_rows)
    leg = jnp.swapaxes(leg, 2, 3).reshape(owned, degrees, lat_total)
    leg_turned = jnp.swapaxes(leg, 1, 2)
    kernels_pad = jnp.pad(kernels, ((0, 0), (BAND_REACH, BAND_REACH), (0, 0), (0, 0)))
    offsets_pad = jnp.pad(offsets, BAND_REACH, constant_values=far_below)
    forward_band = band_table(
        kernels_pad, offsets_pad, lat_first, lat_rows, lat_first - BAND_REACH, extent
    )
    rows_global = lat_first - BAND_REACH + jnp.arange(extent, dtype=jnp.int32)
    inside = (rows_global >= 0) & (rows_global < lat_total)
    forward_band = jnp.where(inside[None, None, :, None], forward_band, 0.0)
    backward_band = band_table(
        kernels_pad, offsets_pad, lat_first - BAND_REACH, extent, lat_first, lat_rows
    )
    forward_matrix = toeplitz(jnp.transpose(forward_band, (1, 0, 2, 3)), False)
    backward_matrix = toeplitz(jnp.transpose(backward_band, (1, 2, 0, 3)), True)
    groups = jnp.eye(group_count, dtype=bf16)
    mix_wide = (mixing[:, :, :, None, :] * groups[None, :, None, :, None]).reshape(
        kernel_number, channels, channels
    )
    mix_turned = jnp.swapaxes(mix_wide, 1, 2)

    transform_flops = 4 * waves * LONGITUDES * lat_rows * quarter
    legendre_flops = 4 * owned * degrees * lat_total * 2 * quarter
    band_flops = 2 * blocks * forward_matrix.size * channels
    row_scratch = pltpu.VMEM((4 * waves, LANES), f32)

    def band(x, matrix, mix, with_basis):
        outs = [wide_shape]
        if with_basis:
            outs.append(sds((kernel_number, lat_rows, padded, channels), bf16))
        return call(band_kernel, outs, (x, matrix, mix), band_flops)

    (packed,) = call(pack_kernel, [field_shape], (fields,), 0)
    circle = exchange(packed, "lon")
    extended = with_columns(fields)
    circle, extended = lax.optimization_barrier((circle, extended))
    (analysed,) = call(
        analysis_kernel,
        [sds((lat_count, main, LANES), bf16)],
        (circle, by_wave),
        transform_flops,
        [row_scratch],
    )
    owned_rows = exchange(analysed, "lat")
    x_padded = with_rows(extended, even, padded_in)
    synthesis, coeffs = call(
        legendre_forward_kernel,
        [sds((lat_count, main, LANES), bf16), sds((owned, degrees, LANES), f32)],
        (orders, owned_rows, leg, leg_turned, gains),
        legendre_flops,
        [row_scratch, row_scratch],
        (0,),
    )
    returned = exchange(synthesis, "lat")
    (spectrum,) = call(
        synthesis_kernel, [sds((lon_count, sector, channels), bf16)], (returned, by_point), transform_flops, [row_scratch]
    )
    spectrum = exchange(spectrum, "lon")
    mixed, basis = band(x_padded, forward_matrix, mix_wide, True)
    next_state, grad_pre, packed_back = call(
        activation_kernel,
        [field_shape, field_shape, field_shape],
        (spectrum, mixed, fields, cot),
        40 * fields.size,
    )

    circle_back = exchange(packed_back, "lon")
    extended_back = with_columns(grad_pre)
    (mix_part,) = call(
        mixing_gradient_kernel,
        [sds((group_count, kernel_number, width, width), f32)],
        (basis, grad_pre),
        2 * kernel_number * fields.size * width,
    )
    mix_part = mix_part.reshape(group_count, kernel_number * width, width)
    swap = [(0, 1), (1, 0)]
    kept = lax.dynamic_index_in_dim(mix_part, ens_index, 0, False)
    sent = lax.dynamic_index_in_dim(mix_part, 1 - ens_index, 0, False)
    mix_half = kept + lax.ppermute(sent, "ens", swap)
    mix_rows = mix_half.shape[0] // lat_count
    mix_high = lax.reduce_precision(mix_half, 8, 7)
    mix_chunks = jnp.concatenate(
        [
            mix_high.reshape(lat_count, mix_rows, width),
            (mix_half - mix_high).reshape(lat_count, mix_rows, width),
        ],
        axis=1,
    ).astype(bf16)
    circle_back, extended_back = lax.optimization_barrier((circle_back, extended_back))
    (analysed_back,) = call(
        analysis_kernel,
        [sds((lat_count, main + 2 * mix_rows, LANES), bf16)],
        (circle_back, by_wave, mix_chunks),
        transform_flops,
        [row_scratch],
    )
    owned_back = exchange(analysed_back, "lat")
    g_padded = with_rows(extended_back, even, padded_in)
    (synthesis_back,) = call(
        legendre_backward_kernel,
        [sds((lat_count, main + 16, LANES), bf16)],
        (orders, owned_back, leg, leg_turned, gains, coeffs),
        legendre_flops,
        [row_scratch, row_scratch, pltpu.VMEM((degrees, LANES), f32)],
        (0,),
    )
    mix_got = jnp.sum(owned_back[:, main:].astype(f32), axis=0)
    mix_got = lax.psum(mix_got[:mix_rows] + mix_got[mix_rows:], "lon")
    returned_back = exchange(synthesis_back, "lat")
    (spectrum_back,) = call(
        synthesis_kernel, [sds((lon_count, sector, channels), bf16)], (returned_back, by_point), transform_flops, [row_scratch]
    )
    gain_got = jnp.sum(returned_back[:, main:].astype(f32), axis=0)
    gain_got = gain_got[:8] + gain_got[8:]
    spectrum_back = exchange(spectrum_back, "lon")
    (backward,) = band(g_padded, backward_matrix, mix_turned, False)
    (grad_state,) = call(
        finish_kernel, [field_shape], (spectrum_back, backward, cot), 4 * fields.size
    )

    mix_scale = 1.0 / math.sqrt(members * lat_total * LONGITUDES)
    gain_scale = 1.0 / math.sqrt(2 * members * degrees)
    pieces_here = jnp.concatenate([gain_got, mix_got], axis=0)
    pieces_all = lax.all_gather(pieces_here, "lat", axis=0)
    gain_half = pieces_all[: degrees // 16, :8].reshape(degrees // 2, LANES)
    mix_mine = pieces_all[:, 8:].reshape(kernel_number * width, width)
    both = jnp.concatenate([gain_half, mix_mine], axis=0)
    other = lax.ppermute(both, "ens", swap)
    gain_sum = (gain_half + other[: degrees // 2]) * gain_scale
    grad_gain = jnp.concatenate([gain_sum[:, :quarter], gain_sum[:, quarter:]], axis=0)
    mix_other = other[degrees // 2 :]
    first = ens_index == 0
    mix_all = jnp.stack([jnp.where(first, mix_mine, mix_other), jnp.where(first, mix_other, mix_mine)])
    mix_all = mix_all.reshape(group_count, kernel_number, width, width) * mix_scale
    grad_mixing = jnp.swapaxes(mix_all, 0, 1)
    return (next_state[None], grad_state[None], grad_mixing, grad_gain)


def solution(mesh):
    in_specs = (
        P("ens", "lat", "lon", None),
        P("ens", "lat", "lon", None),
        P(),
        P(),
        P(),
        P("lat", None, None),
        P(),
        P(),
    )
    out_specs = (P("ens", "lat", "lon", None), P("ens", "lat", "lon", None), P(), P(None, "lon"))
    return jax.shard_map(
        on_device, mesh=mesh, in_specs=in_specs, out_specs=out_specs, check_vma=False
    )
```

time: 612 us -> 426 us (0.70)
  waiting for transfers between devices: 318 us -> 67.9 us
  blocking collectives: 0 us -> 123 us
  matrix products: 61.9 us -> 5.37 us
  Pallas kernels: 0 us -> 31.6 us
  local copies, waits for them, and re-layouts: 97.9 us -> 67.4 us
  other arithmetic: 25.9 us -> 40.5 us
  between operations: 14.7 us -> 1.32 us
    psum x1 -> x0, waiting for transfers between devices: 198 us -> none  [on_device(): lax.psum((mix_part, full_gain), ('lat', 'lon', 'ens'))]
    all_gather x0 -> x1, blocking collectives: none -> 113 us  [on_device(): pieces_all = lax.all_gather(pieces_here, 'lat', axis=0)]
    dot_general x15 -> x4, matrix products: 61.9 us -> 5.37 us  [the longest x2 4.3 us: toeplitz(): jnp.einsum('bord,dnm->bonrm', table.astype(bf16), spread, preferred_eleme...]
    all_to_all x8, waiting for transfers between devices: 36.6 us -> 4.9 us  [exchange(): return lax.all_to_all(x, axis, split_axis=0, concat_axis=0, tiled=True)]
    pallas_call x0 -> x12, Pallas kernels: none -> 31.6 us  [call(): pl.pallas_call(kernel, out_shape=out_shape, in_specs=specs, out_specs=[pl...]
    convert_element_type x13 -> x0, local copies, waits for them, and re-layouts: 22 us -> none  [the longest x2 6.04 us: spectral(): spectrum = jnp.einsum('ktrc,nkr->tnc', returned.reshape(owned_total, lat_...]
    ppermute x8 -> x12, waiting for transfers between devices: 83.2 us -> 63 us  [the longest x2 38.3 us: with_rows(): far = lax.ppermute(jnp.where(even, x[:reach], x[1:reach + 1]), 'lat', pair)]
    all_to_all x12 -> x0, local copies, waits for them, and re-layouts: 13.4 us -> none  [the longest x6 10.5 us: spectral(): lax.all_to_all(fields, 'lon', split_axis=2, concat_axis=1, tiled=True)]
  transfers between devices with their start and end apart: 17 -> 20, of which waited for: 11 -> 7; matrix products, arithmetic and copies ran while one was open for 20% -> 20% of each run, Pallas kernels for 0% -> 5%
where the time goes in v1:
time: 426 us; the launch traced here: 420 us
  blocking collectives  123 us (29%)
  starting transfers between devices  82.4 us (19%)
  waiting for transfers between devices  67.9 us (16%)
  local copies, waits for them, and re-layouts  67.4 us (16%)
  other arithmetic  40.5 us (10%)
  Pallas kernels  31.6 us (7%)
  matrix products  5.37 us (1%)
    all_gather x1, blocking collectives, on_device(): pieces_all = lax.all_gather(pieces_here, 'lat', axis=0)  113 us
    all_to_all x8, starting transfers between devices, exchange(): return lax.all_to_all(x, axis, split_axis=0, concat_axis=0, tiled=True)  52.6 us
    ppermute x2, waiting for transfers between devices, with_rows(): far = lax.ppermute(jnp.where(even, x[:reach], x[1:reach + 1]), 'lat', pair)  38.3 us
    unnamed x126, local copies, waits for them, and re-layouts  33.4 us
    pallas_call x12, Pallas kernels, call(): pl.pallas_call(kernel, out_shape=out_shape, in_specs=specs, out_specs=[pl...  31.6 us
    ppermute x2, waiting for transfers between devices, with_rows(): rest = lax.ppermute(jnp.where(even, x[reach:], x[:1]), 'lat', pair)  24.1 us
    reshape x4, local copies, waits for them, and re-layouts, toeplitz(): return out.astype(bf16).reshape(b * o * BLOCK, r * WINDOW)  12 us
    ppermute x2, starting transfers between devices, with_rows(): far = lax.ppermute(jnp.where(even, x[:reach], x[1:reach + 1]), 'lat', pair)  10.8 us
  transfers between devices with their start and end apart: 20, of which 7 were waited for; matrix products, arithmetic and copies ran while one was open for 20% of the time, Pallas kernels for 5%

profile of v1, /device:TPU:2, one launch (start us, length us, event | category | flops | bytes accessed | tf_op | source)
XLA Modules:
  0.0 419.8 jit_solution(12256934175552395402)
XLA Ops:
  8.5 3.6 all-to-all-start
  13.8 3.2 sine_multiply_fusion.1
  27.5 3.7 all-to-all-done.circle_ref
  33.1 13.1 %all-to-all-start.1 = ((bf16[32,48,128]{2,1,0:T(8,128)(2,1)}), bf16[32,48,128]{2,1,0:T(8,128)(2,1)}, u32[]{:S(2)}, u32[]{:S(2)}) async-start(bf16[32,48,128]{2,1,0:T(8,128)(2,1)} %shard_map.112), calls=%async_computation.1 | async-start | bytes 786432 | tf_op jit(solution)/shard_map/all_to_all | solution.py:302
  59.3 5.4 %collective-permute-start.2 = (bf16[3,366,256]{2,1,0:T(8,128)(2,1)}, bf16[3,366,256]{2,1,0:T(8,128)(2,1)}, u32[]{:S(2)}, u32[]{:S(2)}) collective-permute-start(bf16[3,366,256]{2,1,0:T(8,128)(2,1)} %slice_select_fusion.1), channel_id=1, source_target_pairs={{0,8},{8,0},{16,24},{24,16},{32,40},{40,32},{48,56},{56,48},{64,72... | collective-permute-start | bytes 1686536 | tf_op jit(solution)/shard_map/ppermute | solution.py:320
  71.4 7.4 %all-to-all-start.2 = ((bf16[32,48,128]{2,1,0:T(8,128)(2,1)}), bf16[32,48,128]{2,1,0:T(8,128)(2,1)}, u32[]{:S(2)}, u32[]{:S(2)}) async-start(bf16[32,48,128]{2,1,0:T(8,128)(2,1)} %copy-done.31), calls=%async_computation.2 | async-start | bytes 786432 | tf_op jit(solution)/shard_map/all_to_all | solution.py:302
  89.8 5.6 %collective-permute-done.2 = bf16[3,366,256]{2,1,0:T(8,128)(2,1)} collective-permute-done((bf16[3,366,256]{2,1,0:T(8,128)(2,1)}, bf16[3,366,256]{2,1,0:T(8,128)(2,1)}, u32[]{:S(2)}, u32[]{:S(2)}) %collective-permute-start.2) | collective-permute-done | bytes 562208 | tf_op jit(solution)/shard_map/ppermute | solution.py:320
  103.4 3.0 reshape.325.toeplitz_ref
  110.8 4.2 all-to-all-start.3
  119.0 13.2 %collective-permute-done.4 = bf16[1,366,256]{2,1,0:T(8,128)(2,1)S(1)} collective-permute-done((bf16[1,366,256]{2,1,0:T(8,128)(2,1)S(1)}, bf16[1,366,256]{2,1,0:T(8,128)(2,1)S(1)}, u32[]{:S(2)}, u32[]{:S(2)}) %collective-permute-start.4) | collective-permute-done | bytes 187424 | tf_op jit(solution)/shard_map/ppermute | solution.py:321
  134.6 5.7 %shard_map.115 = (f32[4,384,256]{2,1,0:T(8,128)S(1)}, bf16[3,4,384,256]{3,2,1,0:T(8,128)(2,1)S(1)}) custom-call(bf16[10,400,256]{2,1,0:T(8,128)(2,1)S(1)} %fusion.7.x_ref, bf16[384,480]{1,0:T(8,128)(2,1)S(1)} %copy-done.32, bf16[3,256,256]{2,1,0:T(8,128)(2,1)S(1)} %copy-done.30), custom_call_target="tpu_custom_call" | custom-call | flops 1132462080 | bytes 6742016 | tf_op jit(solution)/shard_map/pallas_call | solution.py:32
  146.5 4.7 %shard_map.116 = (bf16[4,360,256]{2,1,0:T(8,128)(2,1)}, bf16[4,360,256]{2,1,0:T(8,128)(2,1)S(1)}, bf16[4,360,256]{2,1,0:T(8,128)(2,1)S(1)}) custom-call(bf16[4,360,256]{2,1,0:T(8,128)(2,1)} %all-to-all-done.3.spec_ref, f32[4,384,256]{2,1,0:T(8,128)S(1)} %copy-done.25, bf16[4,360,256]{2,1,0:T(8,128)(2,1)S(1)} %bitcast.89, bf16[4,360,256]{2,1,0:T(8,128)(2,1)S(1)} %bitcast.90), custom_call_target="tpu_custom_call" | custom-call | flops 14745600 | bytes 5996544 | tf_op jit(solution)/shard_map/pallas_call | solution.py:32
  153.0 4.9 %all-to-all-start.4 = ((bf16[4,360,256]{2,1,0:T(8,128)(2,1)}), bf16[4,360,256]{2,1,0:T(8,128)(2,1)}, u32[]{:S(2)}, u32[]{:S(2)}) async-start(bf16[4,360,256]{2,1,0:T(8,128)(2,1)} %copy-done.29), calls=%async_computation.4 | async-start | bytes 1474560 | tf_op jit(solution)/shard_map/all_to_all | solution.py:302
  182.5 8.6 %all-to-all-start.5 = ((bf16[32,72,128]{2,1,0:T(8,128)(2,1)}), bf16[32,72,128]{2,1,0:T(8,128)(2,1)S(1)}, u32[]{:S(2)}, u32[]{:S(2)}) async-start(bf16[32,72,128]{2,1,0:T(8,128)(2,1)} %copy-done.19), calls=%async_computation.5 | async-start | bytes 1179648 | tf_op jit(solution)/shard_map/all_to_all | solution.py:302
  192.5 5.5 %collective-permute-start.8 = (bf16[3,366,256]{2,1,0:T(8,128)(2,1)S(1)}, bf16[3,366,256]{2,1,0:T(8,128)(2,1)}, u32[]{:S(2)}, u32[]{:S(2)}) collective-permute-start(bf16[3,366,256]{2,1,0:T(8,128)(2,1)S(1)} %slice_select_fusion), channel_id=1, source_target_pairs={{0,8},{8,0},{16,24},{24,16},{32,40},{40,32},{48,56},{56,48},{64,72... | collective-permute-start | bytes 1686536 | tf_op jit(solution)/shard_map/ppermute | solution.py:320
  200.2 32.6 %collective-permute-done.8 = bf16[3,366,256]{2,1,0:T(8,128)(2,1)} collective-permute-done((bf16[3,366,256]{2,1,0:T(8,128)(2,1)S(1)}, bf16[3,366,256]{2,1,0:T(8,128)(2,1)}, u32[]{:S(2)}, u32[]{:S(2)}) %collective-permute-start.8) | collective-permute-done | bytes 562208 | tf_op jit(solution)/shard_map/ppermute | solution.py:320
  235.1 3.1 copy.67
  246.9 7.2 %all-to-all-start.6 = ((bf16[32,64,128]{2,1,0:T(8,128)(2,1)}), bf16[32,64,128]{2,1,0:T(8,128)(2,1)S(1)}, u32[]{:S(2)}, u32[]{:S(2)}) async-start(bf16[32,64,128]{2,1,0:T(8,128)(2,1)} %copy-done.20), calls=%async_computation.6 | async-start | bytes 1048576 | tf_op jit(solution)/shard_map/all_to_all | solution.py:302
  255.2 5.5 %collective-permute-start.10 = (bf16[1,366,256]{2,1,0:T(8,128)(2,1)S(1)}, bf16[1,366,256]{2,1,0:T(8,128)(2,1)S(1)}, u32[]{:S(2)}, u32[]{:S(2)}) collective-permute-start(bf16[1,366,256]{2,1,0:T(8,128)(2,1)S(1)} %slice_select_fusion.2), channel_id=1, source_target_pairs={{0,8},{8,0},{16,24},{24,16},{32,40},{40,32},{48,56},{56,48},{64,72... | collective-permute-start | bytes 562184 | tf_op jit(solution)/shard_map/ppermute | solution.py:321
  261.8 10.8 %collective-permute-done.10 = bf16[1,366,256]{2,1,0:T(8,128)(2,1)S(1)} collective-permute-done((bf16[1,366,256]{2,1,0:T(8,128)(2,1)S(1)}, bf16[1,366,256]{2,1,0:T(8,128)(2,1)S(1)}, u32[]{:S(2)}, u32[]{:S(2)}) %collective-permute-start.10) | collective-permute-done | bytes 187424 | tf_op jit(solution)/shard_map/ppermute | solution.py:321
  275.8 9.9 %psum.7 = f32[12,128]{1,0:T(8,128)S(1)} all-reduce(f32[12,128]{1,0:T(8,128)S(1)} %slice_add_fusion.1), channel_id=1, replica_groups=mesh['lat'=32,'lon'=4,'ens'=2] {'lon'}, use_global_device_ids=true, to_apply=%region_2.3 | all-reduce | flops 1536 | bytes 12288 | tf_op jit(solution)/shard_map/psum | solution.py:470
  285.8 113.2 %all-gather.1 = f32[32,20,128]{2,1,0:T(8,128)S(1)} all-gather(f32[1,20,128]{2,1,0:T(8,128)S(1)} %maximum_bitcast_fusion.8), channel_id=2, replica_groups=mesh['lat'=32,'lon'=4,'ens'=2] {'lat'}, dimensions={0}, use_global_device_ids=true | all-gather | bytes 337920 | tf_op jit(solution)/shard_map/all_gather | solution.py:486
  402.3 3.6 all-to-all-start.7
  408.9 5.6 %shard_map.121.back_ref = f32[4,384,256]{2,1,0:T(8,128)S(1)} custom-call(bf16[10,400,256]{2,1,0:T(8,128)(2,1)S(1)} %fusion.9.x_ref, bf16[384,480]{1,0:T(8,128)(2,1)S(1)} %copy-done.26, bf16[3,256,256]{2,1,0:T(8,128)(2,1)S(1)} %copy-done.23), custom_call_target="tpu_custom_call" | custom-call | flops 1132462080 | bytes 4382720 | tf_op jit(solution)/shard_map/pallas_call | solution.py:32
  (239 shorter events, 135.0 us)
Async XLA Ops:
  0.6 19.3 %copy-start = (bf16[384,256]{1,0:T(8,128)(2,1)S(1)}, bf16[384,256]{1,0:T(8,128)(2,1)}, u32[]{:S(2)}) copy-start(bf16[384,256]{1,0:T(8,128)(2,1)} %param.15) | copy-start | bytes 589828
  1.4 24.9 %collective-permute-start = (bf16[4,3,256]{2,1,0:T(4,128)(2,1)S(1)}, bf16[4,3,256]{2,1,0:T(4,128)(2,1)S(1)}, u32[]{:S(2)}, u32[]{:S(2)}) collective-permute-start(bf16[4,3,256]{2,1,0:T(4,128)(2,1)S(1)} %get-tuple-element.78), channel_id=1, source_target_pairs={{0,2},{2,4},{4,6},{6,0},{1,3},{3,5},{5,7},{7,1},{8,10},{10,12},{12... | collective-permute-start | bytes 18440 | tf_op jit(solution)/shard_map/ppermute | solution.py:310
  3.4 22.9 %collective-permute-start.1 = (bf16[4,3,256]{2,1,0:T(4,128)(2,1)S(1)}, bf16[4,3,256]{2,1,0:T(4,128)(2,1)S(1)}, u32[]{:S(2)}, u32[]{:S(2)}) collective-permute-start(bf16[4,3,256]{2,1,0:T(4,128)(2,1)S(1)} %get-tuple-element.79), channel_id=1, source_target_pairs={{2,0},{4,2},{6,4},{0,6},{3,1},{5,3},{7,5},{1,7},{10,8},{12,10},{14... | collective-permute-start | bytes 18440 | tf_op jit(solution)/shard_map/ppermute | solution.py:311
  8.5 22.6 %all-to-all-start = ((bf16[4,360,256]{2,1,0:T(8,128)(2,1)}), bf16[4,360,256]{2,1,0:T(8,128)(2,1)S(1)}, u32[]{:S(2)}, u32[]{:S(2)}) async-start(bf16[4,360,256]{2,1,0:T(8,128)(2,1)} %shard_map.111), calls=%async_computation | async-start | bytes 1474560 | tf_op jit(solution)/shard_map/all_to_all | solution.py:302
  33.1 31.5 %all-to-all-start.1 = ((bf16[32,48,128]{2,1,0:T(8,128)(2,1)}), bf16[32,48,128]{2,1,0:T(8,128)(2,1)}, u32[]{:S(2)}, u32[]{:S(2)}) async-start(bf16[32,48,128]{2,1,0:T(8,128)(2,1)} %shard_map.112), calls=%async_computation.1 | async-start | bytes 786432 | tf_op jit(solution)/shard_map/all_to_all | solution.py:302
  59.3 36.2 %collective-permute-start.2 = (bf16[3,366,256]{2,1,0:T(8,128)(2,1)}, bf16[3,366,256]{2,1,0:T(8,128)(2,1)}, u32[]{:S(2)}, u32[]{:S(2)}) collective-permute-start(bf16[3,366,256]{2,1,0:T(8,128)(2,1)} %slice_select_fusion.1), channel_id=1, source_target_pairs={{0,8},{8,0},{16,24},{24,16},{32,40},{40,32},{48,56},{56,48},{64,72... | collective-permute-start | bytes 1686536 | tf_op jit(solution)/shard_map/ppermute | solution.py:320
  71.4 35.1 %all-to-all-start.2 = ((bf16[32,48,128]{2,1,0:T(8,128)(2,1)}), bf16[32,48,128]{2,1,0:T(8,128)(2,1)}, u32[]{:S(2)}, u32[]{:S(2)}) async-start(bf16[32,48,128]{2,1,0:T(8,128)(2,1)} %copy-done.31), calls=%async_computation.2 | async-start | bytes 786432 | tf_op jit(solution)/shard_map/all_to_all | solution.py:302
  95.5 36.8 %collective-permute-start.3 = (bf16[3,366,256]{2,1,0:T(8,128)(2,1)}, bf16[3,366,256]{2,1,0:T(8,128)(2,1)}, u32[]{:S(2)}, u32[]{:S(2)}) collective-permute-start(bf16[3,366,256]{2,1,0:T(8,128)(2,1)} %collective-permute-done.2), channel_id=1, source_target_pairs={{0,16},{8,248},{16,32},{24,8},{32,48},{40,24},{48,64},{56,40},{64,... | collective-permute-start | bytes 1686536 | tf_op jit(solution)/shard_map/ppermute | solution.py:322
  110.8 32.1 %all-to-all-start.3 = ((bf16[4,360,256]{2,1,0:T(8,128)(2,1)}), bf16[4,360,256]{2,1,0:T(8,128)(2,1)}, u32[]{:S(2)}, u32[]{:S(2)}) async-start(bf16[4,360,256]{2,1,0:T(8,128)(2,1)} %copy-done.12), calls=%async_computation.3 | async-start | bytes 1474560 | tf_op jit(solution)/shard_map/all_to_all | solution.py:302
  116.0 16.2 %collective-permute-start.4 = (bf16[1,366,256]{2,1,0:T(8,128)(2,1)S(1)}, bf16[1,366,256]{2,1,0:T(8,128)(2,1)S(1)}, u32[]{:S(2)}, u32[]{:S(2)}) collective-permute-start(bf16[1,366,256]{2,1,0:T(8,128)(2,1)S(1)} %slice_select_fusion.3), channel_id=1, source_target_pairs={{0,8},{8,0},{16,24},{24,16},{32,40},{40,32},{48,56},{56,48},{64,72... | collective-permute-start | bytes 562184 | tf_op jit(solution)/shard_map/ppermute | solution.py:321
  153.0 25.4 %all-to-all-start.4 = ((bf16[4,360,256]{2,1,0:T(8,128)(2,1)}), bf16[4,360,256]{2,1,0:T(8,128)(2,1)}, u32[]{:S(2)}, u32[]{:S(2)}) async-start(bf16[4,360,256]{2,1,0:T(8,128)(2,1)} %copy-done.29), calls=%async_computation.4 | async-start | bytes 1474560 | tf_op jit(solution)/shard_map/all_to_all | solution.py:302
  159.2 10.4 %collective-permute-start.5 = (bf16[4,3,256]{2,1,0:T(4,128)(2,1)}, bf16[4,3,256]{2,1,0:T(4,128)(2,1)S(1)}, u32[]{:S(2)}, u32[]{:S(2)}) collective-permute-start(bf16[4,3,256]{2,1,0:T(4,128)(2,1)} %get-tuple-element.76), channel_id=1, source_target_pairs={{0,2},{2,4},{4,6},{6,0},{1,3},{3,5},{5,7},{7,1},{8,10},{10,12},{12... | collective-permute-start | bytes 18440 | tf_op jit(solution)/shard_map/ppermute | solution.py:310
  161.3 8.4 %collective-permute-start.6 = (bf16[4,3,256]{2,1,0:T(4,128)(2,1)}, bf16[4,3,256]{2,1,0:T(4,128)(2,1)}, u32[]{:S(2)}, u32[]{:S(2)}) collective-permute-start(bf16[4,3,256]{2,1,0:T(4,128)(2,1)} %get-tuple-element.77), channel_id=1, source_target_pairs={{2,0},{4,2},{6,4},{0,6},{3,1},{5,3},{7,5},{1,7},{10,8},{12,10},{14... | collective-permute-start | bytes 18440 | tf_op jit(solution)/shard_map/ppermute | solution.py:311
  168.2 3.7 collective-permute-start.7
  182.5 58.7 %all-to-all-start.5 = ((bf16[32,72,128]{2,1,0:T(8,128)(2,1)}), bf16[32,72,128]{2,1,0:T(8,128)(2,1)S(1)}, u32[]{:S(2)}, u32[]{:S(2)}) async-start(bf16[32,72,128]{2,1,0:T(8,128)(2,1)} %copy-done.19), calls=%async_computation.5 | async-start | bytes 1179648 | tf_op jit(solution)/shard_map/all_to_all | solution.py:302
  191.1 43.2 %copy-start.36 = (bf16[3,256,256]{1,2,0:T(8,128)(2,1)S(1)}, bf16[3,256,256]{1,2,0:T(8,128)(2,1)}, u32[]{:S(2)}) copy-start(bf16[3,256,256]{1,2,0:T(8,128)(2,1)} %mul.273) | copy-start | bytes 1179652
  191.1 43.2 %copy-start.47 = (bf16[32,8,2,128]{3,1,2,0:T(8,128)(2,1)S(1)}, bf16[32,8,2,128]{3,1,2,0:T(8,128)(2,1)}, u32[]{:S(2)}) copy-start(bf16[32,8,2,128]{3,1,2,0:T(8,128)(2,1)} %copy.78) | copy-start | bytes 393220
  192.5 40.3 %collective-permute-start.8 = (bf16[3,366,256]{2,1,0:T(8,128)(2,1)S(1)}, bf16[3,366,256]{2,1,0:T(8,128)(2,1)}, u32[]{:S(2)}, u32[]{:S(2)}) collective-permute-start(bf16[3,366,256]{2,1,0:T(8,128)(2,1)S(1)} %slice_select_fusion), channel_id=1, source_target_pairs={{0,8},{8,0},{16,24},{24,16},{32,40},{40,32},{48,56},{56,48},{64,72... | collective-permute-start | bytes 1686536 | tf_op jit(solution)/shard_map/ppermute | solution.py:320
  232.8 39.8 %collective-permute-start.9 = (bf16[3,366,256]{2,1,0:T(8,128)(2,1)}, bf16[3,366,256]{2,1,0:T(8,128)(2,1)}, u32[]{:S(2)}, u32[]{:S(2)}) collective-permute-start(bf16[3,366,256]{2,1,0:T(8,128)(2,1)} %collective-permute-done.8), channel_id=1, source_target_pairs={{0,16},{8,248},{16,32},{24,8},{32,48},{40,24},{48,64},{56,40},{64,... | collective-permute-start | bytes 1686536 | tf_op jit(solution)/shard_map/ppermute | solution.py:322
  246.9 38.8 %all-to-all-start.6 = ((bf16[32,64,128]{2,1,0:T(8,128)(2,1)}), bf16[32,64,128]{2,1,0:T(8,128)(2,1)S(1)}, u32[]{:S(2)}, u32[]{:S(2)}) async-start(bf16[32,64,128]{2,1,0:T(8,128)(2,1)} %copy-done.20), calls=%async_computation.6 | async-start | bytes 1048576 | tf_op jit(solution)/shard_map/all_to_all | solution.py:302
  255.2 17.5 %collective-permute-start.10 = (bf16[1,366,256]{2,1,0:T(8,128)(2,1)S(1)}, bf16[1,366,256]{2,1,0:T(8,128)(2,1)S(1)}, u32[]{:S(2)}, u32[]{:S(2)}) collective-permute-start(bf16[1,366,256]{2,1,0:T(8,128)(2,1)S(1)} %slice_select_fusion.2), channel_id=1, source_target_pairs={{0,8},{8,0},{16,24},{24,16},{32,40},{40,32},{48,56},{56,48},{64,72... | collective-permute-start | bytes 562184 | tf_op jit(solution)/shard_map/ppermute | solution.py:321
  272.6 127.9 %copy-start.3 = (bf16[4,360,768]{2,1,0:T(8,128)(2,1)S(1)}, bf16[4,360,768]{2,1,0:T(8,128)(2,1)}, u32[]{:S(2)}) copy-start(bf16[4,360,768]{2,1,0:T(8,128)(2,1)} %pad_maximum_fusion.1.wave_ref) | copy-start | bytes 6635524
  402.3 16.2 %all-to-all-start.7 = ((bf16[4,360,256]{2,1,0:T(8,128)(2,1)}), bf16[4,360,256]{2,1,0:T(8,128)(2,1)S(1)}, u32[]{:S(2)}, u32[]{:S(2)}) async-start(bf16[4,360,256]{2,1,0:T(8,128)(2,1)} %shard_map.120), calls=%async_computation.7 | async-start | bytes 1474560 | tf_op jit(solution)/shard_map/all_to_all | solution.py:302
  407.8 6.8 %collective-permute-start.11 = (f32[576,128]{1,0:T(8,128)S(1)}, f32[576,128]{1,0:T(8,128)S(1)}, u32[]{:S(2)}, u32[]{:S(2)}) collective-permute-start(f32[576,128]{1,0:T(8,128)S(1)} %pad_maximum_fusion.4), channel_id=1, source_target_pairs={{0,1},{1,0},{2,3},{3,2},{4,5},{5,4},{6,7},{7,6},{8,9},{9,8},{10,11... | collective-permute-start | bytes 884744 | tf_op jit(solution)/shard_map/ppermute | solution.py:490
  (56 other events, 230.7 us)

commit v2 on v1

v2 whole, which is shorter than its diff:
```python
import functools
import math

import jax
import jax.numpy as jnp
from jax import lax
from jax.experimental import pallas as pl
from jax.experimental.pallas import tpu as pltpu
from jax.sharding import PartitionSpec as P

LONGITUDES = 1440
BAND_REACH = 3
SUPPORT = 4
HALF = 64
LANES = 128
BLOCK = 32
WINDOW = 48
CHUNK = 48
TILE = 96
WINDOWS = 3
EDGE = 16
PARTS = 3

bf16 = jnp.bfloat16
f32 = jnp.float32
highest = lax.Precision.HIGHEST
far_below = -1000000


VMEM = pltpu.VMEM
SMEM = pltpu.SMEM


def call(kernel, out_shape, args, flops, scratch=(), places=None, grid=(), blocks=None, outs=None, limit=24):
    moved = sum(a.size * a.dtype.itemsize for a in args)
    moved += sum(math.prod(o.shape) * jnp.dtype(o.dtype).itemsize for o in out_shape)
    places = places or {}
    specs = blocks or [pl.BlockSpec(memory_space=places.get(i, VMEM)) for i in range(len(args))]
    out_specs = outs or [
        pl.BlockSpec(memory_space=places[-1 - i]) if -1 - i in places else pl.BlockSpec()
        for i in range(len(out_shape))
    ]
    return pl.pallas_call(
        kernel,
        grid=grid,
        out_shape=out_shape,
        in_specs=specs,
        out_specs=out_specs,
        scratch_shapes=list(scratch),
        compiler_params=pltpu.CompilerParams(vmem_limit_bytes=limit * 1024 * 1024),
        cost_estimate=pl.CostEstimate(
            flops=int(flops), bytes_accessed=int(moved), transcendentals=0
        ),
    )(*args)


def hbm(x):
    return pltpu.with_memory_space_constraint(x, pltpu.HBM)


def dot(a, b):
    return lax.dot_general(a, b, (((1,), (0,)), ((), ())), preferred_element_type=f32)


def swap_pair(first, second):
    left = lax.broadcasted_iota(jnp.int32, first.shape, 1) < HALF
    low = jnp.where(left, first, pltpu.roll(second, HALF, 1))
    high = jnp.where(left, pltpu.roll(first, HALF, 1), second)
    return low, high


def quads():
    for a in range(2):
        for v in range(2):
            yield a, v, pl.ds(a * LANES, LANES), pl.ds(v * LANES, LANES)


def edge_rows(columns):
    rows = []
    for column in columns:
        rows += [column, jnp.zeros((1, column.shape[1]), f32)]
    return jnp.concatenate(rows, axis=0)


def pack_kernel(place_ref, x_ref, out_ref):
    sector = x_ref.shape[1]
    for first in range(0, sector, CHUNK):
        rows = pl.ds(first, min(CHUNK, sector - first))
        for a, v, at, av in quads():
            low, high = swap_pair(
                x_ref[2 * a, rows, av].astype(f32), x_ref[2 * a + 1, rows, av].astype(f32)
            )
            out_ref[2 * v, rows, at] = low.astype(bf16)
            out_ref[2 * v + 1, rows, at] = high.astype(bf16)
    lat_rows = x_ref.shape[0]
    begin = edge_rows([x_ref[t, 0:16, :].astype(f32)[:BAND_REACH] for t in range(lat_rows)])
    end = edge_rows([x_ref[t, sector - 8 : sector, :].astype(f32)[8 - BAND_REACH :] for t in range(lat_rows)])
    peers = out_ref.shape[0]
    for p in range(peers):
        to_right = p == lax.rem(place_ref[0] + 1, peers)
        out_ref[p, sector : sector + EDGE, :] = jnp.where(to_right, end, begin).astype(bf16)


def analysis_kernel(circle_ref, wave_ref, *rest):
    out_ref, rows_ref = rest[2:4] if len(rest) > 2 else rest
    copies = []
    if len(rest) > 2:
        terms_ref, sems = rest[4:]
        for j in range(2):
            copies.append(pltpu.make_async_copy(rest[j], terms_ref.at[j], sems.at[j]))
            copies[j].start()
    waves, sector = wave_ref.shape[1] // 2, wave_ref.shape[2]
    sums = []
    for r in range(2):
        total = None
        for s in range(wave_ref.shape[0]):
            term = dot(wave_ref[s, r * waves : (r + 1) * waves, :], circle_ref[s, 0:sector, :])
            total = term if total is None else total + term
        sums.append(total)
    for a in range(2):
        lanes = slice(a * LANES, (a + 1) * LANES)
        low, high = swap_pair(sums[0][:, lanes], sums[1][:, lanes])
        rows_ref[pl.ds(2 * a, waves, stride=4), :] = low
        rows_ref[pl.ds(2 * a + 1, waves, stride=4), :] = high
    peers = out_ref.shape[0]
    main = 4 * waves // peers
    out_ref[:, 0:main, :] = rows_ref[...].reshape(peers, main, LANES).astype(bf16)
    if copies:
        for copy in copies:
            copy.wait()
        out_ref[:, main:, :] = split_chunks(terms_ref[0] + terms_ref[1], peers)


def chunk_size(rows, peers):
    return 8 * -(-rows // (8 * peers))


def split_chunks(total, peers):
    high = total.astype(bf16).astype(f32)
    low = total - high
    size = chunk_size(total.shape[0], peers)
    used = total.shape[0] // size
    both = jnp.concatenate(
        [high.reshape(used, size, LANES), low.reshape(used, size, LANES)], axis=1
    )
    if used < peers:
        both = jnp.concatenate([both, jnp.zeros((peers - used, 2 * size, LANES), f32)], axis=0)
    return both.astype(bf16)


def joined(got):
    total = jnp.sum(got.astype(f32), axis=0)
    size = total.shape[0] // 2
    return total[:size] + total[size:]


def legendre_steps(order_ref, rows_in_ref, leg_ref, leg_turned_ref, gain_ref, rows_out_ref, peers, part, use):
    owned, degrees = leg_ref.shape[0], leg_ref.shape[1]
    step = 4 * owned
    degree = lax.broadcasted_iota(jnp.int32, (degrees, LANES), 0)
    for k in part:
        field = jnp.concatenate(
            [rows_in_ref[pl.ds(4 * k + t, peers, stride=step), :] for t in range(4)], axis=0
        ).astype(bf16)
        coeffs = dot(leg_ref[k], field)
        coeffs = jnp.where(degree >= order_ref[k], coeffs, 0.0)
        use(k, coeffs)
        weighted = (coeffs * gain_ref[...]).astype(bf16)
        synthesis = dot(leg_turned_ref[k], weighted)
        for t in range(4):
            rows_out_ref[pl.ds(4 * k + t, peers, stride=step), :] = synthesis[
                t * peers : (t + 1) * peers
            ]


def parts(owned):
    count = owned // PARTS
    return [(p, pl.ds(p * count, count), range(p * count, (p + 1) * count)) for p in range(PARTS)]


def legendre_forward_kernel(
    order_ref,
    got_ref,
    leg_hbm,
    leg_turned_hbm,
    gain_ref,
    out_ref,
    coeffs_hbm,
    rows_in_ref,
    rows_out_ref,
    held_ref,
    leg_ref,
    leg_turned_ref,
    sems,
):
    peers = got_ref.shape[0]
    main = rows_in_ref.shape[0] // peers
    reads, writes = [], []
    for p, at, _ in parts(leg_ref.shape[0]):
        reads.append(
            [
                pltpu.make_async_copy(leg_hbm.at[at], leg_ref.at[at], sems.at[0, p]),
                pltpu.make_async_copy(leg_turned_hbm.at[at], leg_turned_ref.at[at], sems.at[1, p]),
            ]
        )
        for copy in reads[p]:
            copy.start()
    rows_in_ref[...] = got_ref[...].astype(f32).reshape(peers * main, LANES)

    def use(k, coeffs):
        held_ref[k] = coeffs

    for p, at, part in parts(leg_ref.shape[0]):
        for copy in reads[p]:
            copy.wait()
        legendre_steps(
            order_ref, rows_in_ref, leg_ref, leg_turned_ref, gain_ref, rows_out_ref, peers, part, use
        )
        writes.append(pltpu.make_async_copy(held_ref.at[at], coeffs_hbm.at[at], sems.at[2, p]))
        writes[p].start()
    out_ref[...] = rows_out_ref[...].reshape(peers, main, LANES).astype(bf16)
    for copy in writes:
        copy.wait()


def legendre_backward_kernel(
    order_ref,
    got_ref,
    leg_hbm,
    leg_turned_hbm,
    gain_ref,
    coeffs_hbm,
    out_ref,
    mix_ref,
    rows_in_ref,
    rows_out_ref,
    sum_ref,
    held_ref,
    leg_ref,
    leg_turned_ref,
    sems,
):
    peers = got_ref.shape[0]
    main = rows_in_ref.shape[0] // peers
    reads = []
    for p, at, _ in parts(leg_ref.shape[0]):
        reads.append(
            [
                pltpu.make_async_copy(leg_hbm.at[at], leg_ref.at[at], sems.at[0, p]),
                pltpu.make_async_copy(leg_turned_hbm.at[at], leg_turned_ref.at[at], sems.at[1, p]),
                pltpu.make_async_copy(coeffs_hbm.at[at], held_ref.at[at], sems.at[2, p]),
            ]
        )
        for copy in reads[p]:
            copy.start()
    rows_in_ref[...] = got_ref[:, 0:main, :].astype(f32).reshape(peers * main, LANES)
    mix_ref[...] = joined(got_ref[:, main:, :])

    def use(k, coeffs):
        term = coeffs * held_ref[k]
        if k == 0:
            sum_ref[...] = term
        else:
            sum_ref[...] += term

    for p, _, part in parts(leg_ref.shape[0]):
        for copy in reads[p]:
            copy.wait()
        legendre_steps(
            order_ref, rows_in_ref, leg_ref, leg_turned_ref, gain_ref, rows_out_ref, peers, part, use
        )
    out_ref[:, 0:main, :] = rows_out_ref[...].reshape(peers, main, LANES).astype(bf16)
    total = sum_ref[...]
    total = total + pltpu.roll(total, HALF, 1)
    half = total.shape[0] // 2
    left = lax.broadcasted_iota(jnp.int32, (half, LANES), 1) < HALF
    out_ref[:, main:, :] = split_chunks(jnp.where(left, total[:half], total[half:]), peers)


def spectrum_of(got_ref, rows_ref, waves):
    peers = got_ref.shape[0]
    main = 4 * waves // peers
    rows_ref[...] = got_ref[:, 0:main, :].astype(f32).reshape(4 * waves, LANES)
    low, high = [], []
    for a in range(2):
        lo, hi = swap_pair(
            rows_ref[pl.ds(2 * a, waves, stride=4), :], rows_ref[pl.ds(2 * a + 1, waves, stride=4), :]
        )
        low.append(lo)
        high.append(hi)
    return jnp.concatenate(
        [jnp.concatenate(low, axis=1), jnp.concatenate(high, axis=1)], axis=0
    ).astype(bf16)


def synthesis_kernel(got_ref, wave_hbm, out_ref, rows_ref, wave_ref, sems):
    peers = out_ref.shape[0]
    reads = []
    for j in range(peers):
        reads.append(pltpu.make_async_copy(wave_hbm.at[j], wave_ref.at[j], sems.at[j]))
        reads[j].start()
    spectrum = spectrum_of(got_ref, rows_ref, wave_ref.shape[2] // 2)
    for j in range(peers):
        reads[j].wait()
        out_ref[j] = dot(wave_ref[j], spectrum).astype(bf16)


def band_kernel(
    turned, parity_ref, own_hbm, far_hbm, rest_hbm, other_hbm, toeplitz_ref, mix_ref, *rest
):
    wide_ref, x_ref, sems = rest[-3:]
    mixed_ref = rest[0]
    basis_ref = rest[1] if len(rest) > 4 else None
    kernels, group_count, width = mix_ref.shape[0], mix_ref.shape[1], mix_ref.shape[2]
    span, channels = x_ref.shape[0], x_ref.shape[2]
    per_kernel = toeplitz_ref.shape[0] // kernels
    rows = per_kernel // BLOCK
    j = pl.program_id(0)

    reach, own, wide = BAND_REACH, own_hbm.shape[0], own_hbm.shape[1]

    def fetch(moves):
        copies = []
        for source, first, count in moves:
            target = x_ref.at[pl.ds(first, count), pl.ds(0, wide), :]
            copies.append(pltpu.make_async_copy(source, target, sems.at[len(copies)]))
            copies[-1].start()
        for copy in copies:
            copy.wait()

    @pl.when((j == 0) & (parity_ref[0] == 0))
    def _():
        fetch(
            [
                (own_hbm, reach, own),
                (other_hbm, 0, reach),
                (rest_hbm, reach + own, 1),
                (far_hbm.at[pl.ds(0, reach - 1)], reach + own + 1, reach - 1),
            ]
        )

    @pl.when((j == 0) & (parity_ref[0] == 1))
    def _():
        fetch(
            [
                (own_hbm, reach, own),
                (far_hbm.at[pl.ds(1, reach - 1)], 0, reach - 1),
                (rest_hbm, reach - 1, 1),
                (other_hbm, reach + own, reach),
            ]
        )

    @pl.when(j == 0)
    def _():
        x_ref[:, wide:, :] = jnp.zeros((span, x_ref.shape[1] - wide, channels), bf16)
        wide_ref[...] = jnp.zeros_like(wide_ref)
        for b in range(kernels):
            for g in range(group_count):
                part = mix_ref[b, g]
                if turned:
                    part = part.astype(f32).T.astype(bf16)
                at = slice(g * width, (g + 1) * width)
                wide_ref[b, at, at] = part

    for w in range(WINDOWS):
        start = pl.multiple_of((j * WINDOWS + w) * BLOCK, BLOCK)
        at = pl.ds(w * BLOCK, BLOCK)
        window = x_ref[:, pl.ds(start, WINDOW), :].reshape(span * WINDOW, channels)
        basis = dot(toeplitz_ref[...], window).astype(bf16)
        total = None
        for b in range(kernels):
            part = basis[b * per_kernel : (b + 1) * per_kernel]
            if basis_ref is not None:
                basis_ref[b, :, at, :] = part.reshape(rows, BLOCK, channels)
            term = dot(part, wide_ref[b])
            total = term if total is None else total + term
        mixed_ref[:, at, :] = total.reshape(rows, BLOCK, channels)


def activation_kernel(
    valid, place_ref, spec_ref, mixed_ref, state_ref, cot_ref, next_ref, grad_ref, packed_ref, begin_ref
):
    scale = math.sqrt(2.0 / math.pi)
    step, steps = pl.program_id(0), pl.num_programs(0)
    lat_rows = state_ref.shape[0]
    peers = packed_ref.shape[0]
    for first in range(0, state_ref.shape[1], CHUNK):
        rows = pl.ds(first, CHUNK)
        for a, v, at, av in quads():
            spectra = swap_pair(
                spec_ref[2 * v, rows, at].astype(f32),
                spec_ref[2 * v + 1, rows, at].astype(f32),
            )
            grads = []
            for h in range(2):
                t = 2 * a + h
                value = spectra[h] + mixed_ref[t, rows, av]
                square = value * value
                turn = jnp.tanh(scale * value * (1.0 + 0.044715 * square))
                share = 0.5 + 0.5 * turn
                next_ref[t, rows, av] = (state_ref[t, rows, av].astype(f32) + value * share).astype(bf16)
                slope = share + (0.5 * scale) * value * (1.0 - turn * turn) * (
                    1.0 + (3.0 * 0.044715) * square
                )
                grad = cot_ref[t, rows, av].astype(f32) * slope
                grad_ref[t, rows, av] = grad.astype(bf16)
                grads.append(grad)
            low, high = swap_pair(*grads)
            packed_ref[2 * v, rows, at] = low.astype(bf16)
            packed_ref[2 * v + 1, rows, at] = high.astype(bf16)

    def edge(first, skip):
        rows = pl.ds(first, 16)
        return edge_rows(
            [grad_ref[t, rows, :].astype(f32)[skip : skip + BAND_REACH] for t in range(lat_rows)]
        )

    @pl.when(step == 0)
    def _():
        begin_ref[...] = edge(0, 0)

    @pl.when(step == steps - 1)
    def _():
        end = edge((valid - 1) // 16 * 16, (valid - 1) % 16 + 1 - BAND_REACH)
        for p in range(peers):
            to_right = p == lax.rem(place_ref[0] + 1, peers)
            packed_ref[p, valid : valid + EDGE, :] = jnp.where(to_right, end, begin_ref[...]).astype(bf16)


def finish_kernel(spec_ref, back_ref, cot_ref, out_ref):
    for first in range(0, cot_ref.shape[1], CHUNK):
        rows = pl.ds(first, CHUNK)
        for a, v, at, av in quads():
            spectra = swap_pair(
                spec_ref[2 * v, rows, at].astype(f32),
                spec_ref[2 * v + 1, rows, at].astype(f32),
            )
            for h in range(2):
                t = 2 * a + h
                out_ref[t, rows, av] = (
                    cot_ref[t, rows, av].astype(f32) + spectra[h] + back_ref[t, rows, av]
                ).astype(bf16)


def mixing_gradient_kernel(basis_ref, grad_ref, out_ref):
    kernels, lat_rows = basis_ref.shape[0], basis_ref.shape[1]
    sector = grad_ref.shape[1]
    for g in range(2):
        lanes = pl.ds(g * LANES, LANES)
        totals = [None] * kernels
        for i in range(lat_rows):
            turned = grad_ref[i, :, lanes].astype(f32).T.astype(bf16)
            for b in range(kernels):
                term = dot(turned, basis_ref[b, i, 0:sector, lanes])
                totals[b] = term if totals[b] is None else totals[b] + term
        for b in range(kernels):
            out_ref[g, b] = totals[b].T


def share_kernel(got_ref, mix_ref, out_ref):
    peers = got_ref.shape[0]
    gain_size = out_ref.shape[1] - mix_ref.shape[0]
    main = got_ref.shape[1] - 2 * gain_size
    total = jnp.concatenate([joined(got_ref[:, main:, :]), mix_ref[...]], axis=0)
    out_ref[...] = jnp.broadcast_to(total[None], out_ref.shape)


def collect_kernel(gain_rows, got_ref, gain_ref, mix_ref):
    peers, mix_rows = got_ref.shape[0], mix_ref.shape[0]
    size, mix_size = chunk_size(gain_rows, peers), chunk_size(mix_rows, peers)
    gain_ref[...] = got_ref[0 : gain_rows // size, 0:size, :].reshape(gain_rows, LANES)
    mix_ref[...] = got_ref[0 : mix_rows // mix_size, size:, :].reshape(mix_rows, LANES)


def totals_kernel(
    mix_scale, gain_scale, place_ref, gain_mine_ref, gain_other_ref, mine_ref, other_ref, mix_ref, gain_ref
):
    half = gain_ref.shape[0] // 2
    gain = (gain_mine_ref[...] + gain_other_ref[...]) * gain_scale
    gain_ref[0:half, :] = gain[:, 0:HALF]
    gain_ref[half:, :] = pltpu.roll(gain, HALF, 1)[:, 0:HALF]
    kernels, group_count, width = mix_ref.shape[0], mix_ref.shape[1], mix_ref.shape[2]
    for b in range(kernels):
        rows = slice(b * width, (b + 1) * width)
        mine, other = mine_ref[rows, :], other_ref[rows, :]
        for g in range(group_count):
            mix_ref[b, g] = jnp.where(place_ref[0] == g, mine, other) * mix_scale


def wave_kernel(column_ref, row_ref, cos_ref, sin_ref, by_wave_ref, by_point_ref):
    sectors, waves, sector = by_wave_ref.shape[0], cos_ref.shape[0], by_wave_ref.shape[2]
    c, s = cos_ref[...], sin_ref[...]
    for turned in range(2):
        orders = row_ref[...] if turned else column_ref[...]
        if turned:
            c, s = c.T, s.T
        for part in range(sectors):
            turns = jnp.broadcast_to((orders * part) & 3, c.shape)
            swap = (turns & 1) == 1
            flip_c = jnp.where((turns == 1) | (turns == 2), -1.0, 1.0)
            flip_s = jnp.where(turns <= 1, -1.0, 1.0)
            cos_part = (jnp.where(swap, s, c) * flip_c).astype(bf16)
            sin_part = (jnp.where(swap, c, s) * flip_s).astype(bf16)
            if turned:
                by_point_ref[part, :, 0:waves] = cos_part[0:sector]
                by_point_ref[part, :, waves : 2 * waves] = sin_part[0:sector]
            else:
                by_wave_ref[part, 0:waves, :] = cos_part[:, 0:sector]
                by_wave_ref[part, waves : 2 * waves, :] = sin_part[:, 0:sector]


def wave_tables(owner_order, sector, sectors):
    waves = owner_order.shape[0]
    n = jnp.arange(-(-sector // LANES) * LANES, dtype=jnp.int32)
    phases = owner_order[:, None] * n[None, :] % LONGITUDES
    angles = phases.astype(f32) * (2.0 * math.pi / LONGITUDES)
    factor = 1.0 / math.sqrt(LONGITUDES)
    c, s = jnp.cos(angles) * factor, jnp.sin(angles) * factor
    outs = [
        jax.ShapeDtypeStruct((sectors, 2 * waves, sector), bf16),
        jax.ShapeDtypeStruct((sectors, sector, 2 * waves), bf16),
    ]
    return call(wave_kernel, outs, (owner_order[:, None], owner_order[None, :], c, s), 30 * c.size)


def legendre_kernel(leg_ref, out_ref, turned_ref):
    owned, total = leg_ref.shape[0], leg_ref.shape[2]
    peers = total // 4
    t = lax.broadcasted_iota(jnp.int32, (total, total), 0)
    u = lax.broadcasted_iota(jnp.int32, (total, total), 1)
    order = (u == (t & 3) * peers + (t >> 2)).astype(f32).astype(bf16)
    order_turned = (t == (u & 3) * peers + (u >> 2)).astype(f32).astype(bf16)
    for k in range(owned):
        out_ref[k] = dot(leg_ref[k], order).astype(bf16)
        turned_ref[k] = lax.dot_general(
            order_turned, leg_ref[k], (((1,), (1,)), ((), ())), preferred_element_type=f32
        ).astype(bf16)


def toeplitz_kernel(table_ref, out_ref):
    outputs, entries = table_ref.shape[1], table_ref.shape[2]
    taps = 2 * BAND_REACH + 1
    shape = out_ref.shape[1:]
    entry = lax.broadcasted_iota(jnp.int32, (entries, shape[1]), 0)
    lane = lax.broadcasted_iota(jnp.int32, (1, shape[1]), 1)
    row_in = jnp.zeros_like(lane)
    for r in range(1, shape[1] // WINDOW):
        row_in += (lane >= r * WINDOW).astype(jnp.int32)
    n = lax.broadcasted_iota(jnp.int32, shape, 0) & (BLOCK - 1)
    tap = (lane - row_in * WINDOW) - n
    for which in range(2):
        tall = jnp.concatenate(
            [jnp.broadcast_to(table_ref[which, q : q + 1, :], (BLOCK, entries)) for q in range(outputs)],
            axis=0,
        ).astype(bf16)
        total = jnp.zeros(shape, f32)
        for d in range(taps):
            pick = (entry == taps * row_in + d).astype(f32).astype(bf16)
            total = jnp.where(tap == d, dot(tall, pick), total)
        out_ref[which] = total.astype(bf16)


def band_table(kernels_pad, offsets_pad, first_in, count_in, first_out, output_count):
    rows_kern = lax.dynamic_slice_in_dim(kernels_pad, first_in + BAND_REACH, count_in, 1)
    rows_start = lax.dynamic_slice_in_dim(offsets_pad, first_in + BAND_REACH, count_in, 0)
    targets = first_out + jnp.arange(output_count, dtype=jnp.int32)
    support_index = jnp.arange(SUPPORT, dtype=jnp.int32)
    matches = (
        rows_start[:, None, None] + support_index[None, :, None] == targets[None, None, :]
    ).astype(f32)
    return jnp.einsum("bikd,ikr->ibrd", rows_kern.astype(f32), matches, precision=highest)


def band_matrices(kernels, offsets, lat_first, lat_rows, lat_total):
    extent = lat_rows + 2 * BAND_REACH
    kernels_pad = jnp.pad(kernels, ((0, 0), (BAND_REACH, BAND_REACH), (0, 0), (0, 0)))
    offsets_pad = jnp.pad(offsets, BAND_REACH, constant_values=far_below)
    forward = band_table(
        kernels_pad, offsets_pad, lat_first, lat_rows, lat_first - BAND_REACH, extent
    )
    rows_global = lat_first - BAND_REACH + jnp.arange(extent, dtype=jnp.int32)
    inside = (rows_global >= 0) & (rows_global < lat_total)
    forward = jnp.where(inside[None, None, :, None], forward, 0.0)
    backward = band_table(
        kernels_pad, offsets_pad, lat_first - BAND_REACH, extent, lat_first, lat_rows
    )
    outputs, entries = kernels.shape[0] * lat_rows, extent * (2 * BAND_REACH + 1)
    tables = jnp.stack(
        [
            jnp.transpose(forward, (1, 0, 2, 3)).reshape(outputs, entries),
            jnp.transpose(backward[..., ::-1], (1, 2, 0, 3)).reshape(outputs, entries),
        ]
    )
    shape = jax.ShapeDtypeStruct((2, outputs * BLOCK, extent * WINDOW), bf16)
    return call(toeplitz_kernel, [shape], (tables,), 28 * math.prod(shape.shape))[0]


def exchange(x, axis):
    return lax.all_to_all(x, axis, split_axis=0, concat_axis=0, tiled=True)


def with_columns(x, circle):
    peers = lax.axis_size("lon")
    me = lax.axis_index("lon")
    lat_rows, sector, channels = x.shape
    edges = circle[:, sector:].reshape(peers, lat_rows, EDGE // lat_rows, channels)[:, :, :BAND_REACH]
    before = lax.dynamic_index_in_dim(edges, lax.rem(me + peers - 1, peers), 0, False)
    after = lax.dynamic_index_in_dim(edges, lax.rem(me + 1, peers), 0, False)
    spare = jnp.zeros((lat_rows, -(sector + 2 * BAND_REACH) % 16, channels), bf16)
    return jnp.concatenate([before, x, after, spare], axis=1)


def pairs():
    return [(i, i ^ 1) for i in range(lax.axis_size("lat"))]


def swapped_rows(x, even):
    return lax.ppermute(jnp.where(even, x[:BAND_REACH], x[1 : BAND_REACH + 1]), "lat", pairs())


def relayed_rows(far):
    peers = lax.axis_size("lat")
    relay = [(i, (i + 2) % peers if i % 2 == 0 else (i - 2) % peers) for i in range(peers)]
    return lax.ppermute(far, "lat", relay)


def rest_rows(x, even):
    return lax.ppermute(jnp.where(even, x[BAND_REACH:], x[:1]), "lat", pairs())


def on_device(states, cotangent, kernels, offsets, mixing, legendre, owner_order, spectral_gain):
    fields = states[0]
    cot = cotangent[0]
    lat_rows, sector, channels = fields.shape
    lon_index = lax.axis_index("lon")
    lat_index = lax.axis_index("lat")
    ens_index = lax.axis_index("ens")
    lon_count = lax.axis_size("lon")
    lat_count = lax.axis_size("lat")
    members = states.shape[0] * lax.axis_size("ens")
    lat_first = lat_index * lat_rows
    lat_total = lat_rows * lat_count
    kernel_number, group_count, width = mixing.shape[0], mixing.shape[1], mixing.shape[2]
    quarter = channels // lon_count
    owned, degrees = legendre.shape[0], legendre.shape[1]
    waves = owner_order.shape[0]
    main = 4 * owned
    gain_size = chunk_size(degrees // 2, lat_count)
    mix_size = chunk_size(kernel_number * width, lat_count)
    even = lat_index % 2 == 0
    blocks = WINDOWS * -(-sector // (WINDOWS * BLOCK))
    padded = blocks * BLOCK
    padded_in = padded + WINDOW - BLOCK
    sds = jax.ShapeDtypeStruct
    field_shape = sds((lat_rows, sector, channels), bf16)
    wide_shape = sds((lat_rows, padded, channels), f32)

    by_wave, by_point = wave_tables(owner_order, sector, lon_count)
    orders = lax.dynamic_slice_in_dim(owner_order, lat_index * owned, owned, 0)
    gains = lax.dynamic_slice_in_dim(spectral_gain, lon_index * quarter, quarter, 1).astype(f32)
    gains = jnp.concatenate([gains, gains], axis=1)
    leg, leg_turned = call(
        legendre_kernel,
        [sds(legendre.shape, bf16), sds((owned, lat_total, degrees), bf16)],
        (legendre,),
        4 * legendre.size * lat_total,
    )
    matrices = band_matrices(kernels, offsets, lat_first, lat_rows, lat_total)
    place = jnp.reshape(lon_index, (1,))
    parity = jnp.reshape(lat_index % 2, (1,))
    extent = lat_rows + 2 * BAND_REACH

    transform_flops = 4 * waves * LONGITUDES * lat_rows * quarter
    legendre_flops = 4 * owned * degrees * lat_total * 2 * quarter
    band_flops = 2 * blocks * matrices[0].size * channels
    row_scratch = pltpu.VMEM((4 * waves, LANES), f32)
    leg_scratch = [
        pltpu.VMEM((owned, degrees, LANES), f32),
        pltpu.VMEM(leg.shape, bf16),
        pltpu.VMEM(leg_turned.shape, bf16),
        pltpu.SemaphoreType.DMA((3, PARTS)),
    ]
    sent_shape = pltpu.HBM((lon_count, sector + EDGE, channels), bf16)
    spectrum_shape = pltpu.HBM((lon_count, sector, channels), bf16)
    tile = pl.BlockSpec((lat_rows, TILE, channels), lambda j: (0, j, 0))
    tiles = pl.cdiv(sector, TILE)

    def whole(x):
        return pl.BlockSpec(x.shape, lambda j: (0,) * x.ndim)

    def synthesized(got):
        return call(
            synthesis_kernel,
            [spectrum_shape],
            (got, by_point),
            transform_flops,
            [row_scratch, pltpu.VMEM(by_point.shape, bf16), pltpu.SemaphoreType.DMA((lon_count,))],
            places={1: pl.ANY},
        )[0]

    def band(x, far, other, which, turned):
        rest = rest_rows(x, even)
        matrix = matrices[which]
        outs = [pltpu.HBM(wide_shape.shape, f32)]
        specs = [pl.BlockSpec((lat_rows, WINDOWS * BLOCK, channels), lambda j: (0, j, 0))]
        if not turned:
            outs.append(pltpu.HBM((kernel_number, lat_rows, padded, channels), bf16))
            specs.append(
                pl.BlockSpec((kernel_number, lat_rows, WINDOWS * BLOCK, channels), lambda j: (0, 0, j, 0))
            )
        return call(
            functools.partial(band_kernel, turned),
            outs,
            (parity, hbm(x), hbm(far), hbm(rest), hbm(other), matrix, mixing),
            band_flops * 12,
            [
                pltpu.VMEM((kernel_number, channels, channels), bf16),
                pltpu.VMEM((extent, padded_in, channels), bf16),
                pltpu.SemaphoreType.DMA((4,)),
            ],
            grid=(blocks // WINDOWS,),
            blocks=[pl.BlockSpec(memory_space=SMEM)]
            + [pl.BlockSpec(memory_space=pl.ANY)] * 4
            + [whole(matrix), whole(mixing)],
            outs=specs,
        )

    (packed,) = call(pack_kernel, [sent_shape], (place, fields), 0, places={0: SMEM})
    circle = exchange(packed, "lon")
    circle, by_wave, by_point, leg, leg_turned, matrices, gains = lax.optimization_barrier(
        (circle, by_wave, by_point, leg, leg_turned, matrices, gains)
    )
    by_point, leg, leg_turned = hbm(by_point), hbm(leg), hbm(leg_turned)
    extended = with_columns(fields, circle)
    far = swapped_rows(extended, even)
    (analysed,) = call(
        analysis_kernel,
        [pltpu.HBM((lat_count, main, LANES), bf16)],
        (circle, by_wave),
        transform_flops,
        [row_scratch],
    )
    owned_rows = exchange(analysed, "lat")
    synthesis, coeffs = call(
        legendre_forward_kernel,
        [pltpu.HBM((lat_count, main, LANES), bf16), pltpu.HBM((owned, degrees, LANES), f32)],
        (orders, owned_rows, leg, leg_turned, gains),
        legendre_flops,
        [row_scratch, row_scratch] + leg_scratch,
        places={0: SMEM, 2: pl.ANY, 3: pl.ANY, -2: pl.ANY},
    )
    returned = exchange(synthesis, "lat")
    other = relayed_rows(far)
    spectrum = exchange(synthesized(returned), "lon")
    mixed, basis = band(extended, far, other, 0, False)
    next_state, grad_pre, packed_back = call(
        functools.partial(activation_kernel, sector - (tiles - 1) * TILE),
        [field_shape, pltpu.HBM(field_shape.shape, bf16), sent_shape],
        (place, hbm(spectrum), hbm(mixed), hbm(fields), hbm(cot)),
        40 * fields.size,
        [pltpu.VMEM((EDGE, channels), f32)],
        grid=(tiles,),
        blocks=[pl.BlockSpec(memory_space=SMEM), tile, tile, tile, tile],
        outs=[tile, tile, tile],
    )

    circle_back = exchange(packed_back, "lon")
    (mix_part,) = call(
        mixing_gradient_kernel,
        [sds((group_count, kernel_number, width, width), f32)],
        (basis, grad_pre),
        2 * kernel_number * fields.size * width,
    )
    mix_part = mix_part.reshape(group_count, kernel_number * width, width)
    swap = [(0, 1), (1, 0)]
    kept = lax.dynamic_index_in_dim(mix_part, ens_index, 0, False)
    sent = lax.dynamic_index_in_dim(mix_part, 1 - ens_index, 0, False)
    mix_got = lax.ppermute(sent, "ens", swap)
    circle_back, kept, mix_got = lax.optimization_barrier((circle_back, kept, mix_got))
    extended_back = with_columns(grad_pre, circle_back)
    far_back = swapped_rows(extended_back, even)
    (analysed_back,) = call(
        analysis_kernel,
        [pltpu.HBM((lat_count, main + 2 * mix_size, LANES), bf16)],
        (circle_back, by_wave, hbm(kept), hbm(mix_got)),
        transform_flops,
        [row_scratch, pltpu.VMEM((2,) + kept.shape, f32), pltpu.SemaphoreType.DMA((2,))],
        places={2: pl.ANY, 3: pl.ANY},
    )
    owned_back = exchange(analysed_back, "lat")
    synthesis_back, mix_sum = call(
        legendre_backward_kernel,
        [pltpu.HBM((lat_count, main + 2 * gain_size, LANES), bf16), sds((mix_size, LANES), f32)],
        (orders, owned_back, leg, leg_turned, gains, hbm(coeffs)),
        legendre_flops,
        [row_scratch, row_scratch, pltpu.VMEM((degrees, LANES), f32)] + leg_scratch,
        places={0: SMEM, 2: pl.ANY, 3: pl.ANY, 5: pl.ANY},
    )
    returned_back = exchange(synthesis_back, "lat")
    other_back = relayed_rows(far_back)
    for bit in (1, 2):
        mix_sum += lax.ppermute(mix_sum, "lon", [(i, i ^ bit) for i in range(lon_count)])
    returned_back, other_back, mix_sum = lax.optimization_barrier((returned_back, other_back, mix_sum))
    shares = call(
        share_kernel,
        [sds((lat_count, gain_size + mix_size, LANES), f32)],
        (returned_back, mix_sum),
        0,
    )[0]
    shares = exchange(shares, "lat")
    spectrum_back = exchange(synthesized(returned_back), "lon")
    (backward,) = band(extended_back, far_back, other_back, 1, True)
    (grad_state,) = call(
        finish_kernel,
        [field_shape],
        (hbm(spectrum_back), hbm(backward), hbm(cot)),
        4 * fields.size,
        grid=(tiles,),
        blocks=[tile, tile, tile],
        outs=[tile],
    )

    mix_scale = 1.0 / math.sqrt(members * lat_total * LONGITUDES)
    gain_scale = 1.0 / math.sqrt(2 * members * degrees)
    gain_mine, mix_mine = call(
        functools.partial(collect_kernel, degrees // 2),
        [sds((degrees // 2, LANES), f32), sds((kernel_number * width, LANES), f32)],
        (shares,),
        0,
    )
    mix_other = lax.ppermute(mix_mine, "ens", swap)
    gain_other = lax.ppermute(gain_mine, "ens", swap)
    grad_mixing, grad_gain = call(
        functools.partial(totals_kernel, mix_scale, gain_scale),
        [sds(mixing.shape, f32), sds((degrees, quarter), f32)],
        (jnp.reshape(ens_index, (1,)), gain_mine, gain_other, mix_mine, mix_other),
        0,
        places={0: SMEM},
    )
    return (next_state[None], grad_state[None], grad_mixing, grad_gain)


def solution(mesh):
    in_specs = (
        P("ens", "lat", "lon", None),
        P("ens", "lat", "lon", None),
        P(),
        P(),
        P(),
        P("lat", None, None),
        P(),
        P(),
    )
    out_specs = (P("ens", "lat", "lon", None), P("ens", "lat", "lon", None), P(), P(None, "lon"))
    return jax.shard_map(
        on_device, mesh=mesh, in_specs=in_specs, out_specs=out_specs, check_vma=False
    )
```

time: 426 us -> 265 us (0.62); the launches traced: 420 us -> 263 us
  blocking collectives: 123 us -> 0 us
  local copies, waits for them, and re-layouts: 67.4 us -> 17.1 us
  other arithmetic: 40.5 us -> 8.11 us
  waiting for transfers between devices: 67.9 us -> 97.7 us
  Pallas kernels: 31.6 us -> 54.3 us
  matrix products: 5.37 us -> 0.44 us
    all_gather x1 -> x0, blocking collectives: 113 us -> none  [on_device(): pieces_all = lax.all_gather(pieces_here, 'lat', axis=0)]
    all_to_all x8 -> x9, waiting for transfers between devices: 4.9 us -> 75.8 us  [exchange(): return lax.all_to_all(x, axis, split_axis=0, concat_axis=0, tiled=True)]
    ppermute x12 -> x11, waiting for transfers between devices: 63 us -> 22 us  [the longest x2 10.3 us: swapped_rows(): lax.ppermute(jnp.where(even, x[:BAND_REACH], x[1:BAND_REACH + 1]), 'lat',...]
    pallas_call x12 -> x18, Pallas kernels: 31.6 us -> 54.3 us  [call(): pl.pallas_call(kernel, grid=grid, out_shape=out_shape, in_specs=specs, ou...]
    unnamed x126 -> x52, local copies, waits for them, and re-layouts: 33.4 us -> 13 us
    reshape x10 -> x2, local copies, waits for them, and re-layouts: 19.5 us -> 0.79 us  [with_columns(): circle[:, sector:].reshape(peers, lat_rows, EDGE // lat_rows, channels)]
    another operation x13 -> x1, other arithmetic: 12.9 us -> 0.01 us  [band_matrices(): jnp.stack([jnp.transpose(forward, (1, 0, 2, 3)).reshape(outputs, entries)...]
    psum x1 -> x0, blocking collectives: 9.92 us -> none  [on_device(): mix_got = lax.psum(mix_got[:mix_rows] + mix_got[mix_rows:], 'lon')]
  transfers between devices with their start and end apart: 20 -> 20, of which waited for: 7 -> 14; matrix products, arithmetic and copies ran while one was open for 20% -> 5% of each run, Pallas kernels for 5% -> 15%
where the time goes in v2:
time: 265 us; the launch traced here: 263 us
  waiting for transfers between devices  97.7 us (37%)
  starting transfers between devices  84.3 us (32%)
  Pallas kernels  54.3 us (20%)
  local copies, waits for them, and re-layouts  17.1 us (6%)
  other arithmetic  8.11 us (3%)
    all_to_all x9, waiting for transfers between devices, exchange(): return lax.all_to_all(x, axis, split_axis=0, concat_axis=0, tiled=True)  75.8 us
    all_to_all x9, starting transfers between devices, exchange(): return lax.all_to_all(x, axis, split_axis=0, concat_axis=0, tiled=True)  58.8 us
    pallas_call x18, Pallas kernels, call(): pl.pallas_call(kernel, grid=grid, out_shape=out_shape, in_specs=specs, ou...  54.3 us
    unnamed x52, local copies, waits for them, and re-layouts  13 us
    ppermute x2, starting transfers between devices, rest_rows(): return lax.ppermute(jnp.where(even, x[BAND_REACH:], x[:1]), 'lat', pairs())  11.1 us
    ppermute x2, starting transfers between devices, swapped_rows(): lax.ppermute(jnp.where(even, x[:BAND_REACH], x[1:BAND_REACH + 1]), 'lat',...  10.8 us
    ppermute x2, waiting for transfers between devices, swapped_rows(): lax.ppermute(jnp.where(even, x[:BAND_REACH], x[1:BAND_REACH + 1]), 'lat',...  10.3 us
    ppermute x2, waiting for transfers between devices, on_device(): lax.ppermute(mix_sum, 'lon', [(i, i ^ bit) for i in range(lon_count)])  8.19 us
  transfers between devices with their start and end apart: 20, of which 14 were waited for; matrix products, arithmetic and copies ran while one was open for 5% of the time, Pallas kernels for 15%

profile of v2, /device:TPU:2, one launch (start us, length us, event | category | flops | bytes accessed | tf_op | source)
XLA Modules:
  0.0 263.2 jit_solution(1996255817556682521)
XLA Ops:
  3.1 5.9 %all-to-all-start = ((bf16[4,376,256]{2,1,0:T(8,128)(2,1)}), bf16[4,376,256]{2,1,0:T(8,128)(2,1)S(1)}, u32[]{:S(2)}, u32[]{:S(2)}) async-start(bf16[4,376,256]{2,1,0:T(8,128)(2,1)} %shard_map.111), calls=%async_computation | async-start | bytes 1540096 | tf_op jit(solution)/shard_map/all_to_all | solution.py:599
  21.6 7.1 %all-to-all-done.circle_ref = bf16[4,376,256]{2,1,0:T(8,128)(2,1)S(1)} async-done(((bf16[4,376,256]{2,1,0:T(8,128)(2,1)}), bf16[4,376,256]{2,1,0:T(8,128)(2,1)S(1)}, u32[]{:S(2)}, u32[]{:S(2)}) %all-to-all-start) | async-done | bytes 770080 | tf_op jit(solution)/shard_map/all_to_all | solution.py:599
  34.2 12.1 %all-to-all-start.1 = ((bf16[32,48,128]{2,1,0:T(8,128)(2,1)}), bf16[32,48,128]{2,1,0:T(8,128)(2,1)}, u32[]{:S(2)}, u32[]{:S(2)}) async-start(bf16[32,48,128]{2,1,0:T(8,128)(2,1)} %shard_map.115), calls=%async_computation.1 | async-start | bytes 786432 | tf_op jit(solution)/shard_map/all_to_all | solution.py:599
  49.6 5.4 %collective-permute-start = (bf16[3,368,256]{2,1,0:T(8,128)(2,1)}, bf16[3,368,256]{2,1,0:T(8,128)(2,1)}, u32[]{:S(2)}, u32[]{:S(2)}) collective-permute-start(bf16[3,368,256]{2,1,0:T(8,128)(2,1)} %slice_select_fusion.1), channel_id=1, source_target_pairs={{0,8},{8,0},{16,24},{24,16},{32,40},{40,32},{48,56},{56,48},{64,72... | collective-permute-start | bytes 1695752 | tf_op jit(solution)/shard_map/ppermute | solution.py:618
  55.1 9.4 %all-to-all-done.1.got_ref = bf16[32,48,128]{2,1,0:T(8,128)(2,1)} async-done(((bf16[32,48,128]{2,1,0:T(8,128)(2,1)}), bf16[32,48,128]{2,1,0:T(8,128)(2,1)}, u32[]{:S(2)}, u32[]{:S(2)}) %all-to-all-start.1) | async-done | bytes 393248 | tf_op jit(solution)/shard_map/all_to_all | solution.py:599
  64.5 5.3 %shard_map.116 = (bf16[32,48,128]{2,1,0:T(8,128)(2,1)}, f32[12,384,128]{2,1,0:T(8,128)}) custom-call(s32[12]{0:T(128)S(1)} %dynamic_slice.38.order_ref, bf16[32,48,128]{2,1,0:T(8,128)(2,1)} %all-to-all-done.1.got_ref, bf16[12,384,128]{2,1,0:T(8,128)(2,1)} %copy-done.4, bf16[12,128,384]{2,1,0:T(8,128)(2,1)} %copy-done.5, ...), custom_call_target="tpu_custom_call" | custom-call | flops 301989888 | bytes 5701680 | tf_op jit(solution)/shard_map/pallas_call | solution.py:43
  69.8 5.6 %all-to-all-start.2 = ((bf16[32,48,128]{2,1,0:T(8,128)(2,1)}), bf16[32,48,128]{2,1,0:T(8,128)(2,1)}, u32[]{:S(2)}, u32[]{:S(2)}) async-start(bf16[32,48,128]{2,1,0:T(8,128)(2,1)} %get-tuple-element.43), calls=%async_computation.2 | async-start | bytes 786432 | tf_op jit(solution)/shard_map/all_to_all | solution.py:599
  79.9 5.4 %collective-permute-start.1 = (bf16[1,368,256]{2,1,0:T(8,128)(2,1)}, bf16[1,368,256]{2,1,0:T(8,128)(2,1)}, u32[]{:S(2)}, u32[]{:S(2)}) collective-permute-start(bf16[1,368,256]{2,1,0:T(8,128)(2,1)} %slice_select_fusion.3), channel_id=1, source_target_pairs={{0,8},{8,0},{16,24},{24,16},{32,40},{40,32},{48,56},{56,48},{64,72... | collective-permute-start | bytes 565256 | tf_op jit(solution)/shard_map/ppermute | solution.py:628
  86.2 10.6 %all-to-all-done.2.got_ref = bf16[32,48,128]{2,1,0:T(8,128)(2,1)} async-done(((bf16[32,48,128]{2,1,0:T(8,128)(2,1)}), bf16[32,48,128]{2,1,0:T(8,128)(2,1)}, u32[]{:S(2)}, u32[]{:S(2)}) %all-to-all-start.2) | async-done | bytes 393248 | tf_op jit(solution)/shard_map/all_to_all | solution.py:599
  96.8 4.7 %shard_map.117 = bf16[4,360,256]{2,1,0:T(8,128)(2,1)} custom-call(bf16[32,48,128]{2,1,0:T(8,128)(2,1)} %all-to-all-done.2.got_ref, bf16[4,360,768]{2,1,0:T(8,128)(2,1)} %copy-done.1), custom_call_target="tpu_custom_call" | custom-call | flops 566231040 | bytes 3342336 | tf_op jit(solution)/shard_map/pallas_call | solution.py:43
  105.7 7.5 %shard_map.118 = (f32[4,384,256]{2,1,0:T(8,128)}, bf16[3,4,384,256]{3,2,1,0:T(8,128)(2,1)}) custom-call(s32[1]{0:T(128)} %bitcast.9.parity_ref, bf16[4,368,256]{2,1,0:T(8,128)(2,1)} %maximum_maximum_fusion.own_hbm, bf16[3,368,256]{2,1,0:T(8,128)(2,1)} %collective-permute-done.far_hbm, bf16[1,368,256]{2,1,0:T(8,128)(2,1)} %collective-permute-done.1.rest_hbm, ...), custom_call_target="tpu_custom_call" | custom-call | flops 13589544960 | bytes 6569988 | tf_op jit(solution)/shard_map/pallas_call | solution.py:43
  113.2 5.8 %all-to-all-done.3.spec_ref = bf16[4,360,256]{2,1,0:T(8,128)(2,1)} async-done(((bf16[4,360,256]{2,1,0:T(8,128)(2,1)}), bf16[4,360,256]{2,1,0:T(8,128)(2,1)}, u32[]{:S(2)}, u32[]{:S(2)}) %all-to-all-start.3) | async-done | bytes 737312 | tf_op jit(solution)/shard_map/all_to_all | solution.py:599
  119.1 5.2 %shard_map.119 = (bf16[4,360,256]{2,1,0:T(8,128)(2,1)}, bf16[4,360,256]{2,1,0:T(8,128)(2,1)}, bf16[4,376,256]{2,1,0:T(8,128)(2,1)}) custom-call(s32[1]{0:T(128)} %bitcast.place_ref, bf16[4,360,256]{2,1,0:T(8,128)(2,1)} %all-to-all-done.3.spec_ref, f32[4,384,256]{2,1,0:T(8,128)} %get-tuple-element.46.mixed_ref, bf16[4,360,256]{2,1,0:T(8,128)(2,1)} %bitcast.41, ...), custom_call_target="tpu_custom_call" | custom-call | flops 14745600 | bytes 6029316 | tf_op jit(solution)/shard_map/pallas_call | solution.py:43
  133.7 10.9 %all-to-all-done.4.circle_ref = bf16[4,376,256]{2,1,0:T(8,128)(2,1)S(1)} async-done(((bf16[4,376,256]{2,1,0:T(8,128)(2,1)}), bf16[4,376,256]{2,1,0:T(8,128)(2,1)S(1)}, u32[]{:S(2)}, u32[]{:S(2)}) %all-to-all-start.4) | async-done | bytes 770080 | tf_op jit(solution)/shard_map/all_to_all | solution.py:599
  147.4 7.7 %all-to-all-start.5 = ((bf16[32,80,128]{2,1,0:T(8,128)(2,1)}), bf16[32,80,128]{2,1,0:T(8,128)(2,1)S(1)}, u32[]{:S(2)}, u32[]{:S(2)}) async-start(bf16[32,80,128]{2,1,0:T(8,128)(2,1)} %shard_map.121), calls=%async_computation.5 | async-start | bytes 1310720 | tf_op jit(solution)/shard_map/all_to_all | solution.py:599
  155.4 5.5 %collective-permute-start.4 = (bf16[3,368,256]{2,1,0:T(8,128)(2,1)S(1)}, bf16[3,368,256]{2,1,0:T(8,128)(2,1)}, u32[]{:S(2)}, u32[]{:S(2)}) collective-permute-start(bf16[3,368,256]{2,1,0:T(8,128)(2,1)S(1)} %slice_select_fusion), channel_id=1, source_target_pairs={{0,8},{8,0},{16,24},{24,16},{32,40},{40,32},{48,56},{56,48},{64,72... | collective-permute-start | bytes 1695752 | tf_op jit(solution)/shard_map/ppermute | solution.py:618
  160.9 24.2 %all-to-all-done.5.got_ref = bf16[32,80,128]{2,1,0:T(8,128)(2,1)S(1)} async-done(((bf16[32,80,128]{2,1,0:T(8,128)(2,1)}), bf16[32,80,128]{2,1,0:T(8,128)(2,1)S(1)}, u32[]{:S(2)}, u32[]{:S(2)}) %all-to-all-start.5) | async-done | bytes 655392 | tf_op jit(solution)/shard_map/all_to_all | solution.py:599
  189.6 5.0 %all-to-all-start.6 = ((bf16[32,64,128]{2,1,0:T(8,128)(2,1)}), bf16[32,64,128]{2,1,0:T(8,128)(2,1)S(1)}, u32[]{:S(2)}, u32[]{:S(2)}) async-start(bf16[32,64,128]{2,1,0:T(8,128)(2,1)} %get-tuple-element.55), calls=%async_computation.6 | async-start | bytes 1048576 | tf_op jit(solution)/shard_map/all_to_all | solution.py:599
  194.6 9.1 %collective-permute-done.4.far_hbm = bf16[3,368,256]{2,1,0:T(8,128)(2,1)} collective-permute-done((bf16[3,368,256]{2,1,0:T(8,128)(2,1)S(1)}, bf16[3,368,256]{2,1,0:T(8,128)(2,1)}, u32[]{:S(2)}, u32[]{:S(2)}) %collective-permute-start.4) | collective-permute-done | bytes 565280 | tf_op jit(solution)/shard_map/ppermute | solution.py:618
  208.8 4.5 %collective-permute-done.7 = f32[16,128]{1,0:T(8,128)S(1)} collective-permute-done((f32[16,128]{1,0:T(8,128)S(1)}, f32[16,128]{1,0:T(8,128)S(1)}, u32[]{:S(2)}, u32[]{:S(2)}) %collective-permute-start.7) | collective-permute-done | bytes 8224 | tf_op jit(solution)/shard_map/ppermute | solution.py:802
  216.0 11.3 %all-to-all-start.8 = ((f32[32,24,128]{2,1,0:T(8,128)}), f32[32,24,128]{2,1,0:T(8,128)S(1)}, u32[]{:S(2)}, u32[]{:S(2)}) async-start(f32[32,24,128]{2,1,0:T(8,128)} %shard_map.126), calls=%async_computation.8 | async-start | bytes 786432 | tf_op jit(solution)/shard_map/all_to_all | solution.py:599
  227.4 5.7 %collective-permute-start.8 = (bf16[1,368,256]{2,1,0:T(8,128)(2,1)S(1)}, bf16[1,368,256]{2,1,0:T(8,128)(2,1)S(1)}, u32[]{:S(2)}, u32[]{:S(2)}) collective-permute-start(bf16[1,368,256]{2,1,0:T(8,128)(2,1)S(1)} %slice_select_fusion.2), channel_id=1, source_target_pairs={{0,8},{8,0},{16,24},{24,16},{32,40},{40,32},{48,56},{56,48},{64,72... | collective-permute-start | bytes 565256 | tf_op jit(solution)/shard_map/ppermute | solution.py:628
  236.9 4.8 %all-to-all-done.8.got_ref = f32[32,24,128]{2,1,0:T(8,128)S(1)} async-done(((f32[32,24,128]{2,1,0:T(8,128)}), f32[32,24,128]{2,1,0:T(8,128)S(1)}, u32[]{:S(2)}, u32[]{:S(2)}) %all-to-all-start.8) | async-done | bytes 393248 | tf_op jit(solution)/shard_map/all_to_all | solution.py:599
  246.6 7.3 %shard_map.124.back_ref = f32[4,384,256]{2,1,0:T(8,128)} custom-call(s32[1]{0:T(128)} %bitcast.9.parity_ref, bf16[4,368,256]{2,1,0:T(8,128)(2,1)} %copy-done.18, bf16[3,368,256]{2,1,0:T(8,128)(2,1)} %collective-permute-done.4.far_hbm, bf16[1,368,256]{2,1,0:T(8,128)(2,1)} %copy-done.23, bf16[3,368,256]{2,1,0:T(8,128)(2,1)} %copy-done.22, ...), custom_call_target="tpu_custom_call" | custom-call | flops 13589544960 | bytes 4210692 | tf_op jit(solution)/shard_map/pallas_call | solution.py:43
  (125 shorter events, 76.0 us)
Async XLA Ops:
  0.6 20.8 %copy-start = (bf16[384,256]{1,0:T(8,128)(2,1)S(1)}, bf16[384,256]{1,0:T(8,128)(2,1)}, u32[]{:S(2)}) copy-start(bf16[384,256]{1,0:T(8,128)(2,1)} %param.15) | copy-start | bytes 589828
  3.1 25.7 %all-to-all-start = ((bf16[4,376,256]{2,1,0:T(8,128)(2,1)}), bf16[4,376,256]{2,1,0:T(8,128)(2,1)S(1)}, u32[]{:S(2)}, u32[]{:S(2)}) async-start(bf16[4,376,256]{2,1,0:T(8,128)(2,1)} %shard_map.111), calls=%async_computation | async-start | bytes 1540096 | tf_op jit(solution)/shard_map/all_to_all | solution.py:599
  34.2 30.3 %all-to-all-start.1 = ((bf16[32,48,128]{2,1,0:T(8,128)(2,1)}), bf16[32,48,128]{2,1,0:T(8,128)(2,1)}, u32[]{:S(2)}, u32[]{:S(2)}) async-start(bf16[32,48,128]{2,1,0:T(8,128)(2,1)} %shard_map.115), calls=%async_computation.1 | async-start | bytes 786432 | tf_op jit(solution)/shard_map/all_to_all | solution.py:599
  49.6 27.1 %collective-permute-start = (bf16[3,368,256]{2,1,0:T(8,128)(2,1)}, bf16[3,368,256]{2,1,0:T(8,128)(2,1)}, u32[]{:S(2)}, u32[]{:S(2)}) collective-permute-start(bf16[3,368,256]{2,1,0:T(8,128)(2,1)} %slice_select_fusion.1), channel_id=1, source_target_pairs={{0,8},{8,0},{16,24},{24,16},{32,40},{40,32},{48,56},{56,48},{64,72... | collective-permute-start | bytes 1695752 | tf_op jit(solution)/shard_map/ppermute | solution.py:618
  55.1 30.2 %copy-start.9 = (bf16[2,384,480]{2,1,0:T(8,128)(2,1)S(1)}, bf16[2,384,480]{2,1,0:T(8,128)(2,1)}, u32[]{:S(2)}) copy-start(bf16[2,384,480]{2,1,0:T(8,128)(2,1)} %copy-done.8) | copy-start | bytes 2211844
  69.8 27.0 %all-to-all-start.2 = ((bf16[32,48,128]{2,1,0:T(8,128)(2,1)}), bf16[32,48,128]{2,1,0:T(8,128)(2,1)}, u32[]{:S(2)}, u32[]{:S(2)}) async-start(bf16[32,48,128]{2,1,0:T(8,128)(2,1)} %get-tuple-element.43), calls=%async_computation.2 | async-start | bytes 786432 | tf_op jit(solution)/shard_map/all_to_all | solution.py:599
  76.7 29.0 %collective-permute-start.2 = (bf16[3,368,256]{2,1,0:T(8,128)(2,1)}, bf16[3,368,256]{2,1,0:T(8,128)(2,1)}, u32[]{:S(2)}, u32[]{:S(2)}) collective-permute-start(bf16[3,368,256]{2,1,0:T(8,128)(2,1)} %collective-permute-done.far_hbm), channel_id=1, source_target_pairs={{0,16},{8,248},{16,32},{24,8},{32,48},{40,24},{48,64},{56,40},{64,... | collective-permute-start | bytes 1695752 | tf_op jit(solution)/shard_map/ppermute | solution.py:624
  79.9 25.8 %collective-permute-start.1 = (bf16[1,368,256]{2,1,0:T(8,128)(2,1)}, bf16[1,368,256]{2,1,0:T(8,128)(2,1)}, u32[]{:S(2)}, u32[]{:S(2)}) collective-permute-start(bf16[1,368,256]{2,1,0:T(8,128)(2,1)} %slice_select_fusion.3), channel_id=1, source_target_pairs={{0,8},{8,0},{16,24},{24,16},{32,40},{40,32},{48,56},{56,48},{64,72... | collective-permute-start | bytes 565256 | tf_op jit(solution)/shard_map/ppermute | solution.py:628
  101.5 17.6 %all-to-all-start.3 = ((bf16[4,360,256]{2,1,0:T(8,128)(2,1)}), bf16[4,360,256]{2,1,0:T(8,128)(2,1)}, u32[]{:S(2)}, u32[]{:S(2)}) async-start(bf16[4,360,256]{2,1,0:T(8,128)(2,1)} %shard_map.117), calls=%async_computation.3 | async-start | bytes 1474560 | tf_op jit(solution)/shard_map/all_to_all | solution.py:599
  124.2 20.4 %all-to-all-start.4 = ((bf16[4,376,256]{2,1,0:T(8,128)(2,1)}), bf16[4,376,256]{2,1,0:T(8,128)(2,1)S(1)}, u32[]{:S(2)}, u32[]{:S(2)}) async-start(bf16[4,376,256]{2,1,0:T(8,128)(2,1)} %get-tuple-element.48), calls=%async_computation.4 | async-start | bytes 1540096 | tf_op jit(solution)/shard_map/all_to_all | solution.py:599
  132.1 1.6 collective-permute-start.3
  147.4 37.7 %all-to-all-start.5 = ((bf16[32,80,128]{2,1,0:T(8,128)(2,1)}), bf16[32,80,128]{2,1,0:T(8,128)(2,1)S(1)}, u32[]{:S(2)}, u32[]{:S(2)}) async-start(bf16[32,80,128]{2,1,0:T(8,128)(2,1)} %shard_map.121), calls=%async_computation.5 | async-start | bytes 1310720 | tf_op jit(solution)/shard_map/all_to_all | solution.py:599
  155.4 72.0 %copy-start.18 = (bf16[4,368,256]{2,1,0:T(8,128)(2,1)}, bf16[4,368,256]{2,1,0:T(8,128)(2,1)S(1)}, u32[]{:S(2)}) copy-start(bf16[4,368,256]{2,1,0:T(8,128)(2,1)S(1)} %maximum_maximum_fusion.1.own_hbm) | copy-start | bytes 2260996
  155.4 48.2 %collective-permute-start.4 = (bf16[3,368,256]{2,1,0:T(8,128)(2,1)S(1)}, bf16[3,368,256]{2,1,0:T(8,128)(2,1)}, u32[]{:S(2)}, u32[]{:S(2)}) collective-permute-start(bf16[3,368,256]{2,1,0:T(8,128)(2,1)S(1)} %slice_select_fusion), channel_id=1, source_target_pairs={{0,8},{8,0},{16,24},{24,16},{32,40},{40,32},{48,56},{56,48},{64,72... | collective-permute-start | bytes 1695752 | tf_op jit(solution)/shard_map/ppermute | solution.py:618
  189.6 25.6 %all-to-all-start.6 = ((bf16[32,64,128]{2,1,0:T(8,128)(2,1)}), bf16[32,64,128]{2,1,0:T(8,128)(2,1)S(1)}, u32[]{:S(2)}, u32[]{:S(2)}) async-start(bf16[32,64,128]{2,1,0:T(8,128)(2,1)} %get-tuple-element.55), calls=%async_computation.6 | async-start | bytes 1048576 | tf_op jit(solution)/shard_map/all_to_all | solution.py:599
  203.6 11.5 %collective-permute-start.5 = (bf16[3,368,256]{2,1,0:T(8,128)(2,1)}, bf16[3,368,256]{2,1,0:T(8,128)(2,1)S(1)}, u32[]{:S(2)}, u32[]{:S(2)}) collective-permute-start(bf16[3,368,256]{2,1,0:T(8,128)(2,1)} %collective-permute-done.4.far_hbm), channel_id=1, source_target_pairs={{0,16},{8,248},{16,32},{24,8},{32,48},{40,24},{48,64},{56,40},{64,... | collective-permute-start | bytes 1695752 | tf_op jit(solution)/shard_map/ppermute | solution.py:624
  205.1 3.7 %collective-permute-start.6 = (f32[16,128]{1,0:T(8,128)S(1)}, f32[16,128]{1,0:T(8,128)S(1)}, u32[]{:S(2)}, u32[]{:S(2)}) collective-permute-start(f32[16,128]{1,0:T(8,128)S(1)} %get-tuple-element.56), channel_id=1, source_target_pairs={{0,2},{2,0},{4,6},{6,4},{1,3},{3,1},{5,7},{7,5},{8,10},{10,8},{12,... | collective-permute-start | bytes 24584 | tf_op jit(solution)/shard_map/ppermute | solution.py:802
  208.8 4.5 %collective-permute-start.7 = (f32[16,128]{1,0:T(8,128)S(1)}, f32[16,128]{1,0:T(8,128)S(1)}, u32[]{:S(2)}, u32[]{:S(2)}) collective-permute-start(f32[16,128]{1,0:T(8,128)S(1)} %add.160), channel_id=1, source_target_pairs={{0,4},{2,6},{4,0},{6,2},{1,5},{3,7},{5,1},{7,3},{8,12},{10,14},{12... | collective-permute-start | bytes 24584 | tf_op jit(solution)/shard_map/ppermute | solution.py:802
  215.2 21.7 %copy-start.22 = (bf16[3,368,256]{2,1,0:T(8,128)(2,1)}, bf16[3,368,256]{2,1,0:T(8,128)(2,1)S(1)}, u32[]{:S(2)}) copy-start(bf16[3,368,256]{2,1,0:T(8,128)(2,1)S(1)} %collective-permute-done.5.other_hbm) | copy-start | bytes 1695748
  216.0 25.7 %all-to-all-start.8 = ((f32[32,24,128]{2,1,0:T(8,128)}), f32[32,24,128]{2,1,0:T(8,128)S(1)}, u32[]{:S(2)}, u32[]{:S(2)}) async-start(f32[32,24,128]{2,1,0:T(8,128)} %shard_map.126), calls=%async_computation.8 | async-start | bytes 786432 | tf_op jit(solution)/shard_map/all_to_all | solution.py:599
  227.4 18.5 %collective-permute-start.8 = (bf16[1,368,256]{2,1,0:T(8,128)(2,1)S(1)}, bf16[1,368,256]{2,1,0:T(8,128)(2,1)S(1)}, u32[]{:S(2)}, u32[]{:S(2)}) collective-permute-start(bf16[1,368,256]{2,1,0:T(8,128)(2,1)S(1)} %slice_select_fusion.2), channel_id=1, source_target_pairs={{0,8},{8,0},{16,24},{24,16},{32,40},{40,32},{48,56},{56,48},{64,72... | collective-permute-start | bytes 565256 | tf_op jit(solution)/shard_map/ppermute | solution.py:628
  241.8 16.6 %all-to-all-start.7 = ((bf16[4,360,256]{2,1,0:T(8,128)(2,1)}), bf16[4,360,256]{2,1,0:T(8,128)(2,1)S(1)}, u32[]{:S(2)}, u32[]{:S(2)}) async-start(bf16[4,360,256]{2,1,0:T(8,128)(2,1)} %shard_map.123), calls=%async_computation.7 | async-start | bytes 1474560 | tf_op jit(solution)/shard_map/all_to_all | solution.py:599
  245.3 8.6 %collective-permute-start.10 = (f32[384,128]{1,0:T(8,128)S(1)}, f32[384,128]{1,0:T(8,128)S(1)}, u32[]{:S(2)}, u32[]{:S(2)}) collective-permute-start(f32[384,128]{1,0:T(8,128)S(1)} %get-tuple-element.61.mine_ref), channel_id=1, source_target_pairs={{0,1},{1,0},{2,3},{3,2},{4,5},{5,4},{6,7},{7,6},{8,9},{9,8},{10,11... | collective-permute-start | bytes 589832 | tf_op jit(solution)/shard_map/ppermute | solution.py:831
  245.4 8.5 %collective-permute-start.9 = (f32[192,128]{1,0:T(8,128)S(1)}, f32[192,128]{1,0:T(8,128)S(1)}, u32[]{:S(2)}, u32[]{:S(2)}) collective-permute-start(f32[192,128]{1,0:T(8,128)S(1)} %get-tuple-element.60.gain_mine_ref), channel_id=1, source_target_pairs={{0,1},{1,0},{2,3},{3,2},{4,5},{5,4},{6,7},{7,6},{8,9},{9,8},{10,11... | collective-permute-start | bytes 294920 | tf_op jit(solution)/shard_map/ppermute | solution.py:832
  (21 other events, 121.9 us)

commit v3 on v2

--- a/solution.py
+++ b/solution.py
@@ -128,7 +128,7 @@
     if copies:
         for copy in copies:
             copy.wait()
-        out_ref[:, main:, :] = split_chunks(terms_ref[0] + terms_ref[1], peers)
+        out_ref[:, main:, :] = split_chunks(terms_ref[0] + terms_ref[1], peers)[:, 0 : out_ref.shape[1] - main, :]
 
 
 def chunk_size(rows, peers):
@@ -254,7 +254,7 @@
         for copy in reads[p]:
             copy.start()
     rows_in_ref[...] = got_ref[:, 0:main, :].astype(f32).reshape(peers * main, LANES)
-    mix_ref[...] = joined(got_ref[:, main:, :])
+    mix_ref[...] = jnp.sum(got_ref[:, main:, :].astype(f32), axis=0)
 
     def use(k, coeffs):
         term = coeffs * held_ref[k]
@@ -459,17 +459,21 @@
 
 def share_kernel(got_ref, mix_ref, out_ref):
     peers = got_ref.shape[0]
-    gain_size = out_ref.shape[1] - mix_ref.shape[0]
+    gain_size = out_ref.shape[1] // 2 - mix_ref.shape[0]
     main = got_ref.shape[1] - 2 * gain_size
     total = jnp.concatenate([joined(got_ref[:, main:, :]), mix_ref[...]], axis=0)
-    out_ref[...] = jnp.broadcast_to(total[None], out_ref.shape)
+    high = total.astype(bf16).astype(f32)
+    both = jnp.concatenate([high, total - high], axis=0).astype(bf16)
+    out_ref[...] = jnp.broadcast_to(both[None], out_ref.shape)
 
 
 def collect_kernel(gain_rows, got_ref, gain_ref, mix_ref):
     peers, mix_rows = got_ref.shape[0], mix_ref.shape[0]
     size, mix_size = chunk_size(gain_rows, peers), chunk_size(mix_rows, peers)
-    gain_ref[...] = got_ref[0 : gain_rows // size, 0:size, :].reshape(gain_rows, LANES)
-    mix_ref[...] = got_ref[0 : mix_rows // mix_size, size:, :].reshape(mix_rows, LANES)
+    half = got_ref.shape[1] // 2
+    total = got_ref[:, 0:half, :].astype(f32) + got_ref[:, half:, :].astype(f32)
+    gain_ref[...] = total[0 : gain_rows // size, 0:size, :].reshape(gain_rows, LANES)
+    mix_ref[...] = total[0 : mix_rows // mix_size, size:, :].reshape(mix_rows, LANES)
 
 
 def totals_kernel(
@@ -731,8 +735,6 @@
         (circle, by_wave, by_point, leg, leg_turned, matrices, gains)
     )
     by_point, leg, leg_turned = hbm(by_point), hbm(leg), hbm(leg_turned)
-    extended = with_columns(fields, circle)
-    far = swapped_rows(extended, even)
     (analysed,) = call(
         analysis_kernel,
         [pltpu.HBM((lat_count, main, LANES), bf16)],
@@ -740,6 +742,9 @@
         transform_flops,
         [row_scratch],
     )
+    circle, analysed = lax.optimization_barrier((circle, analysed))
+    extended = with_columns(fields, circle)
+    far = swapped_rows(extended, even)
     owned_rows = exchange(analysed, "lat")
     synthesis, coeffs = call(
         legendre_forward_kernel,
@@ -781,7 +786,7 @@
     far_back = swapped_rows(extended_back, even)
     (analysed_back,) = call(
         analysis_kernel,
-        [pltpu.HBM((lat_count, main + 2 * mix_size, LANES), bf16)],
+        [pltpu.HBM((lat_count, main + mix_size, LANES), bf16)],
         (circle_back, by_wave, hbm(kept), hbm(mix_got)),
         transform_flops,
         [row_scratch, pltpu.VMEM((2,) + kept.shape, f32), pltpu.SemaphoreType.DMA((2,))],
@@ -803,7 +808,7 @@
     returned_back, other_back, mix_sum = lax.optimization_barrier((returned_back, other_back, mix_sum))
     shares = call(
         share_kernel,
-        [sds((lat_count, gain_size + mix_size, LANES), f32)],
+        [pltpu.HBM((lat_count, 2 * (gain_size + mix_size), LANES), bf16)],
         (returned_back, mix_sum),
         0,
     )[0]

time: 265 us -> 261 us (0.985)
    all_to_all x9, waiting for transfers between devices: 75.8 us -> 71 us  [exchange(): return lax.all_to_all(x, axis, split_axis=0, concat_axis=0, tiled=True)]
    unnamed x52 -> x56, local copies, waits for them, and re-layouts: 13 us -> 13.9 us
  transfers between devices with their start and end apart: 20 -> 20, of which waited for: 14 -> 14; matrix products, arithmetic and copies ran while one was open for 5% -> 4% of each run, Pallas kernels for 15% -> 15%
where the time goes in v3:
time: 261 us; the launch traced here: 260 us
  waiting for transfers between devices  95.4 us (37%)
  starting transfers between devices  84.6 us (32%)
  Pallas kernels  54.2 us (21%)
  local copies, waits for them, and re-layouts  18 us (7%)
  other arithmetic  5.98 us (2%)
    all_to_all x9, waiting for transfers between devices, exchange(): return lax.all_to_all(x, axis, split_axis=0, concat_axis=0, tiled=True)  71 us
    all_to_all x9, starting transfers between devices, exchange(): return lax.all_to_all(x, axis, split_axis=0, concat_axis=0, tiled=True)  60.1 us
    pallas_call x18, Pallas kernels, call(): pl.pallas_call(kernel, grid=grid, out_shape=out_shape, in_specs=specs, ou...  54.2 us
    unnamed x56, local copies, waits for them, and re-layouts  13.9 us
    ppermute x2, waiting for transfers between devices, swapped_rows(): lax.ppermute(jnp.where(even, x[:BAND_REACH], x[1:BAND_REACH + 1]), 'lat',...  12.6 us
    ppermute x2, starting transfers between devices, swapped_rows(): lax.ppermute(jnp.where(even, x[:BAND_REACH], x[1:BAND_REACH + 1]), 'lat',...  10.8 us
    ppermute x2, starting transfers between devices, rest_rows(): return lax.ppermute(jnp.where(even, x[BAND_REACH:], x[:1]), 'lat', pairs())  10.2 us
    ppermute x2, waiting for transfers between devices, on_device(): lax.ppermute(mix_sum, 'lon', [(i, i ^ bit) for i in range(lon_count)])  8.19 us
  transfers between devices with their start and end apart: 20, of which 14 were waited for; matrix products, arithmetic and copies ran while one was open for 4% of the time, Pallas kernels for 15%

profile of v3, /device:TPU:2, one launch (start us, length us, event | category | flops | bytes accessed | tf_op | source)
XLA Modules:
  0.0 259.8 jit_solution(10735630626068963700)
XLA Ops:
  3.1 5.9 %all-to-all-start = ((bf16[4,376,256]{2,1,0:T(8,128)(2,1)}), bf16[4,376,256]{2,1,0:T(8,128)(2,1)S(1)}, u32[]{:S(2)}, u32[]{:S(2)}) async-start(bf16[4,376,256]{2,1,0:T(8,128)(2,1)} %shard_map.111), calls=%async_computation | async-start | bytes 1540096 | tf_op jit(solution)/shard_map/all_to_all | solution.py:603
  21.6 7.1 %all-to-all-done.circle_ref = bf16[4,376,256]{2,1,0:T(8,128)(2,1)S(1)} async-done(((bf16[4,376,256]{2,1,0:T(8,128)(2,1)}), bf16[4,376,256]{2,1,0:T(8,128)(2,1)S(1)}, u32[]{:S(2)}, u32[]{:S(2)}) %all-to-all-start) | async-done | bytes 770080 | tf_op jit(solution)/shard_map/all_to_all | solution.py:603
  33.4 12.1 %all-to-all-start.1 = ((bf16[32,48,128]{2,1,0:T(8,128)(2,1)}), bf16[32,48,128]{2,1,0:T(8,128)(2,1)}, u32[]{:S(2)}, u32[]{:S(2)}) async-start(bf16[32,48,128]{2,1,0:T(8,128)(2,1)} %shard_map.115), calls=%async_computation.1 | async-start | bytes 786432 | tf_op jit(solution)/shard_map/all_to_all | solution.py:603
  48.3 5.4 %collective-permute-start = (bf16[3,368,256]{2,1,0:T(8,128)(2,1)}, bf16[3,368,256]{2,1,0:T(8,128)(2,1)}, u32[]{:S(2)}, u32[]{:S(2)}) collective-permute-start(bf16[3,368,256]{2,1,0:T(8,128)(2,1)} %slice_select_fusion.1), channel_id=1, source_target_pairs={{0,8},{8,0},{16,24},{24,16},{32,40},{40,32},{48,56},{56,48},{64,72... | collective-permute-start | bytes 1695752 | tf_op jit(solution)/shard_map/ppermute | solution.py:622
  53.7 10.1 %all-to-all-done.1.got_ref = bf16[32,48,128]{2,1,0:T(8,128)(2,1)} async-done(((bf16[32,48,128]{2,1,0:T(8,128)(2,1)}), bf16[32,48,128]{2,1,0:T(8,128)(2,1)}, u32[]{:S(2)}, u32[]{:S(2)}) %all-to-all-start.1) | async-done | bytes 393248 | tf_op jit(solution)/shard_map/all_to_all | solution.py:603
  63.8 5.3 %shard_map.116 = (bf16[32,48,128]{2,1,0:T(8,128)(2,1)}, f32[12,384,128]{2,1,0:T(8,128)}) custom-call(s32[12]{0:T(128)S(1)} %dynamic_slice.38.order_ref, bf16[32,48,128]{2,1,0:T(8,128)(2,1)} %all-to-all-done.1.got_ref, bf16[12,384,128]{2,1,0:T(8,128)(2,1)} %copy-done.4, bf16[12,128,384]{2,1,0:T(8,128)(2,1)} %copy-done.5, ...), custom_call_target="tpu_custom_call" | custom-call | flops 301989888 | bytes 5701680 | tf_op jit(solution)/shard_map/pallas_call | solution.py:43
  69.1 5.6 %all-to-all-start.2 = ((bf16[32,48,128]{2,1,0:T(8,128)(2,1)}), bf16[32,48,128]{2,1,0:T(8,128)(2,1)}, u32[]{:S(2)}, u32[]{:S(2)}) async-start(bf16[32,48,128]{2,1,0:T(8,128)(2,1)} %get-tuple-element.46), calls=%async_computation.2 | async-start | bytes 786432 | tf_op jit(solution)/shard_map/all_to_all | solution.py:603
  79.7 4.6 %collective-permute-start.1 = (bf16[1,368,256]{2,1,0:T(8,128)(2,1)}, bf16[1,368,256]{2,1,0:T(8,128)(2,1)}, u32[]{:S(2)}, u32[]{:S(2)}) collective-permute-start(bf16[1,368,256]{2,1,0:T(8,128)(2,1)} %slice_select_fusion.3), channel_id=1, source_target_pairs={{0,8},{8,0},{16,24},{24,16},{32,40},{40,32},{48,56},{56,48},{64,72... | collective-permute-start | bytes 565256 | tf_op jit(solution)/shard_map/ppermute | solution.py:632
  85.2 10.7 %all-to-all-done.2.got_ref = bf16[32,48,128]{2,1,0:T(8,128)(2,1)} async-done(((bf16[32,48,128]{2,1,0:T(8,128)(2,1)}), bf16[32,48,128]{2,1,0:T(8,128)(2,1)}, u32[]{:S(2)}, u32[]{:S(2)}) %all-to-all-start.2) | async-done | bytes 393248 | tf_op jit(solution)/shard_map/all_to_all | solution.py:603
  96.0 4.7 %shard_map.117 = bf16[4,360,256]{2,1,0:T(8,128)(2,1)} custom-call(bf16[32,48,128]{2,1,0:T(8,128)(2,1)} %all-to-all-done.2.got_ref, bf16[4,360,768]{2,1,0:T(8,128)(2,1)} %copy-done.1), custom_call_target="tpu_custom_call" | custom-call | flops 566231040 | bytes 3342336 | tf_op jit(solution)/shard_map/pallas_call | solution.py:43
  104.9 7.5 %shard_map.118 = (f32[4,384,256]{2,1,0:T(8,128)}, bf16[3,4,384,256]{3,2,1,0:T(8,128)(2,1)}) custom-call(s32[1]{0:T(128)} %bitcast.9.parity_ref, bf16[4,368,256]{2,1,0:T(8,128)(2,1)} %copy-done.19, bf16[3,368,256]{2,1,0:T(8,128)(2,1)} %collective-permute-done.far_hbm, bf16[1,368,256]{2,1,0:T(8,128)(2,1)} %collective-permute-done.1.rest_hbm, ...), custom_call_target="tpu_custom_call" | custom-call | flops 13589544960 | bytes 6569988 | tf_op jit(solution)/shard_map/pallas_call | solution.py:43
  112.4 5.7 %all-to-all-done.3.spec_ref = bf16[4,360,256]{2,1,0:T(8,128)(2,1)} async-done(((bf16[4,360,256]{2,1,0:T(8,128)(2,1)}), bf16[4,360,256]{2,1,0:T(8,128)(2,1)}, u32[]{:S(2)}, u32[]{:S(2)}) %all-to-all-start.3) | async-done | bytes 737312 | tf_op jit(solution)/shard_map/all_to_all | solution.py:603
  118.1 5.1 %shard_map.119 = (bf16[4,360,256]{2,1,0:T(8,128)(2,1)}, bf16[4,360,256]{2,1,0:T(8,128)(2,1)}, bf16[4,376,256]{2,1,0:T(8,128)(2,1)}) custom-call(s32[1]{0:T(128)} %bitcast.place_ref, bf16[4,360,256]{2,1,0:T(8,128)(2,1)} %all-to-all-done.3.spec_ref, f32[4,384,256]{2,1,0:T(8,128)} %get-tuple-element.50.mixed_ref, bf16[4,360,256]{2,1,0:T(8,128)(2,1)} %bitcast.41, ...), custom_call_target="tpu_custom_call" | custom-call | flops 14745600 | bytes 6029316 | tf_op jit(solution)/shard_map/pallas_call | solution.py:43
  132.8 10.7 %all-to-all-done.4.circle_ref = bf16[4,376,256]{2,1,0:T(8,128)(2,1)S(1)} async-done(((bf16[4,376,256]{2,1,0:T(8,128)(2,1)}), bf16[4,376,256]{2,1,0:T(8,128)(2,1)S(1)}, u32[]{:S(2)}, u32[]{:S(2)}) %all-to-all-start.4) | async-done | bytes 770080 | tf_op jit(solution)/shard_map/all_to_all | solution.py:603
  146.1 8.7 %all-to-all-start.5 = ((bf16[32,64,128]{2,1,0:T(8,128)(2,1)}), bf16[32,64,128]{2,1,0:T(8,128)(2,1)S(1)}, u32[]{:S(2)}, u32[]{:S(2)}) async-start(bf16[32,64,128]{2,1,0:T(8,128)(2,1)} %shard_map.121), calls=%async_computation.5 | async-start | bytes 1048576 | tf_op jit(solution)/shard_map/all_to_all | solution.py:603
  155.2 5.5 %collective-permute-start.4 = (bf16[3,368,256]{2,1,0:T(8,128)(2,1)S(1)}, bf16[3,368,256]{2,1,0:T(8,128)(2,1)S(1)}, u32[]{:S(2)}, u32[]{:S(2)}) collective-permute-start(bf16[3,368,256]{2,1,0:T(8,128)(2,1)S(1)} %slice_select_fusion), channel_id=1, source_target_pairs={{0,8},{8,0},{16,24},{24,16},{32,40},{40,32},{48,56},{56,48},{64,72... | collective-permute-start | bytes 1695752 | tf_op jit(solution)/shard_map/ppermute | solution.py:622
  160.7 19.3 %all-to-all-done.5.got_ref = bf16[32,64,128]{2,1,0:T(8,128)(2,1)S(1)} async-done(((bf16[32,64,128]{2,1,0:T(8,128)(2,1)}), bf16[32,64,128]{2,1,0:T(8,128)(2,1)S(1)}, u32[]{:S(2)}, u32[]{:S(2)}) %all-to-all-start.5) | async-done | bytes 524320 | tf_op jit(solution)/shard_map/all_to_all | solution.py:603
  180.0 4.5 %shard_map.122 = (bf16[32,64,128]{2,1,0:T(8,128)(2,1)}, f32[16,128]{1,0:T(8,128)S(1)}) custom-call(s32[12]{0:T(128)S(1)} %dynamic_slice.38.order_ref, bf16[32,64,128]{2,1,0:T(8,128)(2,1)S(1)} %all-to-all-done.5.got_ref, bf16[12,384,128]{2,1,0:T(8,128)(2,1)} %copy-done.4, bf16[12,128,384]{2,1,0:T(8,128)(2,1)} %copy-done.5, ...), custom_call_target="tpu_custom_call" | custom-call | flops 301989888 | bytes 5972016 | tf_op jit(solution)/shard_map/pallas_call | solution.py:43
  184.5 4.9 %all-to-all-start.6 = ((bf16[32,64,128]{2,1,0:T(8,128)(2,1)}), bf16[32,64,128]{2,1,0:T(8,128)(2,1)S(1)}, u32[]{:S(2)}, u32[]{:S(2)}) async-start(bf16[32,64,128]{2,1,0:T(8,128)(2,1)} %get-tuple-element.59), calls=%async_computation.6 | async-start | bytes 1048576 | tf_op jit(solution)/shard_map/all_to_all | solution.py:603
  189.3 10.9 %collective-permute-done.4.far_hbm = bf16[3,368,256]{2,1,0:T(8,128)(2,1)S(1)} collective-permute-done((bf16[3,368,256]{2,1,0:T(8,128)(2,1)S(1)}, bf16[3,368,256]{2,1,0:T(8,128)(2,1)S(1)}, u32[]{:S(2)}, u32[]{:S(2)}) %collective-permute-start.4) | collective-permute-done | bytes 565280 | tf_op jit(solution)/shard_map/ppermute | solution.py:622
  205.3 4.5 %collective-permute-done.7 = f32[16,128]{1,0:T(8,128)S(1)} collective-permute-done((f32[16,128]{1,0:T(8,128)S(1)}, f32[16,128]{1,0:T(8,128)S(1)}, u32[]{:S(2)}, u32[]{:S(2)}) %collective-permute-start.7) | collective-permute-done | bytes 8224 | tf_op jit(solution)/shard_map/ppermute | solution.py:807
  212.8 11.6 %all-to-all-start.8 = ((bf16[32,48,128]{2,1,0:T(8,128)(2,1)}), bf16[32,48,128]{2,1,0:T(8,128)(2,1)S(1)}, u32[]{:S(2)}, u32[]{:S(2)}) async-start(bf16[32,48,128]{2,1,0:T(8,128)(2,1)} %shard_map.126), calls=%async_computation.8 | async-start | bytes 786432 | tf_op jit(solution)/shard_map/all_to_all | solution.py:603
  224.5 5.7 %collective-permute-start.8 = (bf16[1,368,256]{2,1,0:T(8,128)(2,1)S(1)}, bf16[1,368,256]{2,1,0:T(8,128)(2,1)S(1)}, u32[]{:S(2)}, u32[]{:S(2)}) collective-permute-start(bf16[1,368,256]{2,1,0:T(8,128)(2,1)S(1)} %slice_select_fusion.2), channel_id=1, source_target_pairs={{0,8},{8,0},{16,24},{24,16},{32,40},{40,32},{48,56},{56,48},{64,72... | collective-permute-start | bytes 565256 | tf_op jit(solution)/shard_map/ppermute | solution.py:632
  243.2 7.2 %shard_map.124.back_ref = f32[4,384,256]{2,1,0:T(8,128)} custom-call(s32[1]{0:T(128)} %bitcast.9.parity_ref, bf16[4,368,256]{2,1,0:T(8,128)(2,1)} %copy-done.18, bf16[3,368,256]{2,1,0:T(8,128)(2,1)} %copy-done.23, bf16[1,368,256]{2,1,0:T(8,128)(2,1)} %copy-done.25, bf16[3,368,256]{2,1,0:T(8,128)(2,1)} %copy-done.24, bf16[384,480]{1,0:T(8,128)(2,1)S(1)} %copy-done.14, ...), custom_call_target="tpu_custom_call" | custom-call | flops 13589544960 | bytes 4210692 | tf_op jit(solution)/shard_map/pallas_call | solution.py:43
  (130 shorter events, 75.2 us)
Async XLA Ops:
  0.6 20.8 %copy-start = (bf16[384,256]{1,0:T(8,128)(2,1)S(1)}, bf16[384,256]{1,0:T(8,128)(2,1)}, u32[]{:S(2)}) copy-start(bf16[384,256]{1,0:T(8,128)(2,1)} %param.15) | copy-start | bytes 589828
  3.1 25.7 %all-to-all-start = ((bf16[4,376,256]{2,1,0:T(8,128)(2,1)}), bf16[4,376,256]{2,1,0:T(8,128)(2,1)S(1)}, u32[]{:S(2)}, u32[]{:S(2)}) async-start(bf16[4,376,256]{2,1,0:T(8,128)(2,1)} %shard_map.111), calls=%async_computation | async-start | bytes 1540096 | tf_op jit(solution)/shard_map/all_to_all | solution.py:603
  33.4 30.4 %all-to-all-start.1 = ((bf16[32,48,128]{2,1,0:T(8,128)(2,1)}), bf16[32,48,128]{2,1,0:T(8,128)(2,1)}, u32[]{:S(2)}, u32[]{:S(2)}) async-start(bf16[32,48,128]{2,1,0:T(8,128)(2,1)} %shard_map.115), calls=%async_computation.1 | async-start | bytes 786432 | tf_op jit(solution)/shard_map/all_to_all | solution.py:603
  48.3 28.2 %collective-permute-start = (bf16[3,368,256]{2,1,0:T(8,128)(2,1)}, bf16[3,368,256]{2,1,0:T(8,128)(2,1)}, u32[]{:S(2)}, u32[]{:S(2)}) collective-permute-start(bf16[3,368,256]{2,1,0:T(8,128)(2,1)} %slice_select_fusion.1), channel_id=1, source_target_pairs={{0,8},{8,0},{16,24},{24,16},{32,40},{40,32},{48,56},{56,48},{64,72... | collective-permute-start | bytes 1695752 | tf_op jit(solution)/shard_map/ppermute | solution.py:622
  53.7 30.6 %copy-start.9 = (bf16[2,384,480]{2,1,0:T(8,128)(2,1)S(1)}, bf16[2,384,480]{2,1,0:T(8,128)(2,1)}, u32[]{:S(2)}) copy-start(bf16[2,384,480]{2,1,0:T(8,128)(2,1)} %copy-done.8) | copy-start | bytes 2211844
  69.1 26.8 %all-to-all-start.2 = ((bf16[32,48,128]{2,1,0:T(8,128)(2,1)}), bf16[32,48,128]{2,1,0:T(8,128)(2,1)}, u32[]{:S(2)}, u32[]{:S(2)}) async-start(bf16[32,48,128]{2,1,0:T(8,128)(2,1)} %get-tuple-element.46), calls=%async_computation.2 | async-start | bytes 786432 | tf_op jit(solution)/shard_map/all_to_all | solution.py:603
  76.5 28.3 %collective-permute-start.2 = (bf16[3,368,256]{2,1,0:T(8,128)(2,1)}, bf16[3,368,256]{2,1,0:T(8,128)(2,1)}, u32[]{:S(2)}, u32[]{:S(2)}) collective-permute-start(bf16[3,368,256]{2,1,0:T(8,128)(2,1)} %collective-permute-done.far_hbm), channel_id=1, source_target_pairs={{0,16},{8,248},{16,32},{24,8},{32,48},{40,24},{48,64},{56,40},{64,... | collective-permute-start | bytes 1695752 | tf_op jit(solution)/shard_map/ppermute | solution.py:628
  79.7 25.1 %collective-permute-start.1 = (bf16[1,368,256]{2,1,0:T(8,128)(2,1)}, bf16[1,368,256]{2,1,0:T(8,128)(2,1)}, u32[]{:S(2)}, u32[]{:S(2)}) collective-permute-start(bf16[1,368,256]{2,1,0:T(8,128)(2,1)} %slice_select_fusion.3), channel_id=1, source_target_pairs={{0,8},{8,0},{16,24},{24,16},{32,40},{40,32},{48,56},{56,48},{64,72... | collective-permute-start | bytes 565256 | tf_op jit(solution)/shard_map/ppermute | solution.py:632
  100.7 17.5 %all-to-all-start.3 = ((bf16[4,360,256]{2,1,0:T(8,128)(2,1)}), bf16[4,360,256]{2,1,0:T(8,128)(2,1)}, u32[]{:S(2)}, u32[]{:S(2)}) async-start(bf16[4,360,256]{2,1,0:T(8,128)(2,1)} %shard_map.117), calls=%async_computation.3 | async-start | bytes 1474560 | tf_op jit(solution)/shard_map/all_to_all | solution.py:603
  123.3 20.2 %all-to-all-start.4 = ((bf16[4,376,256]{2,1,0:T(8,128)(2,1)}), bf16[4,376,256]{2,1,0:T(8,128)(2,1)S(1)}, u32[]{:S(2)}, u32[]{:S(2)}) async-start(bf16[4,376,256]{2,1,0:T(8,128)(2,1)} %get-tuple-element.52), calls=%async_computation.4 | async-start | bytes 1540096 | tf_op jit(solution)/shard_map/all_to_all | solution.py:603
  131.2 1.6 collective-permute-start.3
  146.1 33.9 %all-to-all-start.5 = ((bf16[32,64,128]{2,1,0:T(8,128)(2,1)}), bf16[32,64,128]{2,1,0:T(8,128)(2,1)S(1)}, u32[]{:S(2)}, u32[]{:S(2)}) async-start(bf16[32,64,128]{2,1,0:T(8,128)(2,1)} %shard_map.121), calls=%async_computation.5 | async-start | bytes 1048576 | tf_op jit(solution)/shard_map/all_to_all | solution.py:603
  155.1 69.3 %copy-start.18 = (bf16[4,368,256]{2,1,0:T(8,128)(2,1)}, bf16[4,368,256]{2,1,0:T(8,128)(2,1)S(1)}, u32[]{:S(2)}) copy-start(bf16[4,368,256]{2,1,0:T(8,128)(2,1)S(1)} %maximum_maximum_fusion.1.own_hbm) | copy-start | bytes 2260996
  155.2 45.0 %collective-permute-start.4 = (bf16[3,368,256]{2,1,0:T(8,128)(2,1)S(1)}, bf16[3,368,256]{2,1,0:T(8,128)(2,1)S(1)}, u32[]{:S(2)}, u32[]{:S(2)}) collective-permute-start(bf16[3,368,256]{2,1,0:T(8,128)(2,1)S(1)} %slice_select_fusion), channel_id=1, source_target_pairs={{0,8},{8,0},{16,24},{24,16},{32,40},{40,32},{48,56},{56,48},{64,72... | collective-permute-start | bytes 1695752 | tf_op jit(solution)/shard_map/ppermute | solution.py:622
  184.5 27.4 %all-to-all-start.6 = ((bf16[32,64,128]{2,1,0:T(8,128)(2,1)}), bf16[32,64,128]{2,1,0:T(8,128)(2,1)S(1)}, u32[]{:S(2)}, u32[]{:S(2)}) async-start(bf16[32,64,128]{2,1,0:T(8,128)(2,1)} %get-tuple-element.59), calls=%async_computation.6 | async-start | bytes 1048576 | tf_op jit(solution)/shard_map/all_to_all | solution.py:603
  200.2 33.7 %copy-start.23 = (bf16[3,368,256]{2,1,0:T(8,128)(2,1)}, bf16[3,368,256]{2,1,0:T(8,128)(2,1)S(1)}, u32[]{:S(2)}) copy-start(bf16[3,368,256]{2,1,0:T(8,128)(2,1)S(1)} %collective-permute-done.4.far_hbm) | copy-start | bytes 1695748
  200.2 11.6 %collective-permute-start.5 = (bf16[3,368,256]{2,1,0:T(8,128)(2,1)S(1)}, bf16[3,368,256]{2,1,0:T(8,128)(2,1)S(1)}, u32[]{:S(2)}, u32[]{:S(2)}) collective-permute-start(bf16[3,368,256]{2,1,0:T(8,128)(2,1)S(1)} %collective-permute-done.4.far_hbm), channel_id=1, source_target_pairs={{0,16},{8,248},{16,32},{24,8},{32,48},{40,24},{48,64},{56,40},{64,... | collective-permute-start | bytes 1695752 | tf_op jit(solution)/shard_map/ppermute | solution.py:628
  201.6 3.7 %collective-permute-start.6 = (f32[16,128]{1,0:T(8,128)S(1)}, f32[16,128]{1,0:T(8,128)S(1)}, u32[]{:S(2)}, u32[]{:S(2)}) collective-permute-start(f32[16,128]{1,0:T(8,128)S(1)} %get-tuple-element.60), channel_id=1, source_target_pairs={{0,2},{2,0},{4,6},{6,4},{1,3},{3,1},{5,7},{7,5},{8,10},{10,8},{12,... | collective-permute-start | bytes 24584 | tf_op jit(solution)/shard_map/ppermute | solution.py:807
  205.3 4.5 %collective-permute-start.7 = (f32[16,128]{1,0:T(8,128)S(1)}, f32[16,128]{1,0:T(8,128)S(1)}, u32[]{:S(2)}, u32[]{:S(2)}) collective-permute-start(f32[16,128]{1,0:T(8,128)S(1)} %add.160), channel_id=1, source_target_pairs={{0,4},{2,6},{4,0},{6,2},{1,5},{3,7},{5,1},{7,3},{8,12},{10,14},{12... | collective-permute-start | bytes 24584 | tf_op jit(solution)/shard_map/ppermute | solution.py:807
  212.8 25.7 %all-to-all-start.8 = ((bf16[32,48,128]{2,1,0:T(8,128)(2,1)}), bf16[32,48,128]{2,1,0:T(8,128)(2,1)S(1)}, u32[]{:S(2)}, u32[]{:S(2)}) async-start(bf16[32,48,128]{2,1,0:T(8,128)(2,1)} %shard_map.126), calls=%async_computation.8 | async-start | bytes 786432 | tf_op jit(solution)/shard_map/all_to_all | solution.py:603
  224.5 18.1 %collective-permute-start.8 = (bf16[1,368,256]{2,1,0:T(8,128)(2,1)S(1)}, bf16[1,368,256]{2,1,0:T(8,128)(2,1)S(1)}, u32[]{:S(2)}, u32[]{:S(2)}) collective-permute-start(bf16[1,368,256]{2,1,0:T(8,128)(2,1)S(1)} %slice_select_fusion.2), channel_id=1, source_target_pairs={{0,8},{8,0},{16,24},{24,16},{32,40},{40,32},{48,56},{56,48},{64,72... | collective-permute-start | bytes 565256 | tf_op jit(solution)/shard_map/ppermute | solution.py:632
  238.4 16.6 %all-to-all-start.7 = ((bf16[4,360,256]{2,1,0:T(8,128)(2,1)}), bf16[4,360,256]{2,1,0:T(8,128)(2,1)S(1)}, u32[]{:S(2)}, u32[]{:S(2)}) async-start(bf16[4,360,256]{2,1,0:T(8,128)(2,1)} %shard_map.123), calls=%async_computation.7 | async-start | bytes 1474560 | tf_op jit(solution)/shard_map/all_to_all | solution.py:603
  242.0 8.5 %collective-permute-start.10 = (f32[384,128]{1,0:T(8,128)S(1)}, f32[384,128]{1,0:T(8,128)S(1)}, u32[]{:S(2)}, u32[]{:S(2)}) collective-permute-start(f32[384,128]{1,0:T(8,128)S(1)} %get-tuple-element.65.mine_ref), channel_id=1, source_target_pairs={{0,1},{1,0},{2,3},{3,2},{4,5},{5,4},{6,7},{7,6},{8,9},{9,8},{10,11... | collective-permute-start | bytes 589832 | tf_op jit(solution)/shard_map/ppermute | solution.py:836
  242.1 8.4 %collective-permute-start.9 = (f32[192,128]{1,0:T(8,128)S(1)}, f32[192,128]{1,0:T(8,128)S(1)}, u32[]{:S(2)}, u32[]{:S(2)}) collective-permute-start(f32[192,128]{1,0:T(8,128)S(1)} %get-tuple-element.64.gain_mine_ref), channel_id=1, source_target_pairs={{0,1},{1,0},{2,3},{3,2},{4,5},{5,4},{6,7},{7,6},{8,9},{9,8},{10,11... | collective-permute-start | bytes 294920 | tf_op jit(solution)/shard_map/ppermute | solution.py:837
  (24 other events, 127.6 us)

commit v4 on v3

--- a/solution.py
+++ b/solution.py
@@ -374,7 +374,7 @@
                 basis_ref[b, :, at, :] = part.reshape(rows, BLOCK, channels)
             term = dot(part, wide_ref[b])
             total = term if total is None else total + term
-        mixed_ref[:, at, :] = total.reshape(rows, BLOCK, channels)
+        mixed_ref[:, at, :] = total.reshape(rows, BLOCK, channels).astype(bf16)
 
 
 def activation_kernel(
@@ -394,7 +394,7 @@
             grads = []
             for h in range(2):
                 t = 2 * a + h
-                value = spectra[h] + mixed_ref[t, rows, av]
+                value = spectra[h] + mixed_ref[t, rows, av].astype(f32)
                 square = value * value
                 turn = jnp.tanh(scale * value * (1.0 + 0.044715 * square))
                 share = 0.5 + 0.5 * turn
@@ -438,7 +438,7 @@
             for h in range(2):
                 t = 2 * a + h
                 out_ref[t, rows, av] = (
-                    cot_ref[t, rows, av].astype(f32) + spectra[h] + back_ref[t, rows, av]
+                    cot_ref[t, rows, av].astype(f32) + spectra[h] + back_ref[t, rows, av].astype(f32)
                 ).astype(bf16)
 
 
@@ -705,7 +705,7 @@
     def band(x, far, other, which, turned):
         rest = rest_rows(x, even)
         matrix = matrices[which]
-        outs = [pltpu.HBM(wide_shape.shape, f32)]
+        outs = [pltpu.HBM(wide_shape.shape, bf16)]
         specs = [pl.BlockSpec((lat_rows, WINDOWS * BLOCK, channels), lambda j: (0, j, 0))]
         if not turned:
             outs.append(pltpu.HBM((kernel_number, lat_rows, padded, channels), bf16))

time: 261 us -> 261 us (level)
  no operation moved by 1% of the time
where the time goes in v4:
time: 261 us; the launch traced here: 259 us
  waiting for transfers between devices  95.1 us (36%)
  starting transfers between devices  85 us (33%)
  Pallas kernels  53.9 us (21%)
  local copies, waits for them, and re-layouts  17.9 us (7%)
  other arithmetic  5.97 us (2%)
    all_to_all x9, waiting for transfers between devices, exchange(): return lax.all_to_all(x, axis, split_axis=0, concat_axis=0, tiled=True)  71 us
    all_to_all x9, starting transfers between devices, exchange(): return lax.all_to_all(x, axis, split_axis=0, concat_axis=0, tiled=True)  60.4 us
    pallas_call x18, Pallas kernels, call(): pl.pallas_call(kernel, grid=grid, out_shape=out_shape, in_specs=specs, ou...  53.9 us
    unnamed x56, local copies, waits for them, and re-layouts  13.8 us
    ppermute x2, waiting for transfers between devices, swapped_rows(): lax.ppermute(jnp.where(even, x[:BAND_REACH], x[1:BAND_REACH + 1]), 'lat',...  12.3 us
    ppermute x2, starting transfers between devices, swapped_rows(): lax.ppermute(jnp.where(even, x[:BAND_REACH], x[1:BAND_REACH + 1]), 'lat',...  10.8 us
    ppermute x2, starting transfers between devices, rest_rows(): return lax.ppermute(jnp.where(even, x[BAND_REACH:], x[:1]), 'lat', pairs())  10.3 us
    ppermute x2, waiting for transfers between devices, on_device(): lax.ppermute(mix_sum, 'lon', [(i, i ^ bit) for i in range(lon_count)])  8.19 us
  transfers between devices with their start and end apart: 20, of which 14 were waited for; matrix products, arithmetic and copies ran while one was open for 4% of the time, Pallas kernels for 15%

profile of v4, /device:TPU:2, one launch (start us, length us, event | category | flops | bytes accessed | tf_op | source)
XLA Modules:
  0.0 259.5 jit_solution(10421362341506752665)
XLA Ops:
  3.0 5.9 %all-to-all-start = ((bf16[4,376,256]{2,1,0:T(8,128)(2,1)}), bf16[4,376,256]{2,1,0:T(8,128)(2,1)S(1)}, u32[]{:S(2)}, u32[]{:S(2)}) async-start(bf16[4,376,256]{2,1,0:T(8,128)(2,1)} %shard_map.111), calls=%async_computation | async-start | bytes 1540096 | tf_op jit(solution)/shard_map/all_to_all | solution.py:603
  21.5 7.1 %all-to-all-done.circle_ref = bf16[4,376,256]{2,1,0:T(8,128)(2,1)S(1)} async-done(((bf16[4,376,256]{2,1,0:T(8,128)(2,1)}), bf16[4,376,256]{2,1,0:T(8,128)(2,1)S(1)}, u32[]{:S(2)}, u32[]{:S(2)}) %all-to-all-start) | async-done | bytes 770080 | tf_op jit(solution)/shard_map/all_to_all | solution.py:603
  33.2 12.1 %all-to-all-start.1 = ((bf16[32,48,128]{2,1,0:T(8,128)(2,1)}), bf16[32,48,128]{2,1,0:T(8,128)(2,1)}, u32[]{:S(2)}, u32[]{:S(2)}) async-start(bf16[32,48,128]{2,1,0:T(8,128)(2,1)} %shard_map.115), calls=%async_computation.1 | async-start | bytes 786432 | tf_op jit(solution)/shard_map/all_to_all | solution.py:603
  48.1 5.4 %collective-permute-start = (bf16[3,368,256]{2,1,0:T(8,128)(2,1)}, bf16[3,368,256]{2,1,0:T(8,128)(2,1)}, u32[]{:S(2)}, u32[]{:S(2)}) collective-permute-start(bf16[3,368,256]{2,1,0:T(8,128)(2,1)} %slice_select_fusion.1), channel_id=1, source_target_pairs={{0,8},{8,0},{16,24},{24,16},{32,40},{40,32},{48,56},{56,48},{64,72... | collective-permute-start | bytes 1695752 | tf_op jit(solution)/shard_map/ppermute | solution.py:622
  53.6 10.1 %all-to-all-done.1.got_ref = bf16[32,48,128]{2,1,0:T(8,128)(2,1)} async-done(((bf16[32,48,128]{2,1,0:T(8,128)(2,1)}), bf16[32,48,128]{2,1,0:T(8,128)(2,1)}, u32[]{:S(2)}, u32[]{:S(2)}) %all-to-all-start.1) | async-done | bytes 393248 | tf_op jit(solution)/shard_map/all_to_all | solution.py:603
  63.7 5.3 %shard_map.116 = (bf16[32,48,128]{2,1,0:T(8,128)(2,1)}, f32[12,384,128]{2,1,0:T(8,128)}) custom-call(s32[12]{0:T(128)S(1)} %dynamic_slice.38.order_ref, bf16[32,48,128]{2,1,0:T(8,128)(2,1)} %all-to-all-done.1.got_ref, bf16[12,384,128]{2,1,0:T(8,128)(2,1)} %copy-done.4, bf16[12,128,384]{2,1,0:T(8,128)(2,1)} %copy-done.5, ...), custom_call_target="tpu_custom_call" | custom-call | flops 301989888 | bytes 5701680 | tf_op jit(solution)/shard_map/pallas_call | solution.py:43
  69.0 5.6 %all-to-all-start.2 = ((bf16[32,48,128]{2,1,0:T(8,128)(2,1)}), bf16[32,48,128]{2,1,0:T(8,128)(2,1)}, u32[]{:S(2)}, u32[]{:S(2)}) async-start(bf16[32,48,128]{2,1,0:T(8,128)(2,1)} %get-tuple-element.46), calls=%async_computation.2 | async-start | bytes 786432 | tf_op jit(solution)/shard_map/all_to_all | solution.py:603
  79.4 4.6 %collective-permute-start.1 = (bf16[1,368,256]{2,1,0:T(8,128)(2,1)}, bf16[1,368,256]{2,1,0:T(8,128)(2,1)}, u32[]{:S(2)}, u32[]{:S(2)}) collective-permute-start(bf16[1,368,256]{2,1,0:T(8,128)(2,1)} %slice_select_fusion.3), channel_id=1, source_target_pairs={{0,8},{8,0},{16,24},{24,16},{32,40},{40,32},{48,56},{56,48},{64,72... | collective-permute-start | bytes 565256 | tf_op jit(solution)/shard_map/ppermute | solution.py:632
  85.0 10.8 %all-to-all-done.2.got_ref = bf16[32,48,128]{2,1,0:T(8,128)(2,1)} async-done(((bf16[32,48,128]{2,1,0:T(8,128)(2,1)}), bf16[32,48,128]{2,1,0:T(8,128)(2,1)}, u32[]{:S(2)}, u32[]{:S(2)}) %all-to-all-start.2) | async-done | bytes 393248 | tf_op jit(solution)/shard_map/all_to_all | solution.py:603
  95.8 4.7 %shard_map.117 = bf16[4,360,256]{2,1,0:T(8,128)(2,1)} custom-call(bf16[32,48,128]{2,1,0:T(8,128)(2,1)} %all-to-all-done.2.got_ref, bf16[4,360,768]{2,1,0:T(8,128)(2,1)} %copy-done.1), custom_call_target="tpu_custom_call" | custom-call | flops 566231040 | bytes 3342336 | tf_op jit(solution)/shard_map/pallas_call | solution.py:43
  104.8 7.4 %shard_map.118 = (bf16[4,384,256]{2,1,0:T(8,128)(2,1)}, bf16[3,4,384,256]{3,2,1,0:T(8,128)(2,1)}) custom-call(s32[1]{0:T(128)} %bitcast.9.parity_ref, bf16[4,368,256]{2,1,0:T(8,128)(2,1)} %copy-done.19, bf16[3,368,256]{2,1,0:T(8,128)(2,1)} %collective-permute-done.far_hbm, bf16[1,368,256]{2,1,0:T(8,128)(2,1)} %collective-permute-done.1.rest_hbm, ...), custom_call_target="tpu_custom_call" | custom-call | flops 13589544960 | bytes 5783556 | tf_op jit(solution)/shard_map/pallas_call | solution.py:43
  112.2 5.8 %all-to-all-done.3.spec_ref = bf16[4,360,256]{2,1,0:T(8,128)(2,1)} async-done(((bf16[4,360,256]{2,1,0:T(8,128)(2,1)}), bf16[4,360,256]{2,1,0:T(8,128)(2,1)}, u32[]{:S(2)}, u32[]{:S(2)}) %all-to-all-start.3) | async-done | bytes 737312 | tf_op jit(solution)/shard_map/all_to_all | solution.py:603
  118.0 5.2 %shard_map.119 = (bf16[4,360,256]{2,1,0:T(8,128)(2,1)}, bf16[4,360,256]{2,1,0:T(8,128)(2,1)}, bf16[4,376,256]{2,1,0:T(8,128)(2,1)}) custom-call(s32[1]{0:T(128)} %bitcast.place_ref, bf16[4,360,256]{2,1,0:T(8,128)(2,1)} %all-to-all-done.3.spec_ref, bf16[4,384,256]{2,1,0:T(8,128)(2,1)} %get-tuple-element.50.mixed_ref, bf16[4,360,256]{2,1,0:T(8,128)(2,1)} %bitcast.41, ...), custom_call_target="tpu_custom_call" | custom-call | flops 14745600 | bytes 5242884 | tf_op jit(solution)/shard_map/pallas_call | solution.py:43
  132.6 10.6 %all-to-all-done.4.circle_ref = bf16[4,376,256]{2,1,0:T(8,128)(2,1)S(1)} async-done(((bf16[4,376,256]{2,1,0:T(8,128)(2,1)}), bf16[4,376,256]{2,1,0:T(8,128)(2,1)S(1)}, u32[]{:S(2)}, u32[]{:S(2)}) %all-to-all-start.4) | async-done | bytes 770080 | tf_op jit(solution)/shard_map/all_to_all | solution.py:603
  145.9 8.7 %all-to-all-start.5 = ((bf16[32,64,128]{2,1,0:T(8,128)(2,1)}), bf16[32,64,128]{2,1,0:T(8,128)(2,1)S(1)}, u32[]{:S(2)}, u32[]{:S(2)}) async-start(bf16[32,64,128]{2,1,0:T(8,128)(2,1)} %shard_map.121), calls=%async_computation.5 | async-start | bytes 1048576 | tf_op jit(solution)/shard_map/all_to_all | solution.py:603
  154.9 5.5 %collective-permute-start.4 = (bf16[3,368,256]{2,1,0:T(8,128)(2,1)S(1)}, bf16[3,368,256]{2,1,0:T(8,128)(2,1)S(1)}, u32[]{:S(2)}, u32[]{:S(2)}) collective-permute-start(bf16[3,368,256]{2,1,0:T(8,128)(2,1)S(1)} %slice_select_fusion), channel_id=1, source_target_pairs={{0,8},{8,0},{16,24},{24,16},{32,40},{40,32},{48,56},{56,48},{64,72... | collective-permute-start | bytes 1695752 | tf_op jit(solution)/shard_map/ppermute | solution.py:622
  160.4 19.5 %all-to-all-done.5.got_ref = bf16[32,64,128]{2,1,0:T(8,128)(2,1)S(1)} async-done(((bf16[32,64,128]{2,1,0:T(8,128)(2,1)}), bf16[32,64,128]{2,1,0:T(8,128)(2,1)S(1)}, u32[]{:S(2)}, u32[]{:S(2)}) %all-to-all-start.5) | async-done | bytes 524320 | tf_op jit(solution)/shard_map/all_to_all | solution.py:603
  179.9 4.5 %shard_map.122 = (bf16[32,64,128]{2,1,0:T(8,128)(2,1)}, f32[16,128]{1,0:T(8,128)S(1)}) custom-call(s32[12]{0:T(128)S(1)} %dynamic_slice.38.order_ref, bf16[32,64,128]{2,1,0:T(8,128)(2,1)S(1)} %all-to-all-done.5.got_ref, bf16[12,384,128]{2,1,0:T(8,128)(2,1)} %copy-done.4, bf16[12,128,384]{2,1,0:T(8,128)(2,1)} %copy-done.5, ...), custom_call_target="tpu_custom_call" | custom-call | flops 301989888 | bytes 5972016 | tf_op jit(solution)/shard_map/pallas_call | solution.py:43
  184.4 4.9 %all-to-all-start.6 = ((bf16[32,64,128]{2,1,0:T(8,128)(2,1)}), bf16[32,64,128]{2,1,0:T(8,128)(2,1)S(1)}, u32[]{:S(2)}, u32[]{:S(2)}) async-start(bf16[32,64,128]{2,1,0:T(8,128)(2,1)} %get-tuple-element.59), calls=%async_computation.6 | async-start | bytes 1048576 | tf_op jit(solution)/shard_map/all_to_all | solution.py:603
  189.3 10.7 %collective-permute-done.4.far_hbm = bf16[3,368,256]{2,1,0:T(8,128)(2,1)S(1)} collective-permute-done((bf16[3,368,256]{2,1,0:T(8,128)(2,1)S(1)}, bf16[3,368,256]{2,1,0:T(8,128)(2,1)S(1)}, u32[]{:S(2)}, u32[]{:S(2)}) %collective-permute-start.4) | collective-permute-done | bytes 565280 | tf_op jit(solution)/shard_map/ppermute | solution.py:622
  205.1 4.5 %collective-permute-done.7 = f32[16,128]{1,0:T(8,128)S(1)} collective-permute-done((f32[16,128]{1,0:T(8,128)S(1)}, f32[16,128]{1,0:T(8,128)S(1)}, u32[]{:S(2)}, u32[]{:S(2)}) %collective-permute-start.7) | collective-permute-done | bytes 8224 | tf_op jit(solution)/shard_map/ppermute | solution.py:807
  212.5 11.9 %all-to-all-start.8 = ((bf16[32,48,128]{2,1,0:T(8,128)(2,1)}), bf16[32,48,128]{2,1,0:T(8,128)(2,1)S(1)}, u32[]{:S(2)}, u32[]{:S(2)}) async-start(bf16[32,48,128]{2,1,0:T(8,128)(2,1)} %shard_map.126), calls=%async_computation.8 | async-start | bytes 786432 | tf_op jit(solution)/shard_map/all_to_all | solution.py:603
  224.5 5.7 %collective-permute-start.8 = (bf16[1,368,256]{2,1,0:T(8,128)(2,1)S(1)}, bf16[1,368,256]{2,1,0:T(8,128)(2,1)S(1)}, u32[]{:S(2)}, u32[]{:S(2)}) collective-permute-start(bf16[1,368,256]{2,1,0:T(8,128)(2,1)S(1)} %slice_select_fusion.2), channel_id=1, source_target_pairs={{0,8},{8,0},{16,24},{24,16},{32,40},{40,32},{48,56},{56,48},{64,72... | collective-permute-start | bytes 565256 | tf_op jit(solution)/shard_map/ppermute | solution.py:632
  242.9 7.2 %shard_map.124.back_ref = bf16[4,384,256]{2,1,0:T(8,128)(2,1)} custom-call(s32[1]{0:T(128)} %bitcast.9.parity_ref, bf16[4,368,256]{2,1,0:T(8,128)(2,1)} %copy-done.18, bf16[3,368,256]{2,1,0:T(8,128)(2,1)} %copy-done.23, bf16[1,368,256]{2,1,0:T(8,128)(2,1)} %copy-done.25, bf16[3,368,256]{2,1,0:T(8,128)(2,1)} %copy-done.24, bf16[384,480]{1,0:T(8,128)(2,1)S(1)} %copy-done.14, ...), custom_call_target="tpu_custom_call" | custom-call | flops 13589544960 | bytes 3424260 | tf_op jit(solution)/shard_map/pallas_call | solution.py:43
  (130 shorter events, 74.5 us)
Async XLA Ops:
  0.6 20.7 %copy-start = (bf16[384,256]{1,0:T(8,128)(2,1)S(1)}, bf16[384,256]{1,0:T(8,128)(2,1)}, u32[]{:S(2)}) copy-start(bf16[384,256]{1,0:T(8,128)(2,1)} %param.15) | copy-start | bytes 589828
  3.0 25.7 %all-to-all-start = ((bf16[4,376,256]{2,1,0:T(8,128)(2,1)}), bf16[4,376,256]{2,1,0:T(8,128)(2,1)S(1)}, u32[]{:S(2)}, u32[]{:S(2)}) async-start(bf16[4,376,256]{2,1,0:T(8,128)(2,1)} %shard_map.111), calls=%async_computation | async-start | bytes 1540096 | tf_op jit(solution)/shard_map/all_to_all | solution.py:603
  33.2 30.4 %all-to-all-start.1 = ((bf16[32,48,128]{2,1,0:T(8,128)(2,1)}), bf16[32,48,128]{2,1,0:T(8,128)(2,1)}, u32[]{:S(2)}, u32[]{:S(2)}) async-start(bf16[32,48,128]{2,1,0:T(8,128)(2,1)} %shard_map.115), calls=%async_computation.1 | async-start | bytes 786432 | tf_op jit(solution)/shard_map/all_to_all | solution.py:603
  48.1 28.1 %collective-permute-start = (bf16[3,368,256]{2,1,0:T(8,128)(2,1)}, bf16[3,368,256]{2,1,0:T(8,128)(2,1)}, u32[]{:S(2)}, u32[]{:S(2)}) collective-permute-start(bf16[3,368,256]{2,1,0:T(8,128)(2,1)} %slice_select_fusion.1), channel_id=1, source_target_pairs={{0,8},{8,0},{16,24},{24,16},{32,40},{40,32},{48,56},{56,48},{64,72... | collective-permute-start | bytes 1695752 | tf_op jit(solution)/shard_map/ppermute | solution.py:622
  53.6 30.5 %copy-start.9 = (bf16[2,384,480]{2,1,0:T(8,128)(2,1)S(1)}, bf16[2,384,480]{2,1,0:T(8,128)(2,1)}, u32[]{:S(2)}) copy-start(bf16[2,384,480]{2,1,0:T(8,128)(2,1)} %copy-done.8) | copy-start | bytes 2211844
  69.0 26.8 %all-to-all-start.2 = ((bf16[32,48,128]{2,1,0:T(8,128)(2,1)}), bf16[32,48,128]{2,1,0:T(8,128)(2,1)}, u32[]{:S(2)}, u32[]{:S(2)}) async-start(bf16[32,48,128]{2,1,0:T(8,128)(2,1)} %get-tuple-element.46), calls=%async_computation.2 | async-start | bytes 786432 | tf_op jit(solution)/shard_map/all_to_all | solution.py:603
  76.3 28.5 %collective-permute-start.2 = (bf16[3,368,256]{2,1,0:T(8,128)(2,1)}, bf16[3,368,256]{2,1,0:T(8,128)(2,1)}, u32[]{:S(2)}, u32[]{:S(2)}) collective-permute-start(bf16[3,368,256]{2,1,0:T(8,128)(2,1)} %collective-permute-done.far_hbm), channel_id=1, source_target_pairs={{0,16},{8,248},{16,32},{24,8},{32,48},{40,24},{48,64},{56,40},{64,... | collective-permute-start | bytes 1695752 | tf_op jit(solution)/shard_map/ppermute | solution.py:628
  79.4 25.3 %collective-permute-start.1 = (bf16[1,368,256]{2,1,0:T(8,128)(2,1)}, bf16[1,368,256]{2,1,0:T(8,128)(2,1)}, u32[]{:S(2)}, u32[]{:S(2)}) collective-permute-start(bf16[1,368,256]{2,1,0:T(8,128)(2,1)} %slice_select_fusion.3), channel_id=1, source_target_pairs={{0,8},{8,0},{16,24},{24,16},{32,40},{40,32},{48,56},{56,48},{64,72... | collective-permute-start | bytes 565256 | tf_op jit(solution)/shard_map/ppermute | solution.py:632
  100.5 17.5 %all-to-all-start.3 = ((bf16[4,360,256]{2,1,0:T(8,128)(2,1)}), bf16[4,360,256]{2,1,0:T(8,128)(2,1)}, u32[]{:S(2)}, u32[]{:S(2)}) async-start(bf16[4,360,256]{2,1,0:T(8,128)(2,1)} %shard_map.117), calls=%async_computation.3 | async-start | bytes 1474560 | tf_op jit(solution)/shard_map/all_to_all | solution.py:603
  123.1 20.1 %all-to-all-start.4 = ((bf16[4,376,256]{2,1,0:T(8,128)(2,1)}), bf16[4,376,256]{2,1,0:T(8,128)(2,1)S(1)}, u32[]{:S(2)}, u32[]{:S(2)}) async-start(bf16[4,376,256]{2,1,0:T(8,128)(2,1)} %get-tuple-element.52), calls=%async_computation.4 | async-start | bytes 1540096 | tf_op jit(solution)/shard_map/all_to_all | solution.py:603
  131.1 1.6 collective-permute-start.3
  145.9 34.1 %all-to-all-start.5 = ((bf16[32,64,128]{2,1,0:T(8,128)(2,1)}), bf16[32,64,128]{2,1,0:T(8,128)(2,1)S(1)}, u32[]{:S(2)}, u32[]{:S(2)}) async-start(bf16[32,64,128]{2,1,0:T(8,128)(2,1)} %shard_map.121), calls=%async_computation.5 | async-start | bytes 1048576 | tf_op jit(solution)/shard_map/all_to_all | solution.py:603
  154.9 69.6 %copy-start.18 = (bf16[4,368,256]{2,1,0:T(8,128)(2,1)}, bf16[4,368,256]{2,1,0:T(8,128)(2,1)S(1)}, u32[]{:S(2)}) copy-start(bf16[4,368,256]{2,1,0:T(8,128)(2,1)S(1)} %maximum_maximum_fusion.1.own_hbm) | copy-start | bytes 2260996
  154.9 45.0 %collective-permute-start.4 = (bf16[3,368,256]{2,1,0:T(8,128)(2,1)S(1)}, bf16[3,368,256]{2,1,0:T(8,128)(2,1)S(1)}, u32[]{:S(2)}, u32[]{:S(2)}) collective-permute-start(bf16[3,368,256]{2,1,0:T(8,128)(2,1)S(1)} %slice_select_fusion), channel_id=1, source_target_pairs={{0,8},{8,0},{16,24},{24,16},{32,40},{40,32},{48,56},{56,48},{64,72... | collective-permute-start | bytes 1695752 | tf_op jit(solution)/shard_map/ppermute | solution.py:622
  184.4 27.2 %all-to-all-start.6 = ((bf16[32,64,128]{2,1,0:T(8,128)(2,1)}), bf16[32,64,128]{2,1,0:T(8,128)(2,1)S(1)}, u32[]{:S(2)}, u32[]{:S(2)}) async-start(bf16[32,64,128]{2,1,0:T(8,128)(2,1)} %get-tuple-element.59), calls=%async_computation.6 | async-start | bytes 1048576 | tf_op jit(solution)/shard_map/all_to_all | solution.py:603
  200.0 34.0 %copy-start.23 = (bf16[3,368,256]{2,1,0:T(8,128)(2,1)}, bf16[3,368,256]{2,1,0:T(8,128)(2,1)S(1)}, u32[]{:S(2)}) copy-start(bf16[3,368,256]{2,1,0:T(8,128)(2,1)S(1)} %collective-permute-done.4.far_hbm) | copy-start | bytes 1695748
  200.0 11.6 %collective-permute-start.5 = (bf16[3,368,256]{2,1,0:T(8,128)(2,1)S(1)}, bf16[3,368,256]{2,1,0:T(8,128)(2,1)S(1)}, u32[]{:S(2)}, u32[]{:S(2)}) collective-permute-start(bf16[3,368,256]{2,1,0:T(8,128)(2,1)S(1)} %collective-permute-done.4.far_hbm), channel_id=1, source_target_pairs={{0,16},{8,248},{16,32},{24,8},{32,48},{40,24},{48,64},{56,40},{64,... | collective-permute-start | bytes 1695752 | tf_op jit(solution)/shard_map/ppermute | solution.py:628
  201.4 3.7 %collective-permute-start.6 = (f32[16,128]{1,0:T(8,128)S(1)}, f32[16,128]{1,0:T(8,128)S(1)}, u32[]{:S(2)}, u32[]{:S(2)}) collective-permute-start(f32[16,128]{1,0:T(8,128)S(1)} %get-tuple-element.60), channel_id=1, source_target_pairs={{0,2},{2,0},{4,6},{6,4},{1,3},{3,1},{5,7},{7,5},{8,10},{10,8},{12,... | collective-permute-start | bytes 24584 | tf_op jit(solution)/shard_map/ppermute | solution.py:807
  205.0 4.5 %collective-permute-start.7 = (f32[16,128]{1,0:T(8,128)S(1)}, f32[16,128]{1,0:T(8,128)S(1)}, u32[]{:S(2)}, u32[]{:S(2)}) collective-permute-start(f32[16,128]{1,0:T(8,128)S(1)} %add.160), channel_id=1, source_target_pairs={{0,4},{2,6},{4,0},{6,2},{1,5},{3,7},{5,1},{7,3},{8,12},{10,14},{12... | collective-permute-start | bytes 24584 | tf_op jit(solution)/shard_map/ppermute | solution.py:807
  212.5 25.6 %all-to-all-start.8 = ((bf16[32,48,128]{2,1,0:T(8,128)(2,1)}), bf16[32,48,128]{2,1,0:T(8,128)(2,1)S(1)}, u32[]{:S(2)}, u32[]{:S(2)}) async-start(bf16[32,48,128]{2,1,0:T(8,128)(2,1)} %shard_map.126), calls=%async_computation.8 | async-start | bytes 786432 | tf_op jit(solution)/shard_map/all_to_all | solution.py:603
  224.5 17.7 %collective-permute-start.8 = (bf16[1,368,256]{2,1,0:T(8,128)(2,1)S(1)}, bf16[1,368,256]{2,1,0:T(8,128)(2,1)S(1)}, u32[]{:S(2)}, u32[]{:S(2)}) collective-permute-start(bf16[1,368,256]{2,1,0:T(8,128)(2,1)S(1)} %slice_select_fusion.2), channel_id=1, source_target_pairs={{0,8},{8,0},{16,24},{24,16},{32,40},{40,32},{48,56},{56,48},{64,72... | collective-permute-start | bytes 565256 | tf_op jit(solution)/shard_map/ppermute | solution.py:632
  238.1 16.7 %all-to-all-start.7 = ((bf16[4,360,256]{2,1,0:T(8,128)(2,1)}), bf16[4,360,256]{2,1,0:T(8,128)(2,1)S(1)}, u32[]{:S(2)}, u32[]{:S(2)}) async-start(bf16[4,360,256]{2,1,0:T(8,128)(2,1)} %shard_map.123), calls=%async_computation.7 | async-start | bytes 1474560 | tf_op jit(solution)/shard_map/all_to_all | solution.py:603
  241.6 8.5 %collective-permute-start.10 = (f32[384,128]{1,0:T(8,128)S(1)}, f32[384,128]{1,0:T(8,128)S(1)}, u32[]{:S(2)}, u32[]{:S(2)}) collective-permute-start(f32[384,128]{1,0:T(8,128)S(1)} %get-tuple-element.65.mine_ref), channel_id=1, source_target_pairs={{0,1},{1,0},{2,3},{3,2},{4,5},{5,4},{6,7},{7,6},{8,9},{9,8},{10,11... | collective-permute-start | bytes 589832 | tf_op jit(solution)/shard_map/ppermute | solution.py:836
  241.7 8.4 %collective-permute-start.9 = (f32[192,128]{1,0:T(8,128)S(1)}, f32[192,128]{1,0:T(8,128)S(1)}, u32[]{:S(2)}, u32[]{:S(2)}) collective-permute-start(f32[192,128]{1,0:T(8,128)S(1)} %get-tuple-element.64.gain_mine_ref), channel_id=1, source_target_pairs={{0,1},{1,0},{2,3},{3,2},{4,5},{5,4},{6,7},{7,6},{8,9},{9,8},{10,11... | collective-permute-start | bytes 294920 | tf_op jit(solution)/shard_map/ppermute | solution.py:837
  (24 other events, 126.5 us)
